TPU v7x, 128 devices: a whole 4x4x4 slice. The times are simulated.
128 devices in a mesh: dp: 16 (over y_hi, x, core), shard: 8 (over y_lo, z).
Axes of the slice: x: 4, y: 4 (y_hi: 2, y_lo: 2; y = y_hi * 2 + y_lo), z: 4, core: 2. Of those that a mesh axis runs over, the one named last changes fastest.
Arguments:
- hidden: bfloat16 [16, 1024, 1536], P('dp', 'shard'), may hold values from -6 to 6
- cotangent: bfloat16 [16, 1024, 1536], P('dp', 'shard'), may hold values from -6 to 6
- in_master: float32 [1536, 6448], P('shard'), may hold values from -0.15625 to 0.15625
- in_first: float32 [1536, 6448], P('shard'), may hold values from -24 to 24
- in_second: float32 [1536, 6448], P('shard'), may hold values from 73.728 to 294.912
- out_master: float32 [3072, 1536], P('shard'), may hold values from -0.109375 to 0.109375
- out_first: float32 [3072, 1536], P('shard'), may hold values from -80 to 80
- out_second: float32 [3072, 1536], P('shard'), may hold values from 819.2 to 3276.8
- gain_master: float32 [4608], P('shard'), may hold values from 0.5 to 1.5
- gain_first: float32 [4608], P('shard'), may hold values from -24 to 24
- gain_second: float32 [4608], P('shard'), may hold values from 73.728 to 294.912
- conv_master: float32 [5, 3328], P(None, 'shard'), may hold values from -3 to 3
- conv_first: float32 [5, 3328], P(None, 'shard'), may hold values from -24 to 24
- conv_second: float32 [5, 3328], P(None, 'shard'), may hold values from 73.728 to 294.912
- head_master: float32 [3, 48], P(None, 'shard'), may hold values from -10 to 2
- head_first: float32 [3, 48], P(None, 'shard'), may hold values from -80 to 80
- head_second: float32 [3, 48], P(None, 'shard'), may hold values from 819.2 to 3276.8
Outputs:
- layer_out: bfloat16 [16, 1024, 1536], P('dp', 'shard')
- input_grad: bfloat16 [16, 1024, 1536], P('dp', 'shard')
- in_moment: float32 [1536, 6448], P('shard')
- in_square: float32 [1536, 6448], P('shard')
- in_weight: float32 [1536, 6448], P('shard')
- out_moment: float32 [3072, 1536], P('shard')
- out_square: float32 [3072, 1536], P('shard')
- out_weight: float32 [3072, 1536], P('shard')
- gain_moment: float32 [4608], P('shard')
- gain_square: float32 [4608], P('shard')
- gain_value: float32 [4608], P('shard')
- conv_moment: float32 [5, 3328], P(None, 'shard')
- conv_square: float32 [5, 3328], P(None, 'shard')
- conv_value: float32 [5, 3328], P(None, 'shard')
- head_moment: float32 [3, 48], P(None, 'shard')
- head_square: float32 [3, 48], P(None, 'shard')
- head_value: float32 [3, 48], P(None, 'shard')
All inputs are finite; a program needn't handle non-finite values.
Results may differ from a plain program's by a relative error of at most 0.0044.
The roundings to bfloat16 on the way count: a program that leaves them out, or rounds other values in their place, can miss the bound.
Values may be sent and summed in bfloat16 or wider, within the bound.
A program may use at most 320 MiB of HBM per device.

v0:
```python
import jax
import jax.numpy as jnp
from jax import lax
from jax.sharding import PartitionSpec as P

D = 1536
DI = 3072
H = 48
HD = 64
NS = 128
KCONV = 4
STEP = 5
BLOCK = 128
CONVC = 3328


highest = lax.Precision.HIGHEST
epsilon = 1e-05
beta_one = 0.9
beta_two = 0.95
adam_epsilon = 1e-08
rates = (0.05, 0.04, 0.25, 0.5, 0.5)
decays = (0.1, 0.1, 0.0, 0.0, 0.0)


def from_behind(array, axis, by):
    size = lax.axis_size(axis)
    pairs = [(i, i + by) for i in range(size) if 0 <= i + by < size]
    return lax.ppermute(array, axis, pairs)


def prefix(value, axis, join, neutral, backward):
    count, mine = (lax.axis_size(axis), lax.axis_index(axis))
    pieces = jax.tree.map(lambda part: lax.all_gather(part, axis), value)
    if backward:
        pieces = jax.tree.map(lambda part: part[::-1], pieces)
        mine = count - 1 - mine
    so_far = jax.tree.map(
        lambda part, zero: jnp.full_like(part, 0) + jnp.asarray(zero, part.dtype), value, neutral
    )

    def turn(position, so_far):
        longer = join(so_far, jax.tree.map(lambda part: part[position], pieces))
        return jax.tree.map(lambda new, old: jnp.where(position < mine, new, old), longer, so_far)

    return lax.fori_loop(0, count - 1, turn, so_far)


def rms_scale(values):
    return lax.rsqrt(jnp.mean(values * values, axis=-1, keepdims=True) + epsilon)


def front_norm(inputs, norm_gain):
    return inputs * rms_scale(inputs) * norm_gain


def block_step(carry_state, pieces):
    block_input, block_keys, block_query, block_sizes, block_decay = pieces
    length = block_input.shape[0]
    cumulative = jnp.cumsum(block_decay, axis=0)
    query_pos = lax.broadcasted_iota(jnp.int32, (length, length), 0)
    source_pos = lax.broadcasted_iota(jnp.int32, (length, length), 1)
    causal = (query_pos >= source_pos)[None]
    heads_first = jnp.transpose(cumulative)
    differ = heads_first[:, :, None] - heads_first[:, None, :]
    mixing = jnp.exp(jnp.where(causal, differ, -jnp.inf))
    contact = jnp.dot(block_query, jnp.transpose(block_keys), precision=highest)
    scaled_input = block_input * block_sizes[:, :, None]
    within = jnp.einsum("hts,shp->thp", mixing * contact[None], scaled_input, precision=highest)
    carried = (
        jnp.einsum("tn,hpn->thp", block_query, carry_state, precision=highest)
        * jnp.exp(cumulative)[:, :, None]
    )
    remaining = jnp.exp(cumulative[length - 1][None, :] - cumulative)
    added_state = jnp.einsum(
        "sh,shp,sn->hpn", remaining, scaled_input, block_keys, precision=highest
    )
    new_state = jnp.exp(cumulative[length - 1])[:, None, None] * carry_state + added_state
    return (new_state, within + carried)


def local_scan(head_values, state_keys, state_queries, step_sizes, log_decay):
    block_count = head_values.shape[0] // BLOCK
    stacked = (
        head_values.reshape(block_count, BLOCK, H, HD),
        state_keys.reshape(block_count, BLOCK, NS),
        state_queries.reshape(block_count, BLOCK, NS),
        step_sizes.reshape(block_count, BLOCK, H),
        log_decay.reshape(block_count, BLOCK, H),
    )
    initial = jnp.zeros((H, HD, NS), jnp.float32)
    final_state, outputs = lax.scan(jax.checkpoint(block_step), initial, stacked)
    return (outputs.reshape(block_count * BLOCK, H, HD), final_state, jnp.sum(log_decay, axis=0))


def incoming_term(state_queries, log_decay, state_in):
    cumulative = jnp.cumsum(log_decay, axis=0)
    return (
        jnp.einsum("tn,hpn->thp", state_queries, state_in, precision=highest)
        * jnp.exp(cumulative)[:, :, None]
    )


def mixer_inputs(rim_rows, mixed_in, step_raw, conv_params, head_params):
    length = mixed_in.shape[0]
    extended = jnp.concatenate([rim_rows, mixed_in], axis=0)
    conv_out = conv_params[KCONV] + sum(
        (conv_params[offset] * extended[offset : offset + length] for offset in range(KCONV))
    )
    activated = jax.nn.silu(conv_out)
    head_values = activated[:, :DI].reshape(length, H, HD)
    state_keys = activated[:, DI : DI + NS]
    state_queries = activated[:, DI + NS :]
    step_sizes = jax.nn.softplus(step_raw + head_params[0])
    log_decay = -jnp.exp(head_params[1]) * step_sizes
    return (head_values, state_keys, state_queries, step_sizes, log_decay)


def mixer_outputs(core_values, head_values, gate_raw, gate_gain, skip_weight):
    length = core_values.shape[0]
    with_skip = core_values + skip_weight[None, :, None] * head_values
    gated = with_skip.reshape(length, DI) * jax.nn.silu(gate_raw)
    return gated * rms_scale(gated) * gate_gain


def chain_forward(earlier, later):
    return (earlier[0] * later[0], later[0][:, None, None] * earlier[1] + later[1])


def chain_backward(earlier, later):
    return (later[0] * earlier[0], later[1] + later[0][:, None, None] * earlier[1])


def adam_update(master, first, second, gradient, rate, decay):
    first_new = beta_one * first + (1.0 - beta_one) * gradient
    second_new = beta_two * second + (1.0 - beta_two) * gradient * gradient
    scaled = (
        first_new
        / (1.0 - beta_one**STEP)
        / (jnp.sqrt(second_new / (1.0 - beta_two**STEP)) + adam_epsilon)
    )
    return (first_new, second_new, master - rate * (scaled + decay * master))


def on_device(
    hidden,
    cotangent,
    in_master,
    in_first,
    in_second,
    out_master,
    out_first,
    out_second,
    gain_master,
    gain_first,
    gain_second,
    conv_master,
    conv_first,
    conv_second,
    head_master,
    head_first,
    head_second,
):
    in_weights, out_weights, gain_low, conv_low, head_low = (
        lax.all_gather(in_master.astype(jnp.bfloat16), "shard", axis=0, tiled=True),
        lax.all_gather(out_master.astype(jnp.bfloat16), "shard", axis=0, tiled=True),
        lax.all_gather(gain_master.astype(jnp.bfloat16), "shard", axis=0, tiled=True),
        lax.all_gather(conv_master.astype(jnp.bfloat16), "shard", axis=1, tiled=True),
        lax.all_gather(head_master.astype(jnp.bfloat16), "shard", axis=1, tiled=True),
    )
    gains = gain_low.astype(jnp.float32)
    conv_params = conv_low.astype(jnp.float32)
    head_params = head_low.astype(jnp.float32)
    inputs = hidden[0].astype(jnp.float32)
    length = inputs.shape[0]
    rim_count = KCONV - 1
    normed, norm_pull = jax.vjp(front_norm, inputs, gains[:D])
    normed_low = normed.astype(jnp.bfloat16)
    project = jnp.dot(normed_low, in_weights, preferred_element_type=jnp.float32)
    gate_raw = project[:, :DI]
    mixed_in = project[:, DI : DI + CONVC]
    step_raw = project[:, DI + CONVC :]
    rim_rows = from_behind(mixed_in[length - rim_count :], "shard", 1)
    prepared, prepare_pull = jax.vjp(
        mixer_inputs, rim_rows, mixed_in, step_raw, conv_params, head_params
    )
    head_values, state_keys, state_queries, step_sizes, log_decay = prepared
    scanned, scan_pull = jax.vjp(
        local_scan, head_values, state_keys, state_queries, step_sizes, log_decay
    )
    core_local, state_local, total_log = scanned
    decay_local = jnp.exp(total_log)
    unused_decay, state_in = prefix(
        (decay_local, state_local),
        "shard",
        chain_forward,
        (jnp.ones_like(decay_local), jnp.zeros_like(state_local)),
        False,
    )
    incoming, incoming_pull = jax.vjp(incoming_term, state_queries, log_decay, state_in)
    mixed, output_pull = jax.vjp(
        mixer_outputs, core_local + incoming, head_values, gate_raw, gains[D:], head_params[2]
    )
    mixed_low = mixed.astype(jnp.bfloat16)
    layer_out = (
        inputs + jnp.dot(mixed_low, out_weights, preferred_element_type=jnp.float32)
    ).astype(jnp.bfloat16)
    upstream = cotangent[0]
    grad_out_w = lax.dot_general(
        mixed_low, upstream, (((0,), (0,)), ((), ())), preferred_element_type=jnp.float32
    )
    grad_mixed = lax.dot_general(
        upstream, out_weights, (((1,), (1,)), ((), ())), preferred_element_type=jnp.float32
    )
    grad_core, grad_skip_values, grad_gate_raw, grad_gate_gain, grad_skip = output_pull(grad_mixed)
    grad_queries_in, grad_log_in, grad_state_in = incoming_pull(grad_core)
    unused_back, adjoint = prefix(
        (decay_local, grad_state_in),
        "shard",
        chain_backward,
        (jnp.ones_like(decay_local), jnp.zeros_like(grad_state_in)),
        True,
    )
    grad_total_log = jnp.sum(adjoint * state_in, axis=(1, 2)) * decay_local
    grad_values, grad_keys, grad_queries, grad_steps, grad_log = scan_pull(
        (grad_core, adjoint, grad_total_log)
    )
    grads_prepared = (
        grad_values + grad_skip_values,
        grad_keys,
        grad_queries + grad_queries_in,
        grad_steps,
        grad_log + grad_log_in,
    )
    grad_rim, grad_mixed_in, grad_step_raw, grad_conv, grad_heads = prepare_pull(grads_prepared)
    rim_back = from_behind(grad_rim, "shard", -1)
    grad_mixed_in = jnp.concatenate(
        [grad_mixed_in[: length - rim_count], grad_mixed_in[length - rim_count :] + rim_back],
        axis=0,
    )
    grad_project = jnp.concatenate([grad_gate_raw, grad_mixed_in, grad_step_raw], axis=1).astype(
        jnp.bfloat16
    )
    grad_in_w = lax.dot_general(
        normed_low, grad_project, (((0,), (0,)), ((), ())), preferred_element_type=jnp.float32
    )
    grad_normed = lax.dot_general(
        grad_project, in_weights, (((1,), (1,)), ((), ())), preferred_element_type=jnp.float32
    )
    grad_inputs, grad_norm_gain = norm_pull(grad_normed)
    input_grad = (upstream.astype(jnp.float32) + grad_inputs).astype(jnp.bfloat16)
    grad_gains = jnp.concatenate([grad_norm_gain, grad_gate_gain])
    grad_heads = jnp.concatenate([grad_heads[:2], grad_heads[2:] + grad_skip[None]], axis=0)
    owned = (
        lax.psum_scatter(grad_in_w, "shard", scatter_dimension=0, tiled=True),
        lax.psum_scatter(grad_out_w, "shard", scatter_dimension=0, tiled=True),
        lax.psum_scatter(grad_gains, "shard", scatter_dimension=0, tiled=True),
        lax.psum_scatter(grad_conv, "shard", scatter_dimension=1, tiled=True),
        lax.psum_scatter(grad_heads, "shard", scatter_dimension=1, tiled=True),
    )
    totals = lax.psum((owned[0], owned[1], owned[2], owned[3], owned[4]), "dp")
    masters = (in_master, out_master, gain_master, conv_master, head_master)
    firsts = (in_first, out_first, gain_first, conv_first, head_first)
    seconds = (in_second, out_second, gain_second, conv_second, head_second)
    updated = [
        adam_update(
            masters[group],
            firsts[group],
            seconds[group],
            totals[group],
            rates[group],
            decays[group],
        )
        for group in range(5)
    ]
    return (
        layer_out[None],
        input_grad[None],
        updated[0][0],
        updated[0][1],
        updated[0][2],
        updated[1][0],
        updated[1][1],
        updated[1][2],
        updated[2][0],
        updated[2][1],
        updated[2][2],
        updated[3][0],
        updated[3][1],
        updated[3][2],
        updated[4][0],
        updated[4][1],
        updated[4][2],
    )


def solution(mesh):
    return jax.shard_map(
        on_device,
        mesh=mesh,
        in_specs=(
            P("dp", "shard", None),
            P("dp", "shard", None),
            P("shard", None),
            P("shard", None),
            P("shard", None),
            P("shard", None),
            P("shard", None),
            P("shard", None),
            P("shard"),
            P("shard"),
            P("shard"),
            P(None, "shard"),
            P(None, "shard"),
            P(None, "shard"),
            P(None, "shard"),
            P(None, "shard"),
            P(None, "shard"),
        ),
        out_specs=(
            P("dp", "shard", None),
            P("dp", "shard", None),
            P("shard", None),
            P("shard", None),
            P("shard", None),
            P("shard", None),
            P("shard", None),
            P("shard", None),
            P("shard"),
            P("shard"),
            P("shard"),
            P(None, "shard"),
            P(None, "shard"),
            P(None, "shard"),
            P(None, "shard"),
            P(None, "shard"),
            P(None, "shard"),
        ),
        check_vma=False,
    )
```

profile of v0, /device:TPU:1, one launch (start us, length us, event | category | flops | bytes accessed | tf_op | source)
XLA Modules:
  0.0 1448.1 jit_solution(10485759423773860838)
XLA Ops:
  7.2 4.1 convert_element_type.53
  12.1 18.0 %all-gather.4 = bf16[8,6,3]{1,2,0:T(4,128)(2,1)S(1)} all-gather(bf16[1,6,3]{1,2,0:T(4,128)(2,1)S(1)} %convert_bitcast_fusion.1), channel_id=1, replica_groups=mesh['dp'=16,'shard'=8] {'shard'}, dimensions={0}, use_global_device_ids=true | all-gather | bytes 324 | tf_op jit(solution)/shard_map/all_gather | solution.py:169
  31.7 27.3 %all-reduce.16 = bf16[4608]{0:T(1024)(128)(2,1)S(1)} all-reduce(bf16[4608]{0:T(1024)(128)(2,1)S(1)} %dynamic-update-slice), channel_id=1, replica_groups=mesh['dp'=16,'shard'=8] {'shard'}, use_global_device_ids=true, to_apply=%add.16 | all-reduce | flops 4608 | bytes 18432
  59.6 24.5 %all-gather.3 = bf16[8,416,5]{1,2,0:T(8,128)(2,1)S(1)} all-gather(bf16[1,416,5]{1,2,0:T(8,128)(2,1)S(1)} %convert_bitcast_fusion), channel_id=1, replica_groups=mesh['dp'=16,'shard'=8] {'shard'}, dimensions={0}, use_global_device_ids=true | all-gather | bytes 37440 | tf_op jit(solution)/shard_map/all_gather | solution.py:168
  85.7 131.9 %all-gather.10.cloned.1.call-done = bf16[1536,6448]{1,0:T(8,128)(2,1)} async-done(((bf16[192,6448]{1,0:T(8,128)(2,1)}), bf16[1536,6448]{1,0:T(8,128)(2,1)}) %all-gather.10.cloned.1.call-update) | async-done | bytes 19808272 | tf_op jit(solution)/shard_map/all_gather | solution.py:165
  217.6 12.2 fusion.98
  233.5 2.6 copy.215
  246.4 3.5 fusion.45
  250.0 2.8 convert_element_type.57
  253.6 2.7 slice.129
  256.4 15.0 %all-reduce.17 = f32[384]{0:T(512)S(1)} all-reduce(f32[384]{0:T(512)S(1)} %exponential_dynamic-update-slice_fusion), channel_id=2, replica_groups=mesh['dp'=16,'shard'=8] {'shard'}, use_global_device_ids=true, to_apply=%add.17 | all-reduce | flops 384 | bytes 3072
  271.6 3.1 copy.251
  275.8 7.4 fusion.5
  283.2 100.5 %all-gather.14.cloned.1.call-done = f32[384,64,128]{2,1,0:T(8,128)} async-done(((f32[48,64,128]{2,1,0:T(8,128)}), f32[384,64,128]{2,1,0:T(8,128)}) %all-gather.14.cloned.1.call-update) | async-done | bytes 12582928 | tf_op jit(solution)/shard_map/all_gather | solution.py:34
  383.6 12.8 while.18
  399.0 3.7 fusion.27
  402.7 3.0 copy.226
  405.7 2.5 multiply_reduce_fusion.14
  409.3 76.7 %all-gather.12.cloned.1.call-done = bf16[3072,1536]{1,0:T(8,128)(2,1)} async-done(((bf16[384,1536]{1,0:T(8,128)(2,1)}), bf16[3072,1536]{1,0:T(8,128)(2,1)}) %all-gather.12.cloned.1.call-update) | async-done | bytes 9437200 | tf_op jit(solution)/shard_map/all_gather | solution.py:166
  486.0 7.7 multiply_reduce_fusion.7
  493.7 3.3 multiply_reduce_fusion.6
  498.9 3.5 fusion.54
  502.4 9.7 fusion.90
  518.2 2.9 multiply_reduce_fusion.8
  524.1 2.6 reduce_window_sum.44
  526.6 4.7 fusion.60
  531.3 101.2 %all-gather.16.cloned.1.call-done = f32[384,64,128]{2,1,0:T(8,128)} async-done(((f32[48,64,128]{2,1,0:T(8,128)}), f32[384,64,128]{2,1,0:T(8,128)}) %all-gather.16.cloned.1.call-update) | async-done | bytes 12582928 | tf_op jit(solution)/shard_map/all_gather | solution.py:34
  632.6 12.4 rev.6
  644.9 17.5 %while.19 = (s32[]{:T(128)}, f32[48,64,128]{2,1,0:T(8,128)S(1)}, s32[]{:T(128)}, f32[8,48,64,128]{3,2,1,0:T(8,128)}, f32[8,48]{1,0:T(8,128)}, /*index=5*/s32[]{:T(128)}, s32[]{:T(128)}) while((s32[]{:T(128)}, f32[48,64,128]{2,1,0:T(8,128)S(1)}, s32[]{:T(128)}, f32[8,48,64,128]{3,2,1,0:T(8,128)}, f32[8,48]{1,0:T(8,128)}, ...), condition=%wide.region_8.9_spmd.clone, body=%wide.region_7.8_spmd.clone.sunk | while | flops 1572868 | bytes 4719281 | solution.py:46
  678.3 5.5 multiply_reduce_fusion.5
  683.8 3.1 copy.235
  691.2 3.6 multiply_reduce_fusion.9
  694.9 8.5 fusion.14
  705.5 2.6 reduce_window_sum.43
  708.1 4.7 fusion.63
  712.9 2.7 fusion.66
  718.3 2.6 multiply_reduce_fusion.3
  724.5 3.8 collective-permute-done.1
  728.4 16.7 %fusion.94 = f32[1536,6448]{1,0:T(8,128)} fusion(bf16[128,48]{1,0:T(8,128)(2,1)S(1)} %get-tuple-element.391, bf16[3,3328]{1,0:T(4,128)(2,1)S(1)} %fusion.111, bf16[125,3328]{1,0:T(8,128)(2,1)S(1)} %slice.201, bf16[128,3072]{1,0:T(8,128)(2,1)S(1)} %copy-done.25, bf16[1,128,1536]{2,1,0:T(8,128)(2,1)S(1)} %copy-done.20, f32[1536]{0:T(1024)S(1)} %copy-done.32, ...), kind=kOutput, calls=%fused_computation.140 | convolution fusion | flops 2542845952 | bytes 41667072 | tf_op jit(solution)/shard_map/dot_general | solution.py:244
  747.8 77.1 %reduce-scatter.9.cloned.1.call-done = f32[384,1536]{1,0:T(8,128)} async-done(((f32[3072,1536]{1,0:T(8,128)}), f32[384,1536]{1,0:T(8,128)}) %reduce-scatter.9.cloned.1.call-update) | async-done | bytes 2359312 | tf_op jit(solution)/shard_map/reduce_scatter | solution.py:256
  824.9 392.5 %reduce-scatter.7.cloned.1.call-done = f32[192,6448]{1,0:T(8,128)} async-done(((f32[1536,6448]{1,0:T(8,128)}), f32[192,6448]{1,0:T(8,128)}) %reduce-scatter.7.cloned.1.call-update) | async-done | bytes 4952080 | tf_op jit(solution)/shard_map/reduce_scatter | solution.py:255
  1219.1 6.0 fusion.12
  1225.8 10.2 fusion.73
  1236.1 25.3 %all-reduce.22 = (f32[4608]{0:T(1024)S(1)}, f32[3,48]{1,0:T(4,128)S(1)}) all-reduce(f32[4608]{0:T(1024)S(1)} %pad_maximum_fusion.4, f32[3,48]{1,0:T(4,128)S(1)} %pad_maximum_fusion.5), channel_id=7, replica_groups=mesh['dp'=16,'shard'=8] {'shard'}, use_global_device_ids=true, to_apply=%region_28.29.clone | all-reduce | flops 4752 | bytes 38016
  1263.7 66.0 %all-reduce.20 = (f32[576]{0:T(1024)S(1)}, f32[5,416]{1,0:T(8,128)S(1)}, f32[3,6]{1,0:T(4,128)S(1)}) all-reduce(f32[576]{0:T(1024)S(1)} %dynamic-slice.11, f32[5,416]{1,0:T(8,128)S(1)} %copy.246, f32[3,6]{1,0:T(4,128)S(1)} %constant_dynamic-slice_fusion), channel_id=1, replica_groups=mesh['dp'=16,'shard'=8] {'dp'}, use_global_device_ids=true, to_apply=%region_29.30 | all-reduce | flops 2674 | bytes 21392 | tf_op jit(solution)/shard_map/psum | solution.py:261
  1331.6 90.7 %all-reduce.25.cloned.1.call-done = (f32[192,6448]{1,0:T(8,128)}, f32[384,1536]{1,0:T(8,128)}) async-done(((f32[192,6448]{1,0:T(8,128)}, f32[384,1536]{1,0:T(8,128)}), (f32[192,6448]{1,0:T(8,128)}, f32[384,1536]{1,0:T(8,128)})) %all-reduce.25.cloned.1.call-update) | async-done | bytes 7311376 | tf_op jit(solution)/shard_map/psum | solution.py:261
  1422.3 8.2 multiply_subtract_fusion.1
  1430.4 10.6 multiply_subtract_fusion
  (368 shorter events, 99.6 us)
Async XLA Ops:
  7.2 210.4 %all-gather.10.cloned.1.call-start = ((), (), s32[]{:S(2)}) async-start(), calls=%async_computation.3 | async-start | bytes 22560768 | tf_op jit(solution)/shard_map/all_gather | solution.py:165
  11.4 18.8 %copy-start.102 = (u32[128]{0:T(128)S(1)}, u32[128]{0:T(128)}, u32[]{:S(2)}) copy-start(u32[128]{0:T(128)} %constant.239) | copy-start | bytes 1540
  11.4 47.6 %copy-start.73 = (f32[5,416]{1,0:T(8,128)S(1)}, f32[5,416]{1,0:T(8,128)}, u32[]{:S(2)}) copy-start(f32[5,416]{1,0:T(8,128)} %param.32) | copy-start | bytes 24964
  11.4 73.6 %copy-start.19 = (bf16[1,128,1536]{2,1,0:T(8,128)(2,1)S(1)}, bf16[1,128,1536]{2,1,0:T(8,128)(2,1)}, u32[]{:S(2)}) copy-start(bf16[1,128,1536]{2,1,0:T(8,128)(2,1)} %param.21) | copy-start | bytes 1179652
  11.4 372.2 %all-gather.14.cloned.1.call-start = ((), (), s32[]{:S(2)}) async-start(), calls=%async_computation.7 | async-start | bytes 14155776 | tf_op jit(solution)/shard_map/all_gather | solution.py:34
  30.2 199.7 %copy-start.92 = (f32[48,3]{0,1:T(4,128)}, f32[48,3]{0,1:T(4,128)S(1)}, u32[]{:S(2)}) copy-start(f32[48,3]{0,1:T(4,128)S(1)} %reshape.273) | copy-start | bytes 1732
  59.0 170.8 %copy-start.31 = (f32[1536]{0:T(1024)}, f32[1536]{0:T(1024)S(1)}, u32[]{:S(2)}) copy-start(f32[1536]{0:T(1024)S(1)} %slice.114) | copy-start | bytes 18436
  85.2 144.7 %copy-start.103 = (f32[128]{0:T(128)}, f32[128]{0:T(128)S(1)}, u32[]{:S(2)}) copy-start(f32[128]{0:T(128)S(1)} %fusion.76) | copy-start | bytes 1540
  85.7 146.3 %copy-start.93 = (f32[48]{0:T(128)}, f32[48]{0:T(128)S(1)}, u32[]{:S(2)}) copy-start(f32[48]{0:T(128)S(1)} %get-tuple-element.423) | copy-start | bytes 580
  85.7 146.3 %copy-start.95 = (f32[48]{0:T(128)}, f32[48]{0:T(128)S(1)}, u32[]{:S(2)}) copy-start(f32[48]{0:T(128)S(1)} %get-tuple-element.424) | copy-start | bytes 580
  229.9 8.0 copy-start.10
  232.8 38.6 %copy-start.28 = (f32[128,48]{1,0:T(8,128)}, f32[128,48]{1,0:T(8,128)S(1)}, u32[]{:S(2)}) copy-start(f32[128,48]{1,0:T(8,128)S(1)} %reduce_window_sum.41) | copy-start | bytes 73732
  236.1 6.0 collective-permute-start
  246.3 152.7 %copy-start.6 = (f32[128,3072]{0,1:T(8,128)}, f32[128,3072]{0,1:T(8,128)S(1)}, u32[]{:S(2)}) copy-start(f32[128,3072]{0,1:T(8,128)S(1)} %copy.217) | copy-start | bytes 4718596
  249.9 236.0 %all-gather.12.cloned.1.call-start = ((), (), s32[]{:S(2)}) async-start(), calls=%async_computation.4 | async-start | bytes 10616832 | tf_op jit(solution)/shard_map/all_gather | solution.py:166
  252.9 18.6 %copy-start.40 = (f32[128,48]{1,0:T(8,128)S(1)}, f32[128,48]{1,0:T(8,128)}, u32[]{:S(2)}) copy-start(f32[128,48]{1,0:T(8,128)} %get-tuple-element.416) | copy-start | bytes 73732
  252.9 379.7 %all-gather.16.cloned.1.call-start = ((), (), s32[]{:S(2)}) async-start(), calls=%async_computation.8 | async-start | bytes 14155776 | tf_op jit(solution)/shard_map/all_gather | solution.py:34
  253.6 22.2 %copy-start.85 = (pred[128,128]{1,0:T(8,128)(4,1)}, pred[128,128]{1,0:T(8,128)(4,1)S(1)}, u32[]{:S(2)}) copy-start(pred[128,128]{1,0:T(8,128)(4,1)S(1)} %iota_compare_fusion) | copy-start | bytes 49156
  271.6 127.4 %copy-start.38 = (f32[128,48]{0,1:T(8,128)}, f32[128,48]{0,1:T(8,128)S(1)}, u32[]{:S(2)}) copy-start(f32[128,48]{0,1:T(8,128)S(1)} %copy.223) | copy-start | bytes 73732
  405.7 80.3 %copy-start.24 = (bf16[1,128,1536]{2,1,0:T(8,128)(2,1)S(1)}, bf16[1,128,1536]{2,1,0:T(8,128)(2,1)}, u32[]{:S(2)}) copy-start(bf16[1,128,1536]{2,1,0:T(8,128)(2,1)} %param.22) | copy-start | bytes 1179652
  408.3 85.4 %copy-start.3 = (f32[128,3072]{1,0:T(8,128)}, f32[128,3072]{1,0:T(8,128)S(1)}, u32[]{:S(2)}) copy-start(f32[128,3072]{1,0:T(8,128)S(1)} %get-tuple-element.401) | copy-start | bytes 4718596
  486.0 7.7 copy-start.12
  486.0 7.7 copy-start.15
  486.0 7.7 copy-start.16
  486.0 7.7 copy-start.79
  502.4 322.5 %reduce-scatter.9.cloned.1.call-start = ((), (), s32[]{:S(2)}) async-start(), calls=%async_computation.6 | async-start | bytes 21233664 | tf_op jit(solution)/shard_map/reduce_scatter | solution.py:256
  512.2 705.3 %reduce-scatter.7.cloned.1.call-start = ((), (), s32[]{:S(2)}) async-start(), calls=%async_computation.5 | async-start | bytes 45121536 | tf_op jit(solution)/shard_map/reduce_scatter | solution.py:255
  676.0 7.8 copy-start.71
  694.8 8.6 copy-start.33
  694.8 8.6 copy-start.60
  694.8 8.5 copy-start.61
  694.8 8.5 copy-start.62
  694.9 8.5 copy-start.89
  721.5 6.8 collective-permute-start.1
  745.1 517.5 %reduce-scatter.11.cloned.1.call-start = ((), (), s32[]{:S(2)}) async-start(), calls=%async_computation.9 | async-start | bytes 1916928
  747.7 674.5 %all-reduce.25.cloned.1.call-start = ((), (), s32[]{:S(2)}) async-start(), calls=%async_computation.10 | async-start | bytes 14745600 | tf_op jit(solution)/shard_map/psum | solution.py:261
  1225.8 10.3 copy-start.75
  1225.8 35.8 %copy-start.104 = (f32[128]{0:T(128)S(1)}, f32[128]{0:T(128)}, u32[]{:S(2)}) copy-start(f32[128]{0:T(128)} %copy-done.103) | copy-start | bytes 1540
  1236.0 93.7 %copy-start.91 = (f32[3,6]{1,0:T(4,128)S(1)}, f32[3,6]{1,0:T(4,128)}, u32[]{:S(2)}) copy-start(f32[3,6]{1,0:T(4,128)} %param.35) | copy-start | bytes 220
  1236.0 93.7 %copy-start.100 = (f32[3,6]{1,0:T(4,128)S(1)}, f32[3,6]{1,0:T(4,128)}, u32[]{:S(2)}) copy-start(f32[3,6]{1,0:T(4,128)} %param.37) | copy-start | bytes 220
  1236.0 93.7 %copy-start.101 = (f32[3,6]{1,0:T(4,128)S(1)}, f32[3,6]{1,0:T(4,128)}, u32[]{:S(2)}) copy-start(f32[3,6]{1,0:T(4,128)} %param.36) | copy-start | bytes 220
  1236.1 94.3 %copy-start.84 = (f32[576]{0:T(1024)S(1)}, f32[576]{0:T(1024)}, u32[]{:S(2)}) copy-start(f32[576]{0:T(1024)} %param.29) | copy-start | bytes 6916
  1236.1 94.3 %copy-start.98 = (f32[576]{0:T(1024)S(1)}, f32[576]{0:T(1024)}, u32[]{:S(2)}) copy-start(f32[576]{0:T(1024)} %param.31) | copy-start | bytes 6916
  1236.1 94.3 %copy-start.99 = (f32[576]{0:T(1024)S(1)}, f32[576]{0:T(1024)}, u32[]{:S(2)}) copy-start(f32[576]{0:T(1024)} %param.30) | copy-start | bytes 6916
  1236.1 94.9 %copy-start.74 = (f32[5,416]{1,0:T(8,128)S(1)}, f32[5,416]{1,0:T(8,128)}, u32[]{:S(2)}) copy-start(f32[5,416]{1,0:T(8,128)} %param.32) | copy-start | bytes 24964
  1236.1 94.9 %copy-start.81 = (f32[5,416]{1,0:T(8,128)S(1)}, f32[5,416]{1,0:T(8,128)}, u32[]{:S(2)}) copy-start(f32[5,416]{1,0:T(8,128)} %param.34) | copy-start | bytes 24964
  1236.1 94.9 %copy-start.82 = (f32[5,416]{1,0:T(8,128)S(1)}, f32[5,416]{1,0:T(8,128)}, u32[]{:S(2)}) copy-start(f32[5,416]{1,0:T(8,128)} %param.33) | copy-start | bytes 24964
  1422.3 8.2 copy-start.23
  (72 other events, 198.3 us)
Sparse Core Ops, SparseCore 0:
  11.5 206.0 all-gather.9
  250.0 133.5 all-gather.13
  385.3 100.6 all-gather.11
  502.5 130.0 all-gather.15
  634.9 189.9 reduce-scatter.8
  827.2 390.1 reduce-scatter.6
  1220.4 34.9 reduce-scatter.10
  1258.2 164.0 all-reduce.24
where the time goes:
time: 1460 us; the launch traced here: 1450 us
  waiting for transfers between devices  974 us (67%)
  blocking collectives  176 us (12%)
  matrix products  118 us (8%)
  other arithmetic  86.9 us (6%)
  local copies, waits for them, and re-layouts  70.5 us (5%)
  between operations  18.6 us (1%)
    reduce_scatter x1, waiting for transfers between devices, on_device(): lax.psum_scatter(grad_in_w, 'shard', scatter_dimension=0, tiled=True)  393 us
    all_gather x2, waiting for transfers between devices, prefix(): pieces = jax.tree.map(lambda part: lax.all_gather(part, axis), value)  202 us
    all_gather x1, waiting for transfers between devices, on_device(): lax.all_gather(in_master.astype(jnp.bfloat16), 'shard', axis=0, tiled=True)  132 us
    psum x1, waiting for transfers between devices, on_device(): totals = lax.psum((owned[0], owned[1], owned[2], owned[3], owned[4]), 'dp')  90.7 us
    reduce_scatter x1, waiting for transfers between devices, on_device(): lax.psum_scatter(grad_out_w, 'shard', scatter_dimension=0, tiled=True)  77.1 us
    all_gather x1, waiting for transfers between devices, on_device(): lax.all_gather(out_master.astype(jnp.bfloat16), 'shard', axis=0, tiled=True)  76.7 us
    unnamed x3, blocking collectives  67.6 us
    psum x1, blocking collectives, on_device(): totals = lax.psum((owned[0], owned[1], owned[2], owned[3], owned[4]), 'dp')  66 us
  transfers between devices with their start and end apart: 10, of which 8 were waited for; matrix products, arithmetic and copies ran while one was open for 14% of the time, Pallas kernels for 0%

commit v1 on v0

v1 whole, which is shorter than its diff:
```python
import functools

import jax
import jax.numpy as jnp
from jax import lax
from jax.experimental import pallas as pl
from jax.experimental.pallas import tpu as pltpu
from jax.sharding import PartitionSpec as P

D = 1536
DI = 3072
H = 48
HD = 64
NS = 128
KCONV = 4
STEP = 5
BLOCK = 128
CONVC = 3328
PROJ = 6448
LEN = 1024
OWN = 384
COLS = 1152
WIDE = 6528
BLOCKS = LEN // BLOCK

f32 = jnp.float32
bf16 = jnp.bfloat16
highest = lax.Precision.HIGHEST
MESH = pl.DeviceIdType.MESH
epsilon = 1e-05
beta_one = 0.9
beta_two = 0.95
adam_epsilon = 1e-08
rates = (0.05, 0.04, 0.25, 0.5, 0.5)
decays = (0.1, 0.1, 0.0, 0.0, 0.0)
VMEM_LIMIT = 60 * 2**20


class Place:
    def __init__(self):
        self.d = lax.axis_index("dp")
        self.s = lax.axis_index("shard")
        self.c = lax.rem(self.d, 2)
        self.x = lax.rem(self.d // 2, 4)
        self.yh = self.d // 8
        self.big = self.d // 2
        self.z = lax.rem(self.s, 4)
        self.yl = self.s // 4

    def shard_of(self, k):
        return lax.rem(self.yl + k // 4, 2) * 4 + lax.rem(self.z + k % 4, 4)

    def shard_peer(self, k):
        return (self.d, self.shard_of(k))

    def big_of(self, k):
        return lax.rem(self.yh + k // 4, 2) * 4 + lax.rem(self.x + k % 4, 4)

    def big_peer(self, k):
        return (self.big_of(k) * 2 + self.c, self.s)

    def core_peer(self):
        return (self.big * 2 + 1 - self.c, self.s)

    def other_core_of(self, k):
        return (self.big_of(k) * 2 + 1 - self.c, self.s)


ORDER = (6, 2, 5, 7, 1, 3, 4)


def exchange(cid, body, ins, outs, sems, locals_):
    def kernel(*refs):
        in_refs = refs[: len(ins)]
        out_refs = refs[len(ins) : len(ins) + len(outs)]
        send, recv, own = refs[len(ins) + len(outs) :]
        place = Place()

        def meet(peers):
            barrier = pltpu.get_barrier_semaphore()
            for peer in peers:
                pl.semaphore_signal(barrier, inc=1, device_id=peer, device_id_type=MESH)
            pl.semaphore_wait(barrier, len(peers))

        def remote(src, dst, index, peer):
            return pltpu.make_async_remote_copy(
                src_ref=src,
                dst_ref=dst,
                send_sem=send.at[index],
                recv_sem=recv.at[index],
                device_id=peer,
                device_id_type=MESH,
            )

        def local(src, dst, index):
            return pltpu.make_async_copy(src, dst, own.at[index])

        body(place, meet, remote, local, in_refs, out_refs)

    any_spec = pl.BlockSpec(memory_space=pl.ANY)
    return pl.pallas_call(
        kernel,
        out_shape=outs,
        in_specs=[any_spec] * len(ins),
        out_specs=tuple([any_spec] * len(outs)),
        scratch_shapes=[
            pltpu.SemaphoreType.DMA((sems,)),
            pltpu.SemaphoreType.DMA((sems,)),
            pltpu.SemaphoreType.DMA((max(locals_, 1),)),
        ],
        compiler_params=pltpu.CompilerParams(collective_id=cid, has_side_effects=True),
    )(*ins)


def gather_body(place, meet, remote, local, ins, outs):
    hid, cot, wide, small = ins
    u_out, ct_out, w_out, sm_out = outs
    meet([place.shard_peer(k) for k in ORDER])
    me = place.s
    copies = []
    own = [
        local(hid, u_out.at[me], 0),
        local(cot, ct_out.at[me], 1),
        local(small, sm_out.at[me], 2),
    ]

    def weight_parts(k):
        them = place.shard_of(k)
        at = pl.multiple_of(them * OWN, 128)
        return (
            (wide.at[:, pl.ds(at, OWN)], w_out.at[me, :, pl.ds(0, OWN)]),
            (wide.at[:, pl.ds(at + DI, OWN)], w_out.at[me, :, pl.ds(OWN, OWN)]),
            (wide.at[:, pl.ds(2 * DI, OWN)], w_out.at[me, :, pl.ds(2 * OWN, OWN)]),
        )

    for i, (src, dst) in enumerate(weight_parts(0)):
        own.append(local(src, dst, 3 + i))
    for copy in own:
        copy.start()
    for n, k in enumerate(ORDER):
        peer = place.shard_peer(k)
        copies.append(remote(small, sm_out.at[me], n, peer))
    for n, k in enumerate(ORDER):
        peer = place.shard_peer(k)
        for i, (src, dst) in enumerate(weight_parts(k)):
            copies.append(remote(src, dst, 7 + 3 * n + i, peer))
    for n, k in enumerate(ORDER):
        copies.append(remote(hid, u_out.at[me], 28 + n, place.shard_peer(k)))
    for n, k in enumerate(ORDER):
        copies.append(remote(cot, ct_out.at[me], 35 + n, place.shard_peer(k)))
    for copy in copies:
        copy.start()
    for copy in own + copies:
        copy.wait()


def all_body(place, meet, remote, local, ins, outs):
    (block,) = ins
    (out,) = outs
    meet([place.shard_peer(k) for k in ORDER])
    own = local(block, out.at[place.s], 0)
    own.start()
    copies = [
        remote(block, out.at[place.s], n, place.shard_peer(k)) for n, k in enumerate(ORDER)
    ]
    for copy in copies:
        copy.start()
    own.wait()
    for copy in copies:
        copy.wait()


def scatter_body(place, meet, remote, local, ins, outs):
    meet([place.shard_peer(k) for k in ORDER])
    copies = []
    for a in range(len(ins)):
        copies.append(local(ins[a].at[place.s], outs[a].at[place.s], a))
    for n, k in enumerate(ORDER):
        for a in range(len(ins)):
            copies.append(
                remote(
                    ins[a].at[place.shard_of(k)],
                    outs[a].at[place.s],
                    n * len(ins) + a,
                    place.shard_peer(k),
                )
            )
    for copy in copies:
        copy.start()
    for copy in copies:
        copy.wait()


def swap_body(place, meet, remote, local, ins, outs):
    gw, go = ins
    gw_out, go_out = outs
    meet([place.core_peer()])
    other = 1 - place.c
    copies = [
        remote(gw.at[pl.ds(other * 4, 4)], gw_out, 0, place.core_peer()),
        remote(
            go.at[:, :, pl.ds(pl.multiple_of(other * 768, 128), 768)],
            go_out,
            1,
            place.core_peer(),
        ),
    ]
    for copy in copies:
        copy.start()
    for copy in copies:
        copy.wait()


def reduce_body(place, meet, remote, local, ins, outs):
    hw, ho = ins
    hw_out, ho_out = outs
    meet([place.big_peer(k) for k in ORDER])
    copies = [
        local(hw.at[:, place.big], hw_out.at[0], 0),
        local(ho.at[place.big], ho_out.at[0], 1),
    ]
    for n, k in enumerate(ORDER):
        them = place.big_of(k)
        copies.append(remote(hw.at[:, them], hw_out.at[k], 2 * n, place.big_peer(k)))
        copies.append(remote(ho.at[them], ho_out.at[k], 2 * n + 1, place.big_peer(k)))
    for copy in copies:
        copy.start()
    for copy in copies:
        copy.wait()


def owner_body(place, meet, remote, local, ins, outs):
    piece, small = ins
    piece_out, small_out = outs
    meet([place.shard_peer(k) for k in ORDER])
    valid = place.yl == place.c
    own_small = local(small, small_out.at[place.s], 0)
    own_small.start()
    own_piece = local(piece.at[place.z], piece_out.at[place.s], 1)

    @pl.when(valid)
    def _():
        own_piece.start()

    smalls = [
        remote(small, small_out.at[place.s], n, place.shard_peer(k))
        for n, k in enumerate(ORDER)
    ]
    for copy in smalls:
        copy.start()
    pieces = []
    for n, k in enumerate(ORDER):
        them = place.shard_of(k)
        copy = remote(
            piece.at[lax.rem(them, 4)], piece_out.at[place.s], 7 + n, place.shard_peer(k)
        )
        goes = them // 4 == place.c
        pl.when(goes)(copy.start)
        pieces.append((copy, goes))
    own_small.wait()
    pl.when(valid)(own_piece.wait)
    for copy in smalls:
        copy.wait()
    for copy, goes in pieces:
        pl.when(goes)(copy.wait_send)
        pl.when(valid)(copy.wait_recv)


def spread_body(place, meet, remote, local, ins, outs):
    slab, go, small = ins
    slab_out, go_out, small_out = outs
    core = place.core_peer()
    everyone = [place.big_peer(k) for k in ORDER] + [core]
    everyone += [place.other_core_of(k) for k in ORDER]
    meet(everyone)
    valid = place.yl == place.c
    at = pl.multiple_of(place.c * 768, 128)

    def half(index):
        return go_out.at[index, :, pl.ds(at, 768)]

    other_at = pl.multiple_of((1 - place.c) * 768, 128)
    own_small = local(small, small_out.at[place.d], 0)
    own_go = local(go, half(place.big), 1)
    own_slab = local(slab, slab_out.at[place.big], 2)
    own_small.start()
    own_go.start()
    smalls = [
        remote(small, small_out.at[place.d], n, peer) for n, peer in enumerate(everyone)
    ]
    slabs = [
        remote(slab, slab_out.at[place.big], 15 + n, place.big_peer(k))
        for n, k in enumerate(ORDER)
    ]
    gos = [
        remote(go, half(place.big), 22 + n, place.big_peer(k)) for n, k in enumerate(ORDER)
    ]
    to_core_slab = remote(slab, slab_out.at[place.big], 29, core)
    to_core_go = remote(go, half(place.big), 30, core)

    @pl.when(valid)
    def _():
        own_slab.start()
        for copy in slabs:
            copy.start()
        to_core_slab.start()

    for copy in gos:
        copy.start()
    to_core_go.start()
    for copy in smalls:
        copy.start()
    forward_gos = []
    forward_slabs = []
    for n, k in enumerate(ORDER):
        origin = lax.rem(place.yh + k // 4, 2) * 4 + lax.rem(place.x + 4 - k % 4, 4)
        gos[n].wait_recv()
        go_copy = remote(half(origin), half(origin), 31 + n, core)
        go_copy.start()
        forward_gos.append(go_copy)
        slab_copy = remote(slab_out.at[origin], slab_out.at[origin], 38 + n, core)

        @pl.when(valid)
        def _(n=n, slab_copy=slab_copy):
            slabs[n].wait_recv()
            slab_copy.start()

        forward_slabs.append(slab_copy)
    own_small.wait()
    own_go.wait()
    for copy in smalls:
        copy.wait()
    for copy in gos:
        copy.wait_send()
    to_core_go.wait()
    for copy in forward_gos:
        copy.wait()

    @pl.when(valid)
    def _():
        own_slab.wait()
        for copy in slabs:
            copy.wait_send()
        to_core_slab.wait_send()
        for copy in forward_slabs:
            copy.wait_send()

    @pl.when(jnp.logical_not(valid))
    def _():
        to_core_slab.wait_recv()
        for copy in forward_slabs:
            copy.wait_recv()


def dot(a, b, ca, cb, precision=None):
    return lax.dot_general(
        a, b, (((ca,), (cb,)), ((), ())), precision=precision, preferred_element_type=f32
    )


def mm(a, b, ca=1, cb=0):
    return dot(a.astype(f32), b.astype(f32), ca, cb, highest)


def lanes(shape):
    return lax.broadcasted_iota(jnp.int32, shape, 1)


def rows_of(shape):
    return lax.broadcasted_iota(jnp.int32, shape, 0)


def widen(m):
    low = lanes((m.shape[0], 128)) < HD
    return jnp.concatenate(
        [jnp.where(low, m[:, 2 * i : 2 * i + 1], m[:, 2 * i + 1 : 2 * i + 2]) for i in range(3)],
        axis=1,
    )


def lower_ones():
    return (rows_of((BLOCK, BLOCK)) >= lanes((BLOCK, BLOCK))).astype(f32)


def head_ones():
    return (rows_of((OWN, BLOCK)) // HD == lanes((OWN, BLOCK))).astype(f32)


def split_pair(pair):
    low = lanes(pair.shape) < HD
    zero = jnp.zeros_like(pair)
    return jnp.concatenate([jnp.where(low, pair, zero), jnp.where(low, zero, pair)], axis=0)


def decay_parts(log_decay):
    cumulative = dot(lower_ones(), log_decay, 1, 0, highest)
    return cumulative, cumulative.T, widen(cumulative)


def head_mixing(cumulative, turned, h):
    causal = rows_of((BLOCK, BLOCK)) >= lanes((BLOCK, BLOCK))
    differ = cumulative[:, h : h + 1] - turned[h : h + 1, :]
    return jnp.exp(jnp.where(causal, differ, -jnp.inf))


def softplus(v):
    return jnp.maximum(v, 0.0) + jnp.log1p(jnp.exp(-jnp.abs(v)))


TB = 256


def forward_kernel(
    u_ref, ct_ref, w_ref, wo_ref, gn_ref, gg_ref, cv_ref, hd_ref, sk_ref,
    n_ref, z_ref, xbc_ref, cvo_ref, raw_ref, core_ref, dm_ref, st_ref, sums_ref,
    state, halo,
):
    i = pl.program_id(0)

    @pl.when(i == 0)
    def _():
        state[...] = jnp.zeros_like(state)
        halo[...] = jnp.zeros_like(halo)

    u = u_ref[...].astype(f32)
    scale = lax.rsqrt(jnp.mean(u * u, axis=1, keepdims=True) + epsilon)
    normed = (u * scale * gn_ref[0:1, :]).astype(bf16)
    n_ref[...] = normed
    project = dot(normed, w_ref[...], 1, 0)
    z = project[:, :OWN]
    xbc = project[:, OWN : OWN + 640]
    back = 128 - 6 * lax.axis_index("shard")
    raw = pltpu.roll(project[:, 1024:1152], back, 1)
    z_ref[...] = z
    xbc_ref[...] = xbc
    raw_ref[...] = raw
    extended = jnp.concatenate([halo[...], xbc], axis=0)
    halo[...] = xbc[TB - 8 :, :]
    conv = cv_ref[KCONV : KCONV + 1, :] + sum(
        cv_ref[k : k + 1, :] * extended[5 + k : 5 + k + TB, :] for k in range(KCONV)
    )
    cvo_ref[...] = conv
    act = conv * jax.nn.sigmoid(conv)
    dt = softplus(raw + hd_ref[0:1, :])
    log_decay = -jnp.exp(hd_ref[1:2, :]) * dt
    gate = z * jax.nn.sigmoid(z)
    dm = dot(ct_ref[...], wo_ref[...], 1, 1)
    dm_ref[...] = dm
    for j in range(TB // BLOCK):
        at = slice(j * BLOCK, (j + 1) * BLOCK)
        x, keys, query = act[at, :OWN], act[at, OWN : OWN + NS], act[at, OWN + NS :]
        cumulative, turned, wide = decay_parts(log_decay[at])
        contact = mm(query, keys, 1, 1)
        scaled = x * widen(dt[at])
        within = []
        for p in range(3):
            pair = split_pair(scaled[:, 128 * p : 128 * p + 128])
            both = jnp.concatenate(
                [
                    (head_mixing(cumulative, turned, 2 * p + q) * contact)
                    for q in range(2)
                ],
                axis=1,
            )
            within.append(dot(both, pair, 1, 0, highest))
        last = wide[BLOCK - 1 : BLOCK, :]
        before = state[...]
        st_ref[j] = before
        core = jnp.concatenate(within, axis=1) + mm(query, before) * jnp.exp(wide)
        state[...] = jnp.exp(last) * before + mm(keys, scaled * jnp.exp(last - wide), 0, 0)
        core_ref[at, :] = core
        gated = (core + sk_ref[0:1, :] * x) * gate[at]
        ones = jnp.ones((8, OWN), f32)
        first = dot(ones, gated * gated, 1, 1, highest)
        second = dot(ones, gated * (gg_ref[0:1, :] * dm[at]), 1, 1, highest)
        b = (TB // BLOCK) * i + j
        sums_ref[pl.ds(b, 1), :] = first[0:1]
        sums_ref[pl.ds(b + 8, 1), :] = second[0:1]


def backward_kernel(
    z_ref, xbc_ref, cvo_ref, raw_ref, core_ref, dm_ref, st_ref, sums_ref,
    gg_ref, cv_ref, hd_ref, sk_ref,
    dp_ref, mixed_ref, dgain_ref, dskip_ref, dconv_ref, dhead_ref,
    adjoint, halo,
):
    i = pl.program_id(0)

    @pl.when(i == 0)
    def _():
        adjoint[...] = jnp.zeros_like(adjoint)
        halo[...] = jnp.zeros_like(halo)
        dgain_ref[...] = jnp.zeros_like(dgain_ref)
        dskip_ref[...] = jnp.zeros_like(dskip_ref)
        dconv_ref[...] = jnp.zeros_like(dconv_ref)
        dhead_ref[...] = jnp.zeros_like(dhead_ref)

    b = BLOCKS - 1 - i
    totals = sums_ref[0]
    for j in range(1, 8):
        totals += sums_ref[j]
    column = jnp.concatenate([totals, jnp.zeros((112, 128), f32)], axis=0).T
    lane = lanes((BLOCK, 128))
    first = jnp.sum(jnp.where(lane == b, column, 0.0), axis=1, keepdims=True)
    second = jnp.sum(jnp.where(lane == b + 8, column, 0.0), axis=1, keepdims=True)
    z, conv, raw, core, dm = z_ref[...], cvo_ref[...], raw_ref[...], core_ref[...], dm_ref[...]
    sig = jax.nn.sigmoid(conv)
    act = conv * sig
    x, keys, query = act[:, :OWN], act[:, OWN : OWN + NS], act[:, OWN + NS :]
    shifted = raw + hd_ref[0:1, :]
    dt = softplus(shifted)
    rate = jnp.exp(hd_ref[1:2, :])
    log_decay = -rate * dt
    sig_z = jax.nn.sigmoid(z)
    gate = z * sig_z
    skip = sk_ref[0:1, :]
    with_skip = core + skip * x
    gated = with_skip * gate
    scale = lax.rsqrt(first * (1.0 / DI) + epsilon)
    gain = gg_ref[0:1, :]
    unit = gated * scale
    mixed_ref[...] = (unit * gain).astype(bf16)
    dgain_ref[0:1, :] += jnp.sum(dm * unit, axis=0, keepdims=True)
    dgated = scale * (gain * dm) - unit * (scale * scale * (second * (1.0 / DI)))
    dz = dgated * with_skip * (sig_z * (1.0 + z * (1.0 - sig_z)))
    dcore = dgated * gate
    dskip_ref[0:1, :] += jnp.sum(dcore * x, axis=0, keepdims=True)

    cumulative, turned, wide = decay_parts(log_decay)
    contact = mm(query, keys, 1, 1)
    dt_wide = widen(dt)
    scaled = x * dt_wide
    scaled_low = scaled
    dcore_low = dcore
    dcontact = jnp.zeros((BLOCK, BLOCK), f32)
    dscaled = []
    for p in range(3):
        at = slice(128 * p, 128 * p + 128)
        mixing = [head_mixing(cumulative, turned, 2 * p + q) for q in range(2)]
        both = jnp.concatenate([(m * contact) for m in mixing], axis=0)
        pair = split_pair(dcore_low[:, at])
        dscaled.append(dot(both, pair, 0, 0, highest))
        dmix = dot(pair, scaled_low[:, at], 1, 1, highest)
        dcontact += dmix[:BLOCK] * mixing[0] + dmix[BLOCK:] * mixing[1]
    last = wide[BLOCK - 1 : BLOCK, :]
    before = st_ref[0]
    after_adj = adjoint[...]
    grown = jnp.exp(wide)
    left = jnp.exp(last - wide)
    from_core = dcore * grown
    dquery = mm(from_core, before, 1, 1) + mm(dcontact, keys)
    carried = mm(keys, after_adj) * left
    dscaled = jnp.concatenate(dscaled, axis=1) + carried
    dkeys = mm(scaled * left, after_adj, 1, 1) + mm(dcontact, query, 0, 0)
    end = jnp.exp(last)
    adjoint[...] = end * after_adj + mm(query, from_core, 0, 0)
    heads = head_ones()
    last_add = dot(
        jnp.sum(carried * scaled, axis=0, keepdims=True)
        + end * jnp.sum(after_adj * before, axis=0, keepdims=True),
        heads, 1, 0, highest,
    )
    dcum = dot(
        dcore_low.astype(f32) * core - dscaled * scaled_low.astype(f32), heads, 1, 0, highest
    )
    dlog = dot(lower_ones(), dcum, 0, 0, highest) + last_add
    ddt = dot(dscaled * x, heads, 1, 0, highest) - rate * dlog
    draw = ddt * jax.nn.sigmoid(shifted)
    dhead_ref[0:1, :] += jnp.sum(draw, axis=0, keepdims=True)
    dhead_ref[1:2, :] += jnp.sum(dlog * log_decay, axis=0, keepdims=True)
    dx = dscaled * dt_wide + skip * dcore
    dact = jnp.concatenate([dx, dkeys, dquery], axis=1)
    dconv = dact * (sig * (1.0 + conv * (1.0 - sig)))
    extended = jnp.concatenate([dconv, halo[...]], axis=0)
    halo[...] = dconv[:8, :]
    xbc = xbc_ref[...]
    dxbc = jnp.zeros_like(xbc)
    for k in range(KCONV):
        moved = extended[3 - k : 3 - k + BLOCK, :]
        dxbc += cv_ref[k : k + 1, :] * moved
        dconv_ref[k : k + 1, :] += jnp.sum(xbc * moved, axis=0, keepdims=True)
    dconv_ref[KCONV : KCONV + 1, :] += jnp.sum(dconv, axis=0, keepdims=True)
    own_head = lane < 6
    draw_low = jnp.where(own_head, draw, 0.0)
    dp_ref[:, :OWN] = dz.astype(bf16)
    dp_ref[:, OWN : OWN + 640] = dxbc.astype(bf16)
    dp_ref[:, 1024:] = pltpu.roll(draw_low, 6 * lax.axis_index("shard"), 1).astype(bf16)


def sds(shape, dtype=f32):
    return jax.ShapeDtypeStruct(shape, dtype)


def fixed(shape):
    return pl.BlockSpec(shape, lambda i: (0,) * len(shape))


def run_forward(u, ct, w, wo, gn, gg, cv, hd, sk):
    def tokens(columns):
        return pl.BlockSpec((TB, columns), lambda i: (i, 0))

    per = TB // BLOCK
    return pl.pallas_call(
        forward_kernel,
        grid=(LEN // TB,),
        in_specs=[
            tokens(D), tokens(D), fixed((D, COLS)), fixed((OWN, D)),
            fixed((1, D)), fixed((1, OWN)), fixed((8, 640)), fixed((8, 128)), fixed((1, OWN)),
        ],
        out_specs=(
            tokens(D), tokens(OWN), tokens(640), tokens(640), tokens(128), tokens(OWN), tokens(OWN),
            pl.BlockSpec((per, NS, OWN), lambda i: (i, 0, 0)), fixed((16, 128)),
        ),
        out_shape=(
            sds((LEN, D), bf16), sds((LEN, OWN)), sds((LEN, 640)), sds((LEN, 640)),
            sds((LEN, 128)), sds((LEN, OWN)), sds((LEN, OWN)), sds((BLOCKS, NS, OWN)),
            sds((16, 128)),
        ),
        scratch_shapes=[pltpu.VMEM((NS, OWN), f32), pltpu.VMEM((8, 640), f32)],
        compiler_params=pltpu.CompilerParams(vmem_limit_bytes=VMEM_LIMIT),
    )(u, ct, w, wo, gn, gg, cv, hd, sk)


def run_backward(z, xbc, cvo, raw, core, dm, st, sums, gg, cv, hd, sk):
    def tokens(columns):
        return pl.BlockSpec((BLOCK, columns), lambda i: (BLOCKS - 1 - i, 0))

    return pl.pallas_call(
        backward_kernel,
        grid=(BLOCKS,),
        in_specs=[
            tokens(OWN), tokens(640), tokens(640), tokens(128), tokens(OWN), tokens(OWN),
            pl.BlockSpec((1, NS, OWN), lambda i: (BLOCKS - 1 - i, 0, 0)),
            fixed((8, 16, 128)), fixed((1, OWN)), fixed((8, 640)), fixed((8, 128)), fixed((1, OWN)),
        ],
        out_specs=(
            tokens(COLS), tokens(OWN), fixed((8, OWN)), fixed((8, OWN)), fixed((8, 640)),
            fixed((8, 128)),
        ),
        out_shape=(
            sds((LEN, COLS), bf16), sds((LEN, OWN), bf16), sds((8, OWN)), sds((8, OWN)),
            sds((8, 640)), sds((8, 128)),
        ),
        scratch_shapes=[pltpu.VMEM((NS, OWN), f32), pltpu.VMEM((8, 640), f32)],
        compiler_params=pltpu.CompilerParams(vmem_limit_bytes=VMEM_LIMIT),
    )(z, xbc, cvo, raw, core, dm, st, sums, gg, cv, hd, sk)


def adam_update(master, first, second, gradient, rate, decay):
    first_new = beta_one * first + (1.0 - beta_one) * gradient
    second_new = beta_two * second + (1.0 - beta_two) * gradient * gradient
    scaled = (
        first_new
        / (1.0 - beta_one**STEP)
        / (jnp.sqrt(second_new / (1.0 - beta_two**STEP)) + adam_epsilon)
    )
    return (first_new, second_new, master - rate * (scaled + decay * master))


def on_device(
    hidden, cotangent, in_master, in_first, in_second, out_master, out_first, out_second,
    gain_master, gain_first, gain_second, conv_master, conv_first, conv_second,
    head_master, head_first, head_second,
):
    s = lax.axis_index("shard")
    c = lax.rem(lax.axis_index("dp"), 2)
    low = lambda v: lax.reduce_precision(v, 8, 7)
    wide = jnp.pad(in_master.astype(bf16), ((0, 0), (0, WIDE - PROJ)))
    wo = out_master.astype(bf16)
    small = jnp.concatenate(
        [low(gain_master), low(conv_master).reshape(-1), jnp.zeros((416,), f32)]
    ).reshape(24, 128)
    u, ct, w, sm = exchange(
        1, gather_body, (hidden[0], cotangent[0], wide, small),
        (
            sds((8, BLOCK, D), bf16), sds((8, BLOCK, D), bf16), sds((8, 192, COLS), bf16),
            sds((8, 24, 128)),
        ),
        42, 6,
    )
    u, ct, w = u.reshape(LEN, D), ct.reshape(LEN, D), w.reshape(D, COLS)
    sm = sm.reshape(8, 3072)
    gains = sm[:, :576].reshape(4608)
    conv_all = sm[:, 576:2656].reshape(8, 5, 416).transpose(1, 0, 2).reshape(5, CONVC)
    gn = gains[None, :D]
    gg = lax.dynamic_slice(gains, (D + OWN * s,), (OWN,))[None]
    cv = jnp.concatenate(
        [lax.dynamic_slice(conv_all, (0, OWN * s), (5, OWN)), conv_all[:, DI:]], axis=1
    )
    cv = jnp.pad(cv, ((0, 3), (0, 0)))
    heads = low(head_master)
    hd = jnp.pad(heads, ((0, 5), (0, 122)))
    sk = jnp.repeat(heads[2], HD)[None]

    normed, z, xbc, cvo, raw, core, dm, st, sums = run_forward(u, ct, w, wo, gn, gg, cv, hd, sk)
    (sums,) = exchange(2, all_body, (sums,), (sds((8, 16, 128)),), 7, 1)
    dproj, mixed, dgain, dskip, dconv, dhead = run_backward(
        z, xbc, cvo, raw, core, dm, st, sums, gg, cv, hd, sk
    )
    dgain, dskip, dconv, dhead = dgain[0], dskip[0], dconv[:5], dhead[:2, :6]
    part_out = dot(mixed, wo, 1, 0).astype(bf16).reshape(8, BLOCK, D)
    grad_o = dot(mixed, ct, 0, 0)
    grad_w = dot(normed, dproj, 0, 0)
    part_in = dot(dproj, w, 1, 1).astype(bf16).reshape(8, BLOCK, D)
    got_out, got_in = exchange(
        3, scatter_body, (part_out, part_in),
        (sds((8, BLOCK, D), bf16), sds((8, BLOCK, D), bf16)), 14, 2,
    )
    inputs = hidden[0].astype(f32)
    layer_out = (inputs + jnp.sum(got_out.astype(f32), axis=0)).astype(bf16)
    d_normed = jnp.sum(got_in.astype(f32), axis=0)
    scale = lax.rsqrt(jnp.mean(inputs * inputs, axis=-1, keepdims=True) + epsilon)
    gained = gn * d_normed
    grad_inputs = scale * gained - inputs * scale**3 * jnp.mean(
        inputs * gained, axis=-1, keepdims=True
    )
    input_grad = (cotangent[0].astype(f32) + grad_inputs).astype(bf16)
    dnorm = jnp.sum(d_normed * inputs * scale, axis=0)
    small_grad = jnp.concatenate(
        [
            dnorm, dgain, dconv[:, :OWN].reshape(-1), dconv[:, OWN:].reshape(-1),
            dhead.reshape(-1), jnp.sum(dskip.reshape(6, HD), axis=1), jnp.zeros((1006,), f32),
        ]
    ).reshape(48, 128)

    grad_w = grad_w.reshape(8, 8, 24, COLS)
    grad_o = grad_o.reshape(8, 48, D)
    swap_w, swap_o = exchange(
        4, swap_body, (grad_w, grad_o), (sds((4, 8, 24, COLS), f32), sds((8, 48, 768), f32)), 2, 0
    )
    half_w = (
        lax.dynamic_slice_in_dim(grad_w, 4 * c, 4, 0).astype(f32) + swap_w.astype(f32)
    ).astype(bf16)
    half_o = (
        lax.dynamic_slice_in_dim(grad_o, 768 * c, 768, 2).astype(f32) + swap_o.astype(f32)
    ).astype(bf16)
    got_w, got_o = exchange(
        5, reduce_body, (half_w, half_o),
        (sds((8, 4, 24, COLS), bf16), sds((8, 48, 768), bf16)), 14, 2,
    )
    piece_w = jnp.sum(got_w.astype(f32), axis=0)
    piece_o = jnp.sum(got_o.astype(f32), axis=0)
    own_w, small_all = exchange(
        6, owner_body, (piece_w, small_grad), (sds((8, 24, COLS)), sds((8, 48, 128))), 14, 2
    )
    own_w = own_w.transpose(1, 0, 2)
    slab = jnp.concatenate(
        [
            own_w[:, :, :OWN].reshape(24, DI),
            own_w[:, :, OWN : 2 * OWN].reshape(24, DI),
            jnp.sum(own_w[:, :, 2 * OWN :], axis=1),
        ],
        axis=1,
    )
    flat = small_all.reshape(8, 6144)
    g_gain = jnp.concatenate([jnp.sum(flat[:, :D], axis=0), flat[:, D : D + OWN].reshape(-1)])
    g_conv = jnp.concatenate(
        [
            flat[:, 1920:3840].reshape(8, 5, OWN).transpose(1, 0, 2).reshape(5, DI),
            jnp.sum(flat[:, 3840:5120], axis=0).reshape(5, 256),
        ],
        axis=1,
    )
    own_small = jnp.concatenate(
        [
            lax.dynamic_slice(g_gain, (576 * s,), (576,)),
            lax.dynamic_slice(g_conv, (0, 416 * s), (5, 416)).reshape(-1),
            lax.dynamic_slice(flat, (s, 5120), (1, 18))[0],
            jnp.zeros((398,), f32),
        ]
    ).reshape(24, 128)
    total_w, total_o, total_small = exchange(
        7, spread_body, (slab, piece_o, own_small),
        (sds((8, 24, WIDE)), sds((8, 48, D)), sds((16, 24, 128))), 45, 3,
    )
    total_small = jnp.sum(total_small, axis=0).reshape(-1)
    totals = (
        total_w.reshape(192, WIDE)[:, :PROJ].astype(f32),
        total_o.reshape(OWN, D).astype(f32),
        total_small[:576],
        total_small[576:2656].reshape(5, 416),
        total_small[2656:2674].reshape(3, 6),
    )
    masters = (in_master, out_master, gain_master, conv_master, head_master)
    firsts = (in_first, out_first, gain_first, conv_first, head_first)
    seconds = (in_second, out_second, gain_second, conv_second, head_second)
    updated = [
        adam_update(masters[g], firsts[g], seconds[g], totals[g], rates[g], decays[g])
        for g in range(5)
    ]
    return (layer_out[None], input_grad[None]) + tuple(v for group in updated for v in group)


def solution(mesh):
    rows, columns = P("shard", None), P(None, "shard")
    tokens = P("dp", "shard", None)
    state = (rows,) * 6 + (P("shard"),) * 3 + (columns,) * 6
    return jax.shard_map(
        on_device,
        mesh=mesh,
        in_specs=(tokens, tokens) + state,
        out_specs=(tokens, tokens) + state,
        check_vma=False,
    )
```

time: 1460 us -> 477 us (0.33)
  waiting for transfers between devices: 974 us -> 0 us
  Pallas kernels: 0 us -> 365 us
  blocking collectives: 176 us -> 0 us
  matrix products: 118 us -> 27 us
  local copies, waits for them, and re-layouts: 70.5 us -> 28.3 us
  other arithmetic: 86.9 us -> 53.9 us
  between operations: 18.6 us -> 0.96 us
    reduce_scatter x2 -> x0, waiting for transfers between devices: 470 us -> none  [the longest x1 393 us: on_device(): lax.psum_scatter(grad_in_w, 'shard', scatter_dimension=0, tiled=True)]
    all_gather x4 -> x0, waiting for transfers between devices: 410 us -> none  [the longest x2 202 us: prefix(): pieces = jax.tree.map(lambda part: lax.all_gather(part, axis), value)]
    pallas_call x0 -> x9, Pallas kernels: none -> 365 us  [the longest x7 311 us: exchange(): pl.pallas_call(kernel, out_shape=outs, in_specs=[any_spec] * len(ins), ou...]
    dot_general x22 -> x4, matrix products: 118 us -> 27 us  [dot(): lax.dot_general(a, b, (((ca,), (cb,)), ((), ())), precision=precision, pr...]
    psum x1 -> x0, waiting for transfers between devices: 90.7 us -> none  [on_device(): totals = lax.psum((owned[0], owned[1], owned[2], owned[3], owned[4]), 'dp')]
    unnamed x3 -> x0, blocking collectives: 67.6 us -> none
    psum x1 -> x0, blocking collectives: 66 us -> none  [on_device(): totals = lax.psum((owned[0], owned[1], owned[2], owned[3], owned[4]), 'dp')]
    all_gather x2 -> x0, blocking collectives: 42.5 us -> none  [the longest x1 24.5 us: on_device(): lax.all_gather(conv_master.astype(jnp.bfloat16), 'shard', axis=1, tiled=T...]
  transfers between devices with their start and end apart: 10 -> 0, of which waited for: 8 -> 0; matrix products, arithmetic and copies ran while one was open for 14% -> 0% of each run, Pallas kernels for 0% -> 0%
where the time goes in v1:
time: 477 us; the launch traced here: 475 us
  Pallas kernels  365 us (77%)
  other arithmetic  53.9 us (11%)
  local copies, waits for them, and re-layouts  28.3 us (6%)
  matrix products  27 us (6%)
    pallas_call x7, Pallas kernels, exchange(): pl.pallas_call(kernel, out_shape=outs, in_specs=[any_spec] * len(ins), ou...  311 us
    pallas_call x1, Pallas kernels, run_backward(): pl.pallas_call(backward_kernel, grid=(BLOCKS,), in_specs=[tokens(OWN), to...  30.6 us
    dot_general x4, matrix products, dot(): lax.dot_general(a, b, (((ca,), (cb,)), ((), ())), precision=precision, pr...  27 us
    pallas_call x1, Pallas kernels, run_forward(): pl.pallas_call(forward_kernel, grid=(LEN // TB,), in_specs=[tokens(D), to...  23.8 us
    sub x5, other arithmetic, adam_update(): return (first_new, second_new, master - rate * (scaled + decay * master))  22.2 us

profile of v1, /device:TPU:1, one launch (start us, length us, event | category | flops | bytes accessed | tf_op | source)
XLA Modules:
  0.0 475.3 jit_solution(1463272218449658682)
XLA Ops:
  0.7 2.7 convert_element_type.56
  3.4 1.6 pad.12.refs_2_
  5.8 114.7 %shard_map.296 = (bf16[8,128,1536]{2,1,0:T(8,128)(2,1)}, bf16[8,128,1536]{2,1,0:T(8,128)(2,1)}, bf16[8,192,1152]{2,1,0:T(8,128)(2,1)}, f32[8,24,128]{2,1,0:T(8,128)}) custom-call(bf16[128,1536]{1,0:T(8,128)(2,1)} %bitcast.70, bf16[128,1536]{1,0:T(8,128)(2,1)} %bitcast.79, bf16[192,6528]{1,0:T(8,128)(2,1)} %pad.12.refs_2_, f32[24,128]{1,0:T(8,128)} %bitcast.101), custom_call_target="tpu_custom_call" | custom-call | tf_op jit(solution)/shard_map/pallas_call | solution.py:101
  120.5 0.9 copy.49
  125.1 1.2 convert_element_type.57.wo_ref
  126.3 23.8 %shard_map.297 = (bf16[1024,1536]{1,0:T(8,128)(2,1)}, f32[1024,384]{1,0:T(8,128)}, f32[1024,640]{1,0:T(8,128)}, f32[1024,640]{1,0:T(8,128)}, f32[1024,128]{1,0:T...) custom-call(bf16[1024,1536]{1,0:T(8,128)(2,1)} %bitcast.78, ...), custom_call_target="tpu_custom_call" | custom-call | tf_op jit(solution)/shard_map/pallas_call | solution.py:603
  150.1 6.1 %shard_map.298.sums_ref = f32[8,16,128]{2,1,0:T(8,128)} custom-call(f32[16,128]{1,0:T(8,128)} %get-tuple-element.58.refs_0_), custom_call_target="tpu_custom_call" | custom-call | tf_op jit(solution)/shard_map/pallas_call | solution.py:101
  156.2 30.6 %shard_map.299 = (bf16[1024,1152]{1,0:T(8,128)(2,1)}, bf16[1024,384]{1,0:T(8,128)(2,1)}, f32[8,384]{1,0:T(8,128)}, f32[8,384]{1,0:T(8,128)}, f32[8,640]{1,0:T(8,128)}, /*index=5*/f32[8,128]{1,0:T(8,128)}) custom-call(f32[1024,384]{1,0:T(8,128)} %get-tuple-element.51.z_ref, f32[1024,640]{1,0:T(8,128)} %get-tuple-element.52.xbc_ref, ...), custom_call_target="tpu_custom_call" | custom-call | tf_op jit(solution)/shard_map/pallas_call | solution.py:628
  186.8 1.3 slice_reduce_fusion.3
  188.8 8.8 %convolution_convert_fusion.1 = bf16[1024,1536]{1,0:T(8,128)(2,1)} fusion(bf16[1024,1152]{1,0:T(8,128)(2,1)} %get-tuple-element.60, bf16[1536,1152]{1,0:T(8,128)(2,1)} %bitcast.73), kind=kOutput, calls=%fused_computation.7 | convolution fusion | flops 3625451520 | bytes 9043968 | tf_op jit(solution)/shard_map/dot_general | solution.py:356
  197.6 3.5 convolution_convert_fusion
  201.1 72.1 %shard_map.300 = (bf16[8,128,1536]{2,1,0:T(8,128)(2,1)}, bf16[8,128,1536]{2,1,0:T(8,128)(2,1)}) custom-call(bf16[8,128,1536]{2,1,0:T(8,128)(2,1)} %bitcast.75, bf16[8,128,1536]{2,1,0:T(8,128)(2,1)} %bitcast.74), custom_call_target="tpu_custom_call" | custom-call | tf_op jit(solution)/shard_map/pallas_call | solution.py:101
  273.2 4.7 convert_reduce_fusion
  279.2 0.8 fusion.11
  280.5 1.3 reshape.222
  281.9 1.3 slice.73
  283.1 1.3 reshape.223
  284.4 1.2 slice.74
  285.7 1.3 reshape.224
  287.6 1.4 concatenate.23
  289.0 9.8 %fusion.24 = f32[1536,1152]{1,0:T(8,128)} fusion(bf16[1024,1536]{1,0:T(8,128)(2,1)} %get-tuple-element.63, bf16[1024,1152]{1,0:T(8,128)(2,1)} %get-tuple-element.60), kind=kOutput, calls=%fused_computation.69 | convolution fusion | flops 3623878656 | bytes 12582912 | tf_op jit(solution)/shard_map/dot_general | solution.py:356
  298.8 2.3 copy.38
  301.1 4.9 %fusion.25.refs_1_ = f32[8,48,1536]{2,1,0:T(8,128)} fusion(bf16[8,48,1024]{2,1,0:T(8,128)(2,1)} %bitcast.84, bf16[1024,1536,1]{1,0,2:T(8,128)(2,1)} %bitcast.77), kind=kOutput, calls=%fused_computation.70 | convolution fusion | flops 1207959552 | bytes 6291456 | tf_op jit(solution)/shard_map/dot_general | solution.py:356
  306.1 8.5 %shard_map.301 = (f32[4,8,24,1152]{3,2,1,0:T(8,128)}, f32[8,48,768]{2,1,0:T(8,128)}) custom-call(f32[8,8,24,1152]{3,2,1,0:T(8,128)} %bitcast.68, f32[8,48,1536]{2,1,0:T(8,128)} %fusion.25.refs_1_), custom_call_target="tpu_custom_call" | custom-call | tf_op jit(solution)/shard_map/pallas_call | solution.py:101
  314.6 2.6 add_convert_fusion.1.refs_1_
  317.1 4.6 add_convert_fusion.refs_0_
  321.8 37.0 %shard_map.302 = (bf16[8,4,24,1152]{3,2,1,0:T(8,128)(2,1)}, bf16[8,48,768]{2,1,0:T(8,128)(2,1)}) custom-call(bf16[4,8,24,1152]{3,2,1,0:T(8,128)(2,1)} %add_convert_fusion.refs_0_, bf16[8,48,768]{2,1,0:T(8,128)(2,1)} %add_convert_fusion.1.refs_1_), custom_call_target="tpu_custom_call" | custom-call | tf_op jit(solution)/shard_map/pallas_call | solution.py:101
  358.7 2.5 convert_reduce_fusion.2.refs_0_
  361.2 9.8 %shard_map.303 = (f32[8,24,1152]{2,1,0:T(8,128)}, f32[8,48,128]{2,1,0:T(8,128)}) custom-call(f32[4,24,1152]{2,1,0:T(8,128)} %convert_reduce_fusion.2.refs_0_, f32[48,128]{1,0:T(8,128)} %bitcast.96), custom_call_target="tpu_custom_call" | custom-call | tf_op jit(solution)/shard_map/pallas_call | solution.py:101
  371.0 1.0 copy.48
  373.4 1.4 fusion.14
  374.8 1.4 reshape.233
  376.2 1.3 slice.95
  377.5 1.3 reshape.229
  378.8 0.8 slice_reduce_fusion.1
  379.6 1.4 fusion.16
  381.7 1.4 concatenate.27
  383.1 1.3 slice_bitcast_fusion.1
  384.4 0.9 pad_maximum_fusion.refs_0_
  385.3 0.7 convert_reduce_fusion.3.refs_1_
  386.0 62.6 %shard_map.304 = (f32[8,24,6528]{2,1,0:T(8,128)}, f32[8,48,1536]{2,1,0:T(8,128)}, f32[16,24,128]{2,1,0:T(8,128)}) custom-call(f32[24,6528]{1,0:T(8,128)} %pad_maximum_fusion.refs_0_, f32[48,768]{1,0:T(8,128)} %convert_reduce_fusion.3.refs_1_, f32[24,128]{1,0:T(8,128)} %bitcast.102), custom_call_target="tpu_custom_call" | custom-call | tf_op jit(solution)/shard_map/pallas_call | solution.py:101
  448.6 13.9 %multiply_subtract_fusion = (f32[192,6448]{1,0:T(8,128)}, f32[192,6448]{1,0:T(8,128)}, f32[192,6448]{1,0:T(8,128)}) fusion(f32[192,6448]{1,0:T(8,128)} %param.19, f32[192,6528]{1,0:T(8,128)} %bitcast.71, f32[192,6448]{1,0:T(8,128)} %param.21, f32[192,6448]{1,0:T(8,128)} %param.20), kind=kLoop, calls=%fused_computation.4 | loop fusion | flops 18570240 | bytes 34664448 | tf_op jit(solution)/shard_map/sub | solution.py:657
  462.6 4.2 multiply_subtract_fusion.1
  466.9 0.9 reduce_sum.125
  468.0 1.4 multiply_subtract_fusion.2
  469.3 1.3 multiply_subtract_fusion.3
  470.8 1.3 multiply_subtract_fusion.4
  472.8 2.5 fusion.7
  (74 shorter events, 10.5 us)
Async XLA Ops:
  3.3 1.7 copy-start.9
  3.4 1.7 copy-start.11
  5.0 118.7 %copy-start.13 = (f32[3,6]{1,0:T(4,128)S(1)}, f32[3,6]{1,0:T(4,128)}, u32[]{:S(2)}) copy-start(f32[3,6]{1,0:T(4,128)} %param.31) | copy-start | bytes 220
  5.0 120.1 %copy-start = (f32[384,1536]{1,0:T(8,128)S(1)}, f32[384,1536]{1,0:T(8,128)}, u32[]{:S(2)}) copy-start(f32[384,1536]{1,0:T(8,128)} %param.22) | copy-start | bytes 7077892
  188.8 8.8 %copy-start.2 = (bf16[384,1536]{1,0:T(8,128)(2,1)S(1)}, bf16[384,1536]{1,0:T(8,128)(2,1)}, u32[]{:S(2)}) copy-start(bf16[384,1536]{1,0:T(8,128)(2,1)} %convert_element_type.57.wo_ref) | copy-start | bytes 3538948
  188.8 8.8 %copy-start.6 = (bf16[1024,384]{1,0:T(8,128)(2,1)S(1)}, bf16[1024,384]{1,0:T(8,128)(2,1)}, u32[]{:S(2)}) copy-start(bf16[1024,384]{1,0:T(8,128)(2,1)} %get-tuple-element.59) | copy-start | bytes 2359300
  273.2 4.8 %copy-start.1 = (bf16[1,128,1536]{2,1,0:T(8,128)(2,1)S(1)}, bf16[1,128,1536]{2,1,0:T(8,128)(2,1)}, u32[]{:S(2)}) copy-start(bf16[1,128,1536]{2,1,0:T(8,128)(2,1)} %param.17) | copy-start | bytes 1179652
  273.2 6.7 %copy-start.10 = (f32[8,640]{1,0:T(8,128)S(1)}, f32[8,640]{1,0:T(8,128)}, u32[]{:S(2)}) copy-start(f32[8,640]{1,0:T(8,128)} %get-tuple-element.68) | copy-start | bytes 61444
  278.7 0.5 copy-start.15
  372.0 0.7 copy-start.7
  383.1 2.2 copy-start.8
  448.6 14.0 %copy-start.3 = (f32[384,1536]{1,0:T(8,128)S(1)}, f32[384,1536]{1,0:T(8,128)}, u32[]{:S(2)}) copy-start(f32[384,1536]{1,0:T(8,128)} %param.24) | copy-start | bytes 7077892
  448.6 14.0 %copy-start.4 = (f32[384,1536]{1,0:T(8,128)S(1)}, f32[384,1536]{1,0:T(8,128)}, u32[]{:S(2)}) copy-start(f32[384,1536]{1,0:T(8,128)} %param.23) | copy-start | bytes 7077892
  448.6 14.0 %copy-start.5 = (f32[8,48,1536]{2,1,0:T(8,128)S(1)}, f32[8,48,1536]{2,1,0:T(8,128)}, u32[]{:S(2)}) copy-start(f32[8,48,1536]{2,1,0:T(8,128)} %get-tuple-element.75) | copy-start | bytes 7077892
  462.6 6.8 %copy-start.12 = (f32[576]{0:T(1024)S(1)}, f32[576]{0:T(1024)}, u32[]{:S(2)}) copy-start(f32[576]{0:T(1024)} %param.25) | copy-start | bytes 6916
  462.6 8.2 %copy-start.14 = (f32[3,6]{1,0:T(4,128)S(1)}, f32[3,6]{1,0:T(4,128)}, u32[]{:S(2)}) copy-start(f32[3,6]{1,0:T(4,128)} %param.31) | copy-start | bytes 220

commit v2 on v1

v2 whole, which is shorter than its diff:
```python
import functools

import jax
import jax.numpy as jnp
from jax import lax
from jax.experimental import pallas as pl
from jax.experimental.pallas import tpu as pltpu
from jax.sharding import PartitionSpec as P

D = 1536
DI = 3072
H = 48
HD = 64
NS = 128
KCONV = 4
STEP = 5
BLOCK = 128
CONVC = 3328
PROJ = 6448
LEN = 1024
OWN = 384
COLS = 1152
WIDE = 6528
BLOCKS = LEN // BLOCK

f32 = jnp.float32
bf16 = jnp.bfloat16
highest = lax.Precision.HIGHEST
MESH = pl.DeviceIdType.MESH
epsilon = 1e-05
beta_one = 0.9
beta_two = 0.95
adam_epsilon = 1e-08
rates = (0.05, 0.04, 0.25, 0.5, 0.5)
decays = (0.1, 0.1, 0.0, 0.0, 0.0)
VMEM_LIMIT = 60 * 2**20


class Place:
    def __init__(self):
        self.d = lax.axis_index("dp")
        self.s = lax.axis_index("shard")
        self.c = lax.rem(self.d, 2)
        self.x = lax.rem(self.d // 2, 4)
        self.yh = self.d // 8
        self.big = self.d // 2
        self.z = lax.rem(self.s, 4)
        self.yl = self.s // 4

    def shard_of(self, k):
        return lax.rem(self.yl + k // 4, 2) * 4 + lax.rem(self.z + k % 4, 4)

    def shard_peer(self, k):
        return (self.d, self.shard_of(k))

    def big_of(self, k):
        return lax.rem(self.yh + k // 4, 2) * 4 + lax.rem(self.x + k % 4, 4)

    def big_peer(self, k):
        return (self.big_of(k) * 2 + self.c, self.s)

    def core_peer(self):
        return (self.big * 2 + 1 - self.c, self.s)

    def other_core_of(self, k):
        return (self.big_of(k) * 2 + 1 - self.c, self.s)


ORDER = (6, 2, 5, 7, 1, 3, 4)


def exchange(cid, body, ins, outs, sems, locals_):
    def kernel(*refs):
        in_refs = refs[: len(ins)]
        out_refs = refs[len(ins) : len(ins) + len(outs)]
        send, recv, own = refs[len(ins) + len(outs) :]
        place = Place()

        def meet(peers):
            barrier = pltpu.get_barrier_semaphore()
            for peer in peers:
                pl.semaphore_signal(barrier, inc=1, device_id=peer, device_id_type=MESH)
            pl.semaphore_wait(barrier, len(peers))

        def remote(src, dst, index, peer):
            return pltpu.make_async_remote_copy(
                src_ref=src,
                dst_ref=dst,
                send_sem=send.at[index],
                recv_sem=recv.at[index],
                device_id=peer,
                device_id_type=MESH,
            )

        def local(src, dst, index):
            return pltpu.make_async_copy(src, dst, own.at[index])

        body(place, meet, remote, local, in_refs, out_refs)

    any_spec = pl.BlockSpec(memory_space=pl.ANY)
    return pl.pallas_call(
        kernel,
        out_shape=outs,
        in_specs=[any_spec] * len(ins),
        out_specs=tuple([any_spec] * len(outs)),
        scratch_shapes=[
            pltpu.SemaphoreType.DMA((sems,)),
            pltpu.SemaphoreType.DMA((sems,)),
            pltpu.SemaphoreType.DMA((max(locals_, 1),)),
        ],
        compiler_params=pltpu.CompilerParams(collective_id=cid, has_side_effects=True),
    )(*ins)


def scatter_body(place, meet, remote, local, ins, outs):
    meet([place.shard_peer(k) for k in ORDER])
    copies = []
    for a in range(len(ins)):
        copies.append(local(ins[a].at[place.s], outs[a].at[place.s], a))
    for n, k in enumerate(ORDER):
        for a in range(len(ins)):
            copies.append(
                remote(
                    ins[a].at[place.shard_of(k)],
                    outs[a].at[place.s],
                    n * len(ins) + a,
                    place.shard_peer(k),
                )
            )
    for copy in copies:
        copy.start()
    for copy in copies:
        copy.wait()


def swap_body(place, meet, remote, local, ins, outs):
    gw, go = ins
    gw_out, go_out = outs
    meet([place.core_peer()])
    other = 1 - place.c
    copies = [
        remote(gw.at[pl.ds(other * 4, 4)], gw_out, 0, place.core_peer()),
        remote(
            go.at[:, :, pl.ds(pl.multiple_of(other * 768, 128), 768)],
            go_out,
            1,
            place.core_peer(),
        ),
    ]
    for copy in copies:
        copy.start()
    for copy in copies:
        copy.wait()


def reduce_body(place, meet, remote, local, ins, outs):
    hw, ho = ins
    hw_out, ho_out = outs
    meet([place.big_peer(k) for k in ORDER])
    copies = [
        local(hw.at[:, place.big], hw_out.at[0], 0),
        local(ho.at[place.big], ho_out.at[0], 1),
    ]
    for n, k in enumerate(ORDER):
        them = place.big_of(k)
        copies.append(remote(hw.at[:, them], hw_out.at[k], 2 * n, place.big_peer(k)))
        copies.append(remote(ho.at[them], ho_out.at[k], 2 * n + 1, place.big_peer(k)))
    for copy in copies:
        copy.start()
    for copy in copies:
        copy.wait()


def owner_body(place, meet, remote, local, ins, outs):
    piece, small = ins
    piece_out, small_out = outs
    meet([place.shard_peer(k) for k in ORDER])
    valid = place.yl == place.c
    own_small = local(small, small_out.at[place.s], 0)
    own_small.start()
    own_piece = local(piece.at[place.z], piece_out.at[place.s], 1)

    @pl.when(valid)
    def _():
        own_piece.start()

    smalls = [
        remote(small, small_out.at[place.s], n, place.shard_peer(k))
        for n, k in enumerate(ORDER)
    ]
    for copy in smalls:
        copy.start()
    pieces = []
    for n, k in enumerate(ORDER):
        them = place.shard_of(k)
        copy = remote(
            piece.at[lax.rem(them, 4)], piece_out.at[place.s], 7 + n, place.shard_peer(k)
        )
        goes = them // 4 == place.c
        pl.when(goes)(copy.start)
        pieces.append((copy, goes))
    own_small.wait()
    pl.when(valid)(own_piece.wait)
    for copy in smalls:
        copy.wait()
    for copy, goes in pieces:
        pl.when(goes)(copy.wait_send)
        pl.when(valid)(copy.wait_recv)


def spread_body(place, meet, remote, local, ins, outs):
    slab, go, small = ins
    slab_out, go_out, small_out = outs
    core = place.core_peer()
    everyone = [place.big_peer(k) for k in ORDER] + [core]
    everyone += [place.other_core_of(k) for k in ORDER]
    meet(everyone)
    valid = place.yl == place.c
    at = pl.multiple_of(place.c * 768, 128)

    def half(index):
        return go_out.at[index, :, pl.ds(at, 768)]

    other_at = pl.multiple_of((1 - place.c) * 768, 128)
    own_small = local(small, small_out.at[place.d], 0)
    own_go = local(go, half(place.big), 1)
    own_slab = local(slab, slab_out.at[place.big], 2)
    own_small.start()
    own_go.start()
    smalls = [
        remote(small, small_out.at[place.d], n, peer) for n, peer in enumerate(everyone)
    ]
    slabs = [
        remote(slab, slab_out.at[place.big], 15 + n, place.big_peer(k))
        for n, k in enumerate(ORDER)
    ]
    gos = [
        remote(go, half(place.big), 22 + n, place.big_peer(k)) for n, k in enumerate(ORDER)
    ]
    to_core_slab = remote(slab, slab_out.at[place.big], 29, core)
    to_core_go = remote(go, half(place.big), 30, core)

    @pl.when(valid)
    def _():
        own_slab.start()
        for copy in slabs:
            copy.start()
        to_core_slab.start()

    for copy in gos:
        copy.start()
    to_core_go.start()
    for copy in smalls:
        copy.start()
    forward_gos = []
    forward_slabs = []
    for n, k in enumerate(ORDER):
        origin = lax.rem(place.yh + k // 4, 2) * 4 + lax.rem(place.x + 4 - k % 4, 4)
        gos[n].wait_recv()
        go_copy = remote(half(origin), half(origin), 31 + n, core)
        go_copy.start()
        forward_gos.append(go_copy)
        slab_copy = remote(slab_out.at[origin], slab_out.at[origin], 38 + n, core)

        @pl.when(valid)
        def _(n=n, slab_copy=slab_copy):
            slabs[n].wait_recv()
            slab_copy.start()

        forward_slabs.append(slab_copy)
    own_small.wait()
    own_go.wait()
    for copy in smalls:
        copy.wait()
    for copy in gos:
        copy.wait_send()
    to_core_go.wait()
    for copy in forward_gos:
        copy.wait()

    @pl.when(valid)
    def _():
        own_slab.wait()
        for copy in slabs:
            copy.wait_send()
        to_core_slab.wait_send()
        for copy in forward_slabs:
            copy.wait_send()

    @pl.when(jnp.logical_not(valid))
    def _():
        to_core_slab.wait_recv()
        for copy in forward_slabs:
            copy.wait_recv()


def dot(a, b, ca, cb, precision=None):
    return lax.dot_general(
        a, b, (((ca,), (cb,)), ((), ())), precision=precision, preferred_element_type=f32
    )


def mm(a, b, ca=1, cb=0):
    return dot(a.astype(f32), b.astype(f32), ca, cb, highest)


def lanes(shape):
    return lax.broadcasted_iota(jnp.int32, shape, 1)


def rows_of(shape):
    return lax.broadcasted_iota(jnp.int32, shape, 0)


def widen(m):
    low = lanes((m.shape[0], 128)) < HD
    return jnp.concatenate(
        [jnp.where(low, m[:, 2 * i : 2 * i + 1], m[:, 2 * i + 1 : 2 * i + 2]) for i in range(3)],
        axis=1,
    )


def lower_ones():
    return (rows_of((BLOCK, BLOCK)) >= lanes((BLOCK, BLOCK))).astype(f32)


def head_ones():
    return (rows_of((OWN, BLOCK)) // HD == lanes((OWN, BLOCK))).astype(f32)


def split_pair(pair):
    low = lanes(pair.shape) < HD
    zero = jnp.zeros_like(pair)
    return jnp.concatenate([jnp.where(low, pair, zero), jnp.where(low, zero, pair)], axis=0)


def head_mixing(cumulative, turned, h):
    causal = rows_of((BLOCK, BLOCK)) >= lanes((BLOCK, BLOCK))
    differ = cumulative[:, h : h + 1] - turned[h : h + 1, :]
    return jnp.exp(jnp.where(causal, differ, -jnp.inf))


def softplus(v):
    return jnp.maximum(v, 0.0) + jnp.log1p(jnp.exp(-jnp.abs(v)))


TB = 256
HALF = DI // 8


def dot3(a, b, ca, cb):
    a_hi, b_hi = a.astype(bf16), b.astype(bf16)
    a_lo, b_lo = (a - a_hi.astype(f32)).astype(bf16), (b - b_hi.astype(f32)).astype(bf16)
    left = jnp.concatenate([a_hi, a_hi, a_lo], axis=ca)
    right = jnp.concatenate([b_hi, b_lo, b_hi], axis=cb)
    return dot(left, right, ca, cb)


def dot_exact(a, ones, ca, cb):
    a_hi = a.astype(bf16)
    a_lo = (a - a_hi.astype(f32)).astype(bf16)
    low = ones.astype(bf16)
    return dot(
        jnp.concatenate([a_hi, a_lo], axis=ca), jnp.concatenate([low, low], axis=cb), ca, cb
    )


def ones_dot(ones, a, ca, cb):
    a_hi = a.astype(bf16)
    a_lo = (a - a_hi.astype(f32)).astype(bf16)
    low = ones.astype(bf16)
    return dot(
        jnp.concatenate([low, low], axis=ca), jnp.concatenate([a_hi, a_lo], axis=cb), ca, cb
    )


def decay_parts(log_decay):
    cumulative = ones_dot(lower_ones(), log_decay, 1, 0)
    return cumulative, cumulative.T, widen(cumulative)


def forward_block(act, dt, log_decay, before):
    x, keys, query = act[:, :OWN], act[:, OWN : OWN + NS], act[:, OWN + NS :]
    cumulative, turned, wide = decay_parts(log_decay)
    contact = dot3(query, keys, 1, 1)
    scaled = x * widen(dt)
    within = []
    for p in range(3):
        pair = split_pair(scaled[:, 128 * p : 128 * p + 128])
        both = jnp.concatenate(
            [head_mixing(cumulative, turned, 2 * p + q) * contact for q in range(2)], axis=1
        )
        within.append(dot3(both, pair, 1, 0))
    last = wide[BLOCK - 1 : BLOCK, :]
    core = jnp.concatenate(within, axis=1) + dot3(query, before, 1, 0) * jnp.exp(wide)
    after = jnp.exp(last) * before + dot3(keys, scaled * jnp.exp(last - wide), 0, 0)
    return core, after


def whole_kernel(
    hid, cot, wide_ref, small, wo_ref, hd_ref, sk_ref,
    out_ref, n_ref, ct_ref, w_ref, dp_ref, mixed_ref, gn_out,
    dgain_ref, dskip_ref, dconv_ref, dhead_ref,
    sm_ref, gain_ref, conv_ref, z_ref, xbc_ref, cvo_ref, raw_ref, core_ref, y_ref, dm_ref,
    st_ref, sums_ref, got_sums, turned_sums, dcore_ref, po_ref, go_ref, own_out,
    state, halo, hid_v, send, recv, own,
):
    place = Place()
    me = place.s
    barrier = pltpu.get_barrier_semaphore()
    core_peer = place.core_peer()
    x_peers = [place.big_peer(k) for k in (1, 2, 3)]
    group = [place.shard_peer(k) for k in range(1, 8)]
    for peer in group + x_peers + [core_peer]:
        pl.semaphore_signal(barrier, inc=1, device_id=peer, device_id_type=MESH)
    pl.semaphore_wait(barrier, 11)

    def remote(src, dst, index, peer, other=None):
        return pltpu.make_async_remote_copy(
            src_ref=src,
            dst_ref=dst,
            send_sem=send.at[index],
            recv_sem=recv.at[index if other is None else other],
            device_id=peer,
            device_id_type=MESH,
        )

    quarter = pl.multiple_of(48 * place.x, 16)

    def weight_parts(them):
        at = pl.multiple_of(them * OWN, 128)
        rows = pl.ds(quarter, 48)
        return (
            (wide_ref.at[rows, pl.ds(at, OWN)], w_ref.at[me, rows, pl.ds(0, OWN)]),
            (wide_ref.at[rows, pl.ds(at + DI, OWN)], w_ref.at[me, rows, pl.ds(OWN, OWN)]),
            (wide_ref.at[rows, pl.ds(2 * DI, OWN)], w_ref.at[me, rows, pl.ds(2 * OWN, OWN)]),
        )

    locals_ = [
        pltpu.make_async_copy(small, sm_ref.at[me], own.at[0]),
        pltpu.make_async_copy(hid, n_ref.at[me], own.at[1]),
        pltpu.make_async_copy(cot, ct_ref.at[me], own.at[2]),
        pltpu.make_async_copy(hid, hid_v, own.at[3]),
    ]
    for copy in locals_:
        copy.start()
    mine = place.yl == place.c
    own_w = [
        pltpu.make_async_copy(src, dst, own.at[4 + i])
        for i, (src, dst) in enumerate(weight_parts(me))
    ]
    smalls = [remote(small, sm_ref.at[me], k, place.shard_peer(k)) for k in range(1, 8)]
    hids = [remote(hid, n_ref.at[me], 16 + k, place.shard_peer(k)) for k in range(1, 8)]
    cots = [remote(cot, ct_ref.at[me], 24 + k, place.shard_peer(k)) for k in range(1, 8)]
    weights = []
    for k in range(1, 8):
        weights.append(
            [
                remote(src, dst, 40 + 3 * k + i, place.shard_peer(k))
                for i, (src, dst) in enumerate(weight_parts(place.shard_of(k)))
            ]
        )

    @pl.when(mine)
    def _():
        for copy in own_w:
            copy.start()
        for parts in weights:
            for copy in parts:
                copy.start()

    for copy in smalls:
        copy.start()
    for copy in hids:
        copy.start()

    def from_offset(k):
        return lax.rem(place.yl + k // 4, 2)

    for k in range(1, 8):
        @pl.when(from_offset(k) == place.c)
        def _(k=k):
            for copy in weights[k - 1]:
                copy.wait_recv()

    @pl.when(mine)
    def _():
        for copy in own_w:
            copy.wait()

    def w_rows(x, c):
        return w_ref.at[pl.ds(4 * c, 4), pl.ds(pl.multiple_of(48 * x, 16), 48), :]

    w_x = [
        remote(w_rows(place.x, place.c), w_rows(place.x, place.c), 32 + k, x_peers[k - 1])
        for k in (1, 2, 3)
    ]
    for copy in w_x:
        copy.start()
    for copy in w_x:
        copy.wait_recv()
    w_half = w_ref.at[pl.ds(4 * place.c, 4)]
    w_core = remote(w_half, w_half, 36, core_peer)
    w_core.start()

    locals_[0].wait()
    for copy in smalls:
        copy.wait_recv()
    gain_ref[...] = jnp.concatenate([sm_ref[p, 5:6, :576] for p in range(8)], axis=1)
    conv_ref[...] = jnp.concatenate([sm_ref[p, :, :416] for p in range(8)], axis=1)
    gn_out[...] = gain_ref[:, :D]
    gg_at = pl.ds(pl.multiple_of(D + OWN * me, 128), OWN)
    cv_at = pl.ds(pl.multiple_of(OWN * me, 128), OWN)

    def conv_row(k):
        return jnp.concatenate([conv_ref[k : k + 1, cv_at], conv_ref[k : k + 1, DI:]], axis=1)

    locals_[1].wait()
    for copy in hids:
        copy.wait_recv()
    for copy in cots:
        copy.start()
    w_core.wait_recv()

    state[...] = jnp.zeros_like(state)
    halo[...] = jnp.zeros_like(halo)

    @pl.loop(0, LEN // TB)
    def _(i):
        two = pl.ds(2 * i, 2)
        u = n_ref[two].reshape(TB, D).astype(f32)
        scale = lax.rsqrt(jnp.mean(u * u, axis=1, keepdims=True) + epsilon)
        normed = (u * scale * gain_ref[:, :D]).astype(bf16)
        n_ref[two] = normed.reshape(2, BLOCK, D)
        project = dot(normed, w_ref[...].reshape(D, COLS), 1, 0)
        z = project[:, :OWN]
        xbc = project[:, OWN : OWN + 640]
        raw = pltpu.roll(project[:, 1024:1152], 128 - 6 * me, 1)
        z_ref[two] = z.reshape(2, BLOCK, OWN)
        xbc_ref[two] = xbc.reshape(2, BLOCK, 640)
        raw_ref[two] = raw.reshape(2, BLOCK, 128)
        extended = jnp.concatenate([halo[...], xbc], axis=0)
        halo[...] = xbc[TB - 8 :, :]
        conv = conv_row(KCONV)
        for k in range(KCONV):
            conv = conv + conv_row(k) * extended[5 + k : 5 + k + TB, :]
        cvo_ref[two] = conv.reshape(2, BLOCK, 640)
        act = conv * jax.nn.sigmoid(conv)
        dt = softplus(raw + hd_ref[0:1, :])
        log_decay = -jnp.exp(hd_ref[1:2, :]) * dt
        for j in range(TB // BLOCK):
            at = slice(j * BLOCK, (j + 1) * BLOCK)
            before = state[...]
            st_ref[2 * i + j] = before
            core, after = forward_block(act[at], dt[at], log_decay[at], before)
            state[...] = after
            core_ref[2 * i + j] = core
            y_ref[2 * i + j] = core + sk_ref[0:1, :] * act[at, :OWN]

    locals_[2].wait()
    for copy in cots:
        copy.wait_recv()

    @pl.loop(0, LEN // TB)
    def _(i):
        two = pl.ds(2 * i, 2)
        dm = dot(ct_ref[two].reshape(TB, D), wo_ref[...], 1, 1)
        dm_ref[two] = dm.reshape(2, BLOCK, OWN)
        z = z_ref[two].reshape(TB, OWN)
        gated = y_ref[two].reshape(TB, OWN) * (z * jax.nn.sigmoid(z))
        ones = jnp.ones((8, OWN), f32)
        first = ones_dot(ones, gated * gated, 1, 1)
        second = ones_dot(ones, gated * (gain_ref[:, gg_at] * dm), 1, 1)
        for j in range(2):
            sums_ref[pl.ds(2 * i + j, 1), :] = first[0:1, 128 * j : 128 * j + 128]
            sums_ref[pl.ds(2 * i + j + 8, 1), :] = second[0:1, 128 * j : 128 * j + 128]

    sums = [remote(sums_ref, got_sums.at[me], 64 + k, place.shard_peer(k)) for k in range(1, 8)]
    for copy in sums:
        copy.start()
    got_sums[me] = sums_ref[...]
    for copy in sums:
        copy.wait_recv()
    totals = got_sums[0]
    for j in range(1, 8):
        totals += got_sums[j]
    turned_sums[...] = jnp.concatenate([totals, jnp.zeros((112, 128), f32)], axis=0).T
    gain = gain_ref[:, gg_at]
    lane = lanes((BLOCK, 128))
    dgain_ref[...] = jnp.zeros_like(dgain_ref)
    dskip_ref[...] = jnp.zeros_like(dskip_ref)
    dconv_ref[...] = jnp.zeros_like(dconv_ref)
    dhead_ref[...] = jnp.zeros_like(dhead_ref)

    def out_copy(b):
        return remote(po_ref.at[b], go_ref.at[me], 72 + b, (place.d, b), 80 + me)

    @pl.loop(0, BLOCKS)
    def _(i):
        b = lax.rem(me + 1 + i, BLOCKS)
        column = turned_sums[...]
        first = jnp.sum(jnp.where(lane == b, column, 0.0), axis=1, keepdims=True)
        second = jnp.sum(jnp.where(lane == b + 8, column, 0.0), axis=1, keepdims=True)
        z, y, dm = z_ref[b], y_ref[b], dm_ref[b]
        sig_z = jax.nn.sigmoid(z)
        gate = z * sig_z
        scale = lax.rsqrt(first * (1.0 / DI) + epsilon)
        unit = y * gate * scale
        mixed = (unit * gain).astype(bf16)
        mixed_ref[b] = mixed
        dgain_ref[0:1, :] += jnp.sum(dm * unit, axis=0, keepdims=True)
        dgated = scale * (gain * dm) - unit * (scale * scale * (second * (1.0 / DI)))
        dz = dgated * y * (sig_z * (1.0 + z * (1.0 - sig_z)))
        dp_ref[b, :, :OWN] = dz.astype(bf16)
        dcore_ref[b] = dgated * gate
        part = dot(mixed, wo_ref[...], 1, 0)

        @pl.when(i < BLOCKS - 1)
        def _():
            po_ref[b] = part.astype(bf16)
            out_copy(b).start()

        @pl.when(i == BLOCKS - 1)
        def _():
            own_out[...] = part

    state[...] = jnp.zeros_like(state)
    halo[...] = jnp.zeros_like(halo)

    @pl.loop(0, BLOCKS)
    def _(i):
        b = BLOCKS - 1 - i
        conv, raw, core, dcore = cvo_ref[b], raw_ref[b], core_ref[b], dcore_ref[b]
        sig = jax.nn.sigmoid(conv)
        act = conv * sig
        x, keys, query = act[:, :OWN], act[:, OWN : OWN + NS], act[:, OWN + NS :]
        shifted = raw + hd_ref[0:1, :]
        dt = softplus(shifted)
        rate = jnp.exp(hd_ref[1:2, :])
        log_decay = -rate * dt
        dskip_ref[0:1, :] += jnp.sum(dcore * x, axis=0, keepdims=True)
        cumulative, turned, wide = decay_parts(log_decay)
        contact = dot3(query, keys, 1, 1)
        dt_wide = widen(dt)
        scaled = x * dt_wide
        dcontact = jnp.zeros((BLOCK, BLOCK), f32)
        dscaled = []
        for p in range(3):
            at = slice(128 * p, 128 * p + 128)
            mixing = [head_mixing(cumulative, turned, 2 * p + q) for q in range(2)]
            both = jnp.concatenate([m * contact for m in mixing], axis=0)
            pair = split_pair(dcore[:, at])
            dscaled.append(dot3(both, pair, 0, 0))
            dmix = dot3(pair, scaled[:, at], 1, 1)
            dcontact += dmix[:BLOCK] * mixing[0] + dmix[BLOCK:] * mixing[1]
        last = wide[BLOCK - 1 : BLOCK, :]
        before = st_ref[b]
        after_adj = state[...]
        left = jnp.exp(last - wide)
        from_core = dcore * jnp.exp(wide)
        dquery = dot3(from_core, before, 1, 1) + dot3(dcontact, keys, 1, 0)
        carried = dot3(keys, after_adj, 1, 0) * left
        dscaled = jnp.concatenate(dscaled, axis=1) + carried
        dkeys = dot3(scaled * left, after_adj, 1, 1) + dot3(dcontact, query, 0, 0)
        end = jnp.exp(last)
        state[...] = end * after_adj + dot3(query, from_core, 0, 0)
        heads = head_ones()
        last_add = dot_exact(
            jnp.sum(carried * scaled, axis=0, keepdims=True)
            + end * jnp.sum(after_adj * before, axis=0, keepdims=True),
            heads, 1, 0,
        )
        dcum = dot_exact(dcore * core - dscaled * scaled, heads, 1, 0)
        dlog = ones_dot(lower_ones(), dcum, 0, 0) + last_add
        ddt = dot_exact(dscaled * x, heads, 1, 0) - rate * dlog
        draw = ddt * jax.nn.sigmoid(shifted)
        dhead_ref[0:1, :] += jnp.sum(draw, axis=0, keepdims=True)
        dhead_ref[1:2, :] += jnp.sum(dlog * log_decay, axis=0, keepdims=True)
        dx = dscaled * dt_wide + sk_ref[0:1, :] * dcore
        dact = jnp.concatenate([dx, dkeys, dquery], axis=1)
        dconv = dact * (sig * (1.0 + conv * (1.0 - sig)))
        extended = jnp.concatenate([dconv, halo[...]], axis=0)
        halo[...] = dconv[:8, :]
        xbc = xbc_ref[b]
        dxbc = jnp.zeros_like(xbc)
        for k in range(KCONV):
            moved = extended[3 - k : 3 - k + BLOCK, :]
            dxbc += conv_row(k) * moved
            dconv_ref[k : k + 1, :] += jnp.sum(xbc * moved, axis=0, keepdims=True)
        dconv_ref[KCONV : KCONV + 1, :] += jnp.sum(dconv, axis=0, keepdims=True)
        dp_ref[b, :, OWN : OWN + 640] = dxbc.astype(bf16)
        draw_own = jnp.where(lane < 6, draw, 0.0)
        dp_ref[b, :, 1024:] = pltpu.roll(draw_own, 6 * me, 1).astype(bf16)

    locals_[3].wait()
    own_out[...] += hid_v[...].astype(f32)

    @pl.loop(1, BLOCKS)
    def _(k):
        j = lax.rem(me + k, BLOCKS)
        remote(po_ref.at[j], go_ref.at[j], 72 + j, (place.d, j), 80 + j).wait_recv()
        own_out[...] += go_ref[j].astype(f32)

    out_ref[...] = own_out[...].astype(bf16)

    for copy in smalls + hids + cots + sums + w_x + [w_core]:
        copy.wait_send()

    @pl.when(mine)
    def _():
        for parts in weights:
            for copy in parts:
                copy.wait_send()

    @pl.loop(1, BLOCKS)
    def _(k):
        out_copy(lax.rem(me + k, BLOCKS)).wait_send()


def sds(shape, dtype=f32):
    return jax.ShapeDtypeStruct(shape, dtype)


def run_whole(hid, cot, wide, small, wo, hd, sk):
    any_spec = pl.BlockSpec(memory_space=pl.ANY)
    vmem = pl.BlockSpec(memory_space=pltpu.VMEM)

    def v(*shape, dtype=f32):
        return pltpu.VMEM(shape, dtype)

    return pl.pallas_call(
        whole_kernel,
        in_specs=[any_spec] * 4 + [vmem] * 3,
        out_specs=tuple([vmem] * 11),
        out_shape=(
            sds((BLOCK, D), bf16), sds((8, BLOCK, D), bf16), sds((8, BLOCK, D), bf16),
            sds((8, 192, COLS), bf16), sds((8, BLOCK, COLS), bf16), sds((8, BLOCK, OWN), bf16),
            sds((1, D)), sds((8, OWN)), sds((8, OWN)), sds((8, 640)), sds((8, 128)),
        ),
        scratch_shapes=[
            v(8, 8, 640), v(1, 4608), v(8, CONVC), v(8, BLOCK, OWN), v(8, BLOCK, 640),
            v(8, BLOCK, 640), v(8, BLOCK, 128), v(8, BLOCK, OWN), v(8, BLOCK, OWN),
            v(8, BLOCK, OWN), v(8, NS, OWN), v(16, 128), v(8, 16, 128), v(BLOCK, 128),
            v(8, BLOCK, OWN), v(8, BLOCK, D, dtype=bf16), v(8, BLOCK, D, dtype=bf16),
            v(BLOCK, D), v(NS, OWN), v(8, 640), v(BLOCK, D, dtype=bf16),
            pltpu.SemaphoreType.DMA((88,)), pltpu.SemaphoreType.DMA((88,)),
            pltpu.SemaphoreType.DMA((7,)),
        ],
        compiler_params=pltpu.CompilerParams(
            collective_id=1, has_side_effects=True, vmem_limit_bytes=VMEM_LIMIT
        ),
    )(hid, cot, wide, small, wo, hd, sk)


def adam_update(master, first, second, gradient, rate, decay):
    first_new = beta_one * first + (1.0 - beta_one) * gradient
    second_new = beta_two * second + (1.0 - beta_two) * gradient * gradient
    scaled = (
        first_new
        / (1.0 - beta_one**STEP)
        / (jnp.sqrt(second_new / (1.0 - beta_two**STEP)) + adam_epsilon)
    )
    return (first_new, second_new, master - rate * (scaled + decay * master))


def on_device(
    hidden, cotangent, in_master, in_first, in_second, out_master, out_first, out_second,
    gain_master, gain_first, gain_second, conv_master, conv_first, conv_second,
    head_master, head_first, head_second,
):
    s = lax.axis_index("shard")
    c = lax.rem(lax.axis_index("dp"), 2)
    low = lambda v: lax.reduce_precision(v, 8, 7)
    wide = jnp.pad(in_master.astype(bf16), ((0, 0), (0, WIDE - PROJ)))
    wo = out_master.astype(bf16)
    small = jnp.concatenate(
        [
            jnp.pad(low(conv_master), ((0, 0), (0, 224))),
            jnp.pad(low(gain_master), (0, 64))[None],
            jnp.zeros((2, 640), f32),
        ],
        axis=0,
    )
    heads = low(head_master)
    hd = jnp.pad(heads, ((0, 5), (0, 122)))
    sk = jnp.repeat(heads[2], HD)[None]
    layer_out, normed, ct, w, dproj, mixed, gn, dgain, dskip, dconv, dhead = run_whole(
        hidden[0], cotangent[0], wide, small, wo, hd, sk
    )
    normed, ct, w = normed.reshape(LEN, D), ct.reshape(LEN, D), w.reshape(D, COLS)
    dproj, mixed = dproj.reshape(LEN, COLS), mixed.reshape(LEN, OWN)
    dgain, dskip, dconv, dhead = dgain[0], dskip[0], dconv[:5], dhead[:2, :6]
    grad_o = dot(mixed, ct, 0, 0)
    grad_w = dot(normed, dproj, 0, 0)
    part_in = dot(dproj, w, 1, 1).astype(bf16).reshape(8, BLOCK, D)
    (got_in,) = exchange(3, scatter_body, (part_in,), (sds((8, BLOCK, D), bf16),), 7, 1)
    inputs = hidden[0].astype(f32)
    d_normed = jnp.sum(got_in.astype(f32), axis=0)
    scale = lax.rsqrt(jnp.mean(inputs * inputs, axis=-1, keepdims=True) + epsilon)
    gained = gn * d_normed
    grad_inputs = scale * gained - inputs * scale**3 * jnp.mean(
        inputs * gained, axis=-1, keepdims=True
    )
    input_grad = (cotangent[0].astype(f32) + grad_inputs).astype(bf16)
    dnorm = jnp.sum(d_normed * inputs * scale, axis=0)
    small_grad = jnp.concatenate(
        [
            dnorm, dgain, dconv[:, :OWN].reshape(-1), dconv[:, OWN:].reshape(-1),
            dhead.reshape(-1), jnp.sum(dskip.reshape(6, HD), axis=1), jnp.zeros((1006,), f32),
        ]
    ).reshape(48, 128)

    grad_w = grad_w.reshape(8, 8, 24, COLS)
    grad_o = grad_o.reshape(8, 48, D)
    swap_w, swap_o = exchange(
        4, swap_body, (grad_w, grad_o), (sds((4, 8, 24, COLS), f32), sds((8, 48, 768), f32)), 2, 0
    )
    half_w = (
        lax.dynamic_slice_in_dim(grad_w, 4 * c, 4, 0).astype(f32) + swap_w.astype(f32)
    ).astype(bf16)
    half_o = (
        lax.dynamic_slice_in_dim(grad_o, 768 * c, 768, 2).astype(f32) + swap_o.astype(f32)
    ).astype(bf16)
    got_w, got_o = exchange(
        5, reduce_body, (half_w, half_o),
        (sds((8, 4, 24, COLS), bf16), sds((8, 48, 768), bf16)), 14, 2,
    )
    piece_w = jnp.sum(got_w.astype(f32), axis=0)
    piece_o = jnp.sum(got_o.astype(f32), axis=0)
    own_w, small_all = exchange(
        6, owner_body, (piece_w, small_grad), (sds((8, 24, COLS)), sds((8, 48, 128))), 14, 2
    )
    own_w = own_w.transpose(1, 0, 2)
    slab = jnp.concatenate(
        [
            own_w[:, :, :OWN].reshape(24, DI),
            own_w[:, :, OWN : 2 * OWN].reshape(24, DI),
            jnp.sum(own_w[:, :, 2 * OWN :], axis=1),
        ],
        axis=1,
    )
    flat = small_all.reshape(8, 6144)
    g_gain = jnp.concatenate([jnp.sum(flat[:, :D], axis=0), flat[:, D : D + OWN].reshape(-1)])
    g_conv = jnp.concatenate(
        [
            flat[:, 1920:3840].reshape(8, 5, OWN).transpose(1, 0, 2).reshape(5, DI),
            jnp.sum(flat[:, 3840:5120], axis=0).reshape(5, 256),
        ],
        axis=1,
    )
    own_small = jnp.concatenate(
        [
            lax.dynamic_slice(g_gain, (576 * s,), (576,)),
            lax.dynamic_slice(g_conv, (0, 416 * s), (5, 416)).reshape(-1),
            lax.dynamic_slice(flat, (s, 5120), (1, 18))[0],
            jnp.zeros((398,), f32),
        ]
    ).reshape(24, 128)
    total_w, total_o, total_small = exchange(
        7, spread_body, (slab, piece_o, own_small),
        (sds((8, 24, WIDE)), sds((8, 48, D)), sds((16, 24, 128))), 45, 3,
    )
    total_small = jnp.sum(total_small, axis=0).reshape(-1)
    totals = (
        total_w.reshape(192, WIDE)[:, :PROJ].astype(f32),
        total_o.reshape(OWN, D).astype(f32),
        total_small[:576],
        total_small[576:2656].reshape(5, 416),
        total_small[2656:2674].reshape(3, 6),
    )
    masters = (in_master, out_master, gain_master, conv_master, head_master)
    firsts = (in_first, out_first, gain_first, conv_first, head_first)
    seconds = (in_second, out_second, gain_second, conv_second, head_second)
    updated = [
        adam_update(masters[g], firsts[g], seconds[g], totals[g], rates[g], decays[g])
        for g in range(5)
    ]
    return (layer_out[None], input_grad[None]) + tuple(v for group in updated for v in group)


def solution(mesh):
    rows, columns = P("shard", None), P(None, "shard")
    tokens = P("dp", "shard", None)
    state = (rows,) * 6 + (P("shard"),) * 3 + (columns,) * 6
    return jax.shard_map(
        on_device,
        mesh=mesh,
        in_specs=(tokens, tokens) + state,
        out_specs=(tokens, tokens) + state,
        check_vma=False,
    )
```

time: 477 us -> 384 us (0.81)
  Pallas kernels: 365 us -> 302 us
  local copies, waits for them, and re-layouts: 28.3 us -> 13.3 us
  other arithmetic: 53.9 us -> 43.6 us
    pallas_call x7 -> x5, Pallas kernels: 311 us -> 157 us  [exchange(): pl.pallas_call(kernel, out_shape=outs, in_specs=[any_spec] * len(ins), ou...]
    pallas_call x2 -> x1, Pallas kernels: 54.4 us -> 145 us  [run_whole(): pl.pallas_call(whole_kernel, in_specs=[any_spec] * 4 + [vmem] * 3, out_sp...]
    dot_general x4 -> x3, matrix products: 27 us -> 23.4 us  [dot(): lax.dot_general(a, b, (((ca,), (cb,)), ((), ())), precision=precision, pr...]
where the time goes in v2:
time: 384 us; the launch traced here: 383 us
  Pallas kernels  302 us (79%)
  other arithmetic  43.6 us (11%)
  matrix products  23.4 us (6%)
  local copies, waits for them, and re-layouts  13.3 us (3%)
    pallas_call x5, Pallas kernels, exchange(): pl.pallas_call(kernel, out_shape=outs, in_specs=[any_spec] * len(ins), ou...  157 us
    pallas_call x1, Pallas kernels, run_whole(): pl.pallas_call(whole_kernel, in_specs=[any_spec] * 4 + [vmem] * 3, out_sp...  145 us
    dot_general x3, matrix products, dot(): lax.dot_general(a, b, (((ca,), (cb,)), ((), ())), precision=precision, pr...  23.4 us
    sub x5, other arithmetic, adam_update(): return (first_new, second_new, master - rate * (scaled + decay * master))  20.3 us

profile of v2, /device:TPU:1, one launch (start us, length us, event | category | flops | bytes accessed | tf_op | source)
XLA Modules:
  0.0 383.2 jit_solution(9515870840623390100)
XLA Ops:
  0.7 2.7 convert_element_type.46
  3.4 1.6 pad.16.wide_ref
  5.1 0.1 pad.29.clone
  5.1 0.7 fusion.11.small
  5.8 0.1 copy-done
  5.9 1.1 convert_element_type.47.wo_ref
  7.1 0.6 pad.19.hd_ref
  7.8 0.6 broadcast_in_dim_reshape.3.sk_ref
  8.4 144.7 %shard_map.296 = (bf16[128,1536]{1,0:T(8,128)(2,1)}, bf16[8,128,1536]{2,1,0:T(8,128)(2,1)}, bf16[8,128,1536]{2,1,0:T(8,128)(2,1)}, bf16[8,192,1152]{2,1,0:T(8,12...) custom-call(bf16[128,1536]{1,0:T(8,128)(2,1)} %bitcast.71, ...), custom_call_target="tpu_custom_call" | custom-call | tf_op jit(solution)/shard_map/pallas_call | solution.py:731
  153.1 8.6 %convolution_convert_fusion = bf16[1024,1536]{1,0:T(8,128)(2,1)} fusion(bf16[1024,1152]{1,0:T(8,128)(2,1)} %bitcast.98, bf16[1536,1152]{1,0:T(8,128)(2,1)} %bitcast.96), kind=kOutput, calls=%fused_computation.5 | convolution fusion | flops 3625451520 | bytes 9043968 | tf_op jit(solution)/shard_map/dot_general | solution.py:298
  161.8 41.9 %shard_map.297 = bf16[8,128,1536]{2,1,0:T(8,128)(2,1)} custom-call(bf16[8,128,1536]{2,1,0:T(8,128)(2,1)} %bitcast.75), custom_call_target="tpu_custom_call" | custom-call | tf_op jit(solution)/shard_map/pallas_call | solution.py:101
  203.7 2.4 convert_reduce_fusion
  206.1 0.2 fusion.3
  206.3 0.5 multiply_multiply_fusion.5
  206.9 0.9 fusion.6
  207.8 2.1 fusion.10
  209.9 4.6 %copy.34 = bf16[1536,1024]{1,0:T(8,128)(2,1)} copy(bf16[1536,1024]{0,1:T(8,128)(2,1)} %bitcast.73) | data formatting | bytes 6291456 | tf_op jit(solution)/shard_map/dot_general | solution.py:298
  214.5 9.9 %fusion.23.refs_0_ = f32[8,8,24,1152]{3,2,1,0:T(8,128)} fusion(bf16[8,8,24,1024]{3,2,1,0:T(8,128)(2,1)} %bitcast.74, bf16[1024,1152,1,1]{1,0,3,2:T(8,128)(2,1)} %bitcast.99), kind=kOutput, calls=%fused_computation.62 | convolution fusion | flops 3623878656 | bytes 12582912 | tf_op jit(solution)/shard_map/dot_general | solution.py:298
  224.4 1.2 copy.35
  225.5 4.9 %fusion.24.refs_1_ = f32[8,48,1536]{2,1,0:T(8,128)} fusion(bf16[8,48,1024]{2,1,0:T(8,128)(2,1)} %bitcast.81, bf16[1024,1536,1]{1,0,2:T(8,128)(2,1)} %bitcast.97), kind=kOutput, calls=%fused_computation.63 | convolution fusion | flops 1207959552 | bytes 6291456 | tf_op jit(solution)/shard_map/dot_general | solution.py:298
  230.5 8.4 %shard_map.298 = (f32[4,8,24,1152]{3,2,1,0:T(8,128)}, f32[8,48,768]{2,1,0:T(8,128)}) custom-call(f32[8,8,24,1152]{3,2,1,0:T(8,128)} %fusion.23.refs_0_, f32[8,48,1536]{2,1,0:T(8,128)} %fusion.24.refs_1_), custom_call_target="tpu_custom_call" | custom-call | tf_op jit(solution)/shard_map/pallas_call | solution.py:101
  238.9 4.7 %add_convert_fusion.refs_0_ = bf16[4,8,24,1152]{3,2,1,0:T(8,128)(2,1)} fusion(f32[4,8,24,1152]{3,2,1,0:T(8,128)} %get-tuple-element.44, f32[8,8,24,1152]{3,2,1,0:T(8,128)} %fusion.23.refs_0_, s32[]{:T(128)S(6)} %select_n.15), kind=kLoop, calls=%fused_computation.7 | loop fusion | flops 1769472 | bytes 8847364 | tf_op jit(solution)/shard_map/convert_element_type | solution.py:820
  243.6 2.2 add_convert_fusion.1.refs_1_
  245.8 35.3 %shard_map.299 = (bf16[8,4,24,1152]{3,2,1,0:T(8,128)(2,1)}, bf16[8,48,768]{2,1,0:T(8,128)(2,1)}) custom-call(bf16[4,8,24,1152]{3,2,1,0:T(8,128)(2,1)} %add_convert_fusion.refs_0_, bf16[8,48,768]{2,1,0:T(8,128)(2,1)} %add_convert_fusion.1.refs_1_), custom_call_target="tpu_custom_call" | custom-call | tf_op jit(solution)/shard_map/pallas_call | solution.py:101
  281.1 2.6 convert_reduce_fusion.1.refs_0_
  283.7 0.7 slice_reduce_fusion.3
  284.5 0.7 slice.58
  285.1 0.1 reshape.203
  285.2 0.1 reshape_squeeze.3
  285.3 0.1 reduce_sum.107
  285.4 0.7 concatenate.19
  286.1 10.2 %shard_map.300 = (f32[8,24,1152]{2,1,0:T(8,128)}, f32[8,48,128]{2,1,0:T(8,128)}) custom-call(f32[4,24,1152]{2,1,0:T(8,128)} %convert_reduce_fusion.1.refs_0_, f32[48,128]{1,0:T(8,128)} %bitcast.91), custom_call_target="tpu_custom_call" | custom-call | tf_op jit(solution)/shard_map/pallas_call | solution.py:101
  296.3 1.2 slice_bitcast_fusion.1
  297.6 0.9 pad_maximum_fusion.refs_0_
  298.5 0.7 convert_reduce_fusion.2.refs_1_
  299.3 0.1 fusion.15
  299.5 0.1 fusion.13
  299.6 0.1 reshape.212
  299.7 0.7 concatenate.23
  300.4 61.3 %shard_map.301 = (f32[8,24,6528]{2,1,0:T(8,128)}, f32[8,48,1536]{2,1,0:T(8,128)}, f32[16,24,128]{2,1,0:T(8,128)}) custom-call(f32[24,6528]{1,0:T(8,128)} %pad_maximum_fusion.refs_0_, f32[48,768]{1,0:T(8,128)} %convert_reduce_fusion.2.refs_1_, f32[24,128]{1,0:T(8,128)} %bitcast.95), custom_call_target="tpu_custom_call" | custom-call | tf_op jit(solution)/shard_map/pallas_call | solution.py:101
  361.7 14.2 %multiply_subtract_fusion = (f32[192,6448]{1,0:T(8,128)}, f32[192,6448]{1,0:T(8,128)}, f32[192,6448]{1,0:T(8,128)}) fusion(f32[192,6448]{1,0:T(8,128)} %param.19, f32[192,6528]{1,0:T(8,128)} %bitcast.72, f32[192,6448]{1,0:T(8,128)} %param.21, f32[192,6448]{1,0:T(8,128)} %param.20), kind=kLoop, calls=%fused_computation.3 | loop fusion | flops 18570240 | bytes 34664448 | tf_op jit(solution)/shard_map/sub | solution.py:763
  376.0 4.2 %multiply_subtract_fusion.1 = (f32[384,1536]{1,0:T(8,128)}, f32[384,1536]{1,0:T(8,128)}, f32[384,1536]{1,0:T(8,128)}) fusion(f32[384,1536]{1,0:T(8,128)S(1)} %copy-done, f32[8,48,1536]{2,1,0:T(8,128)S(1)} %copy-done.4, f32[384,1536]{1,0:T(8,128)S(1)} %copy-done.2, f32[384,1536]{1,0:T(8,128)S(1)} %copy-done.3), kind=kLoop, calls=%fused_computation.12 | loop fusion | flops 8847360 | bytes 16515072 | tf_op jit(solution)/shard_map/sub | solution.py:763
  380.3 0.6 multiply_subtract_fusion.3
  381.0 0.1 reshape.217
  381.1 0.6 multiply_subtract_fusion.2
  381.8 0.1 reshape.218
  381.9 0.6 multiply_subtract_fusion.4
  382.5 0.7 copy.46
  (79 shorter events, 0.6 us)
Async XLA Ops:
  3.3 1.7 copy-start.11
  3.4 1.7 copy-start.16
  3.4 2.6 copy-start
  3.4 3.7 copy-start.18
  203.7 2.5 copy-start.1
  203.7 3.1 copy-start.20
  214.5 9.9 %copy-start.6 = (bf16[8,128,384]{2,1,0:T(8,128)(2,1)S(1)}, bf16[8,128,384]{2,1,0:T(8,128)(2,1)}, u32[]{:S(2)}) copy-start(bf16[8,128,384]{2,1,0:T(8,128)(2,1)} %get-tuple-element.42) | copy-start | bytes 2359300
  238.9 4.7 %copy-start.5 = (f32[8,48,768]{2,1,0:T(8,128)S(1)}, f32[8,48,768]{2,1,0:T(8,128)}, u32[]{:S(2)}) copy-start(f32[8,48,768]{2,1,0:T(8,128)} %get-tuple-element.45) | copy-start | bytes 3538948
  245.8 38.6 %copy-start.13 = (f32[8,640]{1,0:T(8,128)S(1)}, f32[8,640]{1,0:T(8,128)}, u32[]{:S(2)}) copy-start(f32[8,640]{1,0:T(8,128)} %get-tuple-element.48) | copy-start | bytes 61444
  281.1 17.4 %copy-start.7 = (bf16[8,48,768]{2,1,0:T(8,128)(2,1)S(1)}, bf16[8,48,768]{2,1,0:T(8,128)(2,1)}, u32[]{:S(2)}) copy-start(bf16[8,48,768]{2,1,0:T(8,128)(2,1)} %get-tuple-element.52) | copy-start | bytes 1769476
  296.3 2.9 copy-start.9
  361.7 14.2 %copy-start.2 = (f32[384,1536]{1,0:T(8,128)S(1)}, f32[384,1536]{1,0:T(8,128)}, u32[]{:S(2)}) copy-start(f32[384,1536]{1,0:T(8,128)} %param.24) | copy-start | bytes 7077892
  361.7 14.2 %copy-start.3 = (f32[384,1536]{1,0:T(8,128)S(1)}, f32[384,1536]{1,0:T(8,128)}, u32[]{:S(2)}) copy-start(f32[384,1536]{1,0:T(8,128)} %param.23) | copy-start | bytes 7077892
  361.7 14.2 %copy-start.4 = (f32[8,48,1536]{2,1,0:T(8,128)S(1)}, f32[8,48,1536]{2,1,0:T(8,128)}, u32[]{:S(2)}) copy-start(f32[8,48,1536]{2,1,0:T(8,128)} %get-tuple-element.55) | copy-start | bytes 7077892
  375.9 4.4 %copy-start.10 = (f32[16,24,128]{2,1,0:T(8,128)S(1)}, f32[16,24,128]{2,1,0:T(8,128)}, u32[]{:S(2)}) copy-start(f32[16,24,128]{2,1,0:T(8,128)} %get-tuple-element.56) | copy-start | bytes 589828
  375.9 4.4 %copy-start.17 = (f32[576]{0:T(1024)S(1)}, f32[576]{0:T(1024)}, u32[]{:S(2)}) copy-start(f32[576]{0:T(1024)} %param.25) | copy-start | bytes 6916
  375.9 4.4 %copy-start.21 = (f32[576]{0:T(1024)S(1)}, f32[576]{0:T(1024)}, u32[]{:S(2)}) copy-start(f32[576]{0:T(1024)} %param.27) | copy-start | bytes 6916
  375.9 4.4 %copy-start.22 = (f32[576]{0:T(1024)S(1)}, f32[576]{0:T(1024)}, u32[]{:S(2)}) copy-start(f32[576]{0:T(1024)} %param.26) | copy-start | bytes 6916
  375.9 5.2 %copy-start.12 = (f32[5,416]{1,0:T(8,128)S(1)}, f32[5,416]{1,0:T(8,128)}, u32[]{:S(2)}) copy-start(f32[5,416]{1,0:T(8,128)} %param.28) | copy-start | bytes 24964
  375.9 5.1 %copy-start.14 = (f32[5,416]{1,0:T(8,128)S(1)}, f32[5,416]{1,0:T(8,128)}, u32[]{:S(2)}) copy-start(f32[5,416]{1,0:T(8,128)} %param.30) | copy-start | bytes 24964
  375.9 5.1 %copy-start.15 = (f32[5,416]{1,0:T(8,128)S(1)}, f32[5,416]{1,0:T(8,128)}, u32[]{:S(2)}) copy-start(f32[5,416]{1,0:T(8,128)} %param.29) | copy-start | bytes 24964
  375.9 5.9 %copy-start.19 = (f32[3,6]{1,0:T(4,128)S(1)}, f32[3,6]{1,0:T(4,128)}, u32[]{:S(2)}) copy-start(f32[3,6]{1,0:T(4,128)} %param.31) | copy-start | bytes 220
  376.0 5.9 %copy-start.23 = (f32[3,6]{1,0:T(4,128)S(1)}, f32[3,6]{1,0:T(4,128)}, u32[]{:S(2)}) copy-start(f32[3,6]{1,0:T(4,128)} %param.33) | copy-start | bytes 220
  376.0 5.9 %copy-start.24 = (f32[3,6]{1,0:T(4,128)S(1)}, f32[3,6]{1,0:T(4,128)}, u32[]{:S(2)}) copy-start(f32[3,6]{1,0:T(4,128)} %param.32) | copy-start | bytes 220
  376.0 6.5 %copy-start.8 = (bf16[128,1536]{1,0:T(8,128)(2,1)S(1)}, bf16[128,1536]{1,0:T(8,128)(2,1)}, u32[]{:S(2)}) copy-start(bf16[128,1536]{1,0:T(8,128)(2,1)} %get-tuple-element.37) | copy-start | bytes 1179652

commit v3 on v2

--- a/solution.py
+++ b/solution.py
@@ -110,102 +110,6 @@
         ],
         compiler_params=pltpu.CompilerParams(collective_id=cid, has_side_effects=True),
     )(*ins)
-
-
-def scatter_body(place, meet, remote, local, ins, outs):
-    meet([place.shard_peer(k) for k in ORDER])
-    copies = []
-    for a in range(len(ins)):
-        copies.append(local(ins[a].at[place.s], outs[a].at[place.s], a))
-    for n, k in enumerate(ORDER):
-        for a in range(len(ins)):
-            copies.append(
-                remote(
-                    ins[a].at[place.shard_of(k)],
-                    outs[a].at[place.s],
-                    n * len(ins) + a,
-                    place.shard_peer(k),
-                )
-            )
-    for copy in copies:
-        copy.start()
-    for copy in copies:
-        copy.wait()
-
-
-def swap_body(place, meet, remote, local, ins, outs):
-    gw, go = ins
-    gw_out, go_out = outs
-    meet([place.core_peer()])
-    other = 1 - place.c
-    copies = [
-        remote(gw.at[pl.ds(other * 4, 4)], gw_out, 0, place.core_peer()),
-        remote(
-            go.at[:, :, pl.ds(pl.multiple_of(other * 768, 128), 768)],
-            go_out,
-            1,
-            place.core_peer(),
-        ),
-    ]
-    for copy in copies:
-        copy.start()
-    for copy in copies:
-        copy.wait()
-
-
-def reduce_body(place, meet, remote, local, ins, outs):
-    hw, ho = ins
-    hw_out, ho_out = outs
-    meet([place.big_peer(k) for k in ORDER])
-    copies = [
-        local(hw.at[:, place.big], hw_out.at[0], 0),
-        local(ho.at[place.big], ho_out.at[0], 1),
-    ]
-    for n, k in enumerate(ORDER):
-        them = place.big_of(k)
-        copies.append(remote(hw.at[:, them], hw_out.at[k], 2 * n, place.big_peer(k)))
-        copies.append(remote(ho.at[them], ho_out.at[k], 2 * n + 1, place.big_peer(k)))
-    for copy in copies:
-        copy.start()
-    for copy in copies:
-        copy.wait()
-
-
-def owner_body(place, meet, remote, local, ins, outs):
-    piece, small = ins
-    piece_out, small_out = outs
-    meet([place.shard_peer(k) for k in ORDER])
-    valid = place.yl == place.c
-    own_small = local(small, small_out.at[place.s], 0)
-    own_small.start()
-    own_piece = local(piece.at[place.z], piece_out.at[place.s], 1)
-
-    @pl.when(valid)
-    def _():
-        own_piece.start()
-
-    smalls = [
-        remote(small, small_out.at[place.s], n, place.shard_peer(k))
-        for n, k in enumerate(ORDER)
-    ]
-    for copy in smalls:
-        copy.start()
-    pieces = []
-    for n, k in enumerate(ORDER):
-        them = place.shard_of(k)
-        copy = remote(
-            piece.at[lax.rem(them, 4)], piece_out.at[place.s], 7 + n, place.shard_peer(k)
-        )
-        goes = them // 4 == place.c
-        pl.when(goes)(copy.start)
-        pieces.append((copy, goes))
-    own_small.wait()
-    pl.when(valid)(own_piece.wait)
-    for copy in smalls:
-        copy.wait()
-    for copy, goes in pieces:
-        pl.when(goes)(copy.wait_send)
-        pl.when(valid)(copy.wait_recv)
 
 
 def spread_body(place, meet, remote, local, ins, outs):
@@ -379,6 +283,15 @@
     return cumulative, cumulative.T, widen(cumulative)
 
 
+def two_blocks(ref, i, columns):
+    return ref[i, :, :, :columns].reshape(TB, columns)
+
+
+def block_of(ref, b, columns):
+    four = pl.ds(4 * lax.rem(b, 2), 4)
+    return ref[b // 2, four, :, :columns].reshape(BLOCK, columns)
+
+
 def forward_block(act, dt, log_decay, before):
     x, keys, query = act[:, :OWN], act[:, OWN : OWN + NS], act[:, OWN + NS :]
     cumulative, turned, wide = decay_parts(log_decay)
@@ -398,22 +311,29 @@
 
 
 def whole_kernel(
-    hid, cot, wide_ref, small, wo_ref, hd_ref, sk_ref,
-    out_ref, n_ref, ct_ref, w_ref, dp_ref, mixed_ref, gn_out,
-    dgain_ref, dskip_ref, dconv_ref, dhead_ref,
-    sm_ref, gain_ref, conv_ref, z_ref, xbc_ref, cvo_ref, raw_ref, core_ref, y_ref, dm_ref,
-    st_ref, sums_ref, got_sums, turned_sums, dcore_ref, po_ref, go_ref, own_out,
-    state, halo, hid_v, send, recv, own,
+    hid, cot, in_ref, out_w, small, hd_ref,
+    out_ref, igrad_ref, slab_ref, piece_o_ref, sg_all,
+    n_ref, ct_ref, w_ref, z_ref, big_a, big_b, raw_ref, core_ref, y_ref, dm_ref, st_ref, dcore_ref,
+    dp_ref, mixed_ref, po_ref, go_ref, own_out, wo_f, wq_f, wq, wo_ref, sm_ref, gain_ref, conv_ref,
+    sums_ref, got_sums, turned_sums, rz, ro, own_o, gz, gro, rx, gx, gi_ref, own_dn,
+    piece, ow, sg, dgain_ref, dskip_ref, dconv_ref, dhead_ref,
+    state, halo, hid_v, cot_v, send, recv, own,
 ):
     place = Place()
     me = place.s
+    wq_load = pltpu.make_async_copy(
+        in_ref.at[pl.ds(pl.multiple_of(48 * place.x, 8), 48), :], wq_f, own.at[7]
+    )
+    wq_load.start()
+    wq[:, WIDE - 128 :] = jnp.zeros((48, 128), bf16)
     barrier = pltpu.get_barrier_semaphore()
     core_peer = place.core_peer()
-    x_peers = [place.big_peer(k) for k in (1, 2, 3)]
+    bigs = [place.big_peer(k) for k in range(1, 8)]
+    x_peers = bigs[:3]
     group = [place.shard_peer(k) for k in range(1, 8)]
-    for peer in group + x_peers + [core_peer]:
+    for peer in group + bigs + [core_peer]:
         pl.semaphore_signal(barrier, inc=1, device_id=peer, device_id_type=MESH)
-    pl.semaphore_wait(barrier, 11)
+    pl.semaphore_wait(barrier, 15)
 
     def remote(src, dst, index, peer, other=None):
         return pltpu.make_async_remote_copy(
@@ -431,9 +351,9 @@
         at = pl.multiple_of(them * OWN, 128)
         rows = pl.ds(quarter, 48)
         return (
-            (wide_ref.at[rows, pl.ds(at, OWN)], w_ref.at[me, rows, pl.ds(0, OWN)]),
-            (wide_ref.at[rows, pl.ds(at + DI, OWN)], w_ref.at[me, rows, pl.ds(OWN, OWN)]),
-            (wide_ref.at[rows, pl.ds(2 * DI, OWN)], w_ref.at[me, rows, pl.ds(2 * OWN, OWN)]),
+            (wq.at[:, pl.ds(at, OWN)], w_ref.at[me, rows, pl.ds(0, OWN)]),
+            (wq.at[:, pl.ds(at + DI, OWN)], w_ref.at[me, rows, pl.ds(OWN, OWN)]),
+            (wq.at[:, pl.ds(2 * DI, OWN)], w_ref.at[me, rows, pl.ds(2 * OWN, OWN)]),
         )
 
     locals_ = [
@@ -441,10 +361,23 @@
         pltpu.make_async_copy(hid, n_ref.at[me], own.at[1]),
         pltpu.make_async_copy(cot, ct_ref.at[me], own.at[2]),
         pltpu.make_async_copy(hid, hid_v, own.at[3]),
+        pltpu.make_async_copy(cot, cot_v, own.at[14]),
     ]
     for copy in locals_:
         copy.start()
     mine = place.yl == place.c
+    wo_parts = [
+        pltpu.make_async_copy(
+            out_w.at[pl.ds(BLOCK * (p % 3), BLOCK), pl.ds(768 * (p // 3), 768)],
+            wo_f.at[p],
+            own.at[8 + p],
+        )
+        for p in range(6)
+    ]
+    for copy in wo_parts:
+        copy.start()
+    wq_load.wait()
+    wq[:, :PROJ] = wq_f[...].astype(bf16)
     own_w = [
         pltpu.make_async_copy(src, dst, own.at[4 + i])
         for i, (src, dst) in enumerate(weight_parts(me))
@@ -508,7 +441,6 @@
         copy.wait_recv()
     gain_ref[...] = jnp.concatenate([sm_ref[p, 5:6, :576] for p in range(8)], axis=1)
     conv_ref[...] = jnp.concatenate([sm_ref[p, :, :416] for p in range(8)], axis=1)
-    gn_out[...] = gain_ref[:, :D]
     gg_at = pl.ds(pl.multiple_of(D + OWN * me, 128), OWN)
     cv_at = pl.ds(pl.multiple_of(OWN * me, 128), OWN)
 
@@ -522,8 +454,14 @@
         copy.start()
     w_core.wait_recv()
 
+    for copy in wo_parts:
+        copy.wait()
+    for p in range(6):
+        at = 768 * (p // 3)
+        wo_ref[BLOCK * (p % 3) : BLOCK * (p % 3 + 1), at : at + 768] = wo_f[p].astype(bf16)
     state[...] = jnp.zeros_like(state)
     halo[...] = jnp.zeros_like(halo)
+    skip = hd_ref[3:4, :]
 
     @pl.loop(0, LEN // TB)
     def _(i):
@@ -536,18 +474,18 @@
         z = project[:, :OWN]
         xbc = project[:, OWN : OWN + 640]
         raw = pltpu.roll(project[:, 1024:1152], 128 - 6 * me, 1)
-        z_ref[two] = z.reshape(2, BLOCK, OWN)
-        xbc_ref[two] = xbc.reshape(2, BLOCK, 640)
+        z_ref[i] = z.reshape(8, 32, OWN)
+        big_a[i, :, :, :640] = xbc.reshape(8, 32, 640)
         raw_ref[two] = raw.reshape(2, BLOCK, 128)
         extended = jnp.concatenate([halo[...], xbc], axis=0)
         halo[...] = xbc[TB - 8 :, :]
         conv = conv_row(KCONV)
         for k in range(KCONV):
             conv = conv + conv_row(k) * extended[5 + k : 5 + k + TB, :]
-        cvo_ref[two] = conv.reshape(2, BLOCK, 640)
+        big_b[i, :, :, :640] = conv.reshape(8, 32, 640)
         act = conv * jax.nn.sigmoid(conv)
-        dt = softplus(raw + hd_ref[0:1, :])
-        log_decay = -jnp.exp(hd_ref[1:2, :]) * dt
+        dt = softplus(raw + hd_ref[0:1, :128])
+        log_decay = -jnp.exp(hd_ref[1:2, :128]) * dt
         for j in range(TB // BLOCK):
             at = slice(j * BLOCK, (j + 1) * BLOCK)
             before = state[...]
@@ -555,7 +493,7 @@
             core, after = forward_block(act[at], dt[at], log_decay[at], before)
             state[...] = after
             core_ref[2 * i + j] = core
-            y_ref[2 * i + j] = core + sk_ref[0:1, :] * act[at, :OWN]
+            y_ref[i, 4 * j : 4 * j + 4] = (core + skip * act[at, :OWN]).reshape(4, 32, OWN)
 
     locals_[2].wait()
     for copy in cots:
@@ -565,9 +503,9 @@
     def _(i):
         two = pl.ds(2 * i, 2)
         dm = dot(ct_ref[two].reshape(TB, D), wo_ref[...], 1, 1)
-        dm_ref[two] = dm.reshape(2, BLOCK, OWN)
-        z = z_ref[two].reshape(TB, OWN)
-        gated = y_ref[two].reshape(TB, OWN) * (z * jax.nn.sigmoid(z))
+        dm_ref[i] = dm.reshape(8, 32, OWN)
+        z = two_blocks(z_ref, i, OWN)
+        gated = two_blocks(y_ref, i, OWN) * (z * jax.nn.sigmoid(z))
         ones = jnp.ones((8, OWN), f32)
         first = ones_dot(ones, gated * gated, 1, 1)
         second = ones_dot(ones, gated * (gain_ref[:, gg_at] * dm), 1, 1)
@@ -601,7 +539,7 @@
         column = turned_sums[...]
         first = jnp.sum(jnp.where(lane == b, column, 0.0), axis=1, keepdims=True)
         second = jnp.sum(jnp.where(lane == b + 8, column, 0.0), axis=1, keepdims=True)
-        z, y, dm = z_ref[b], y_ref[b], dm_ref[b]
+        z, y, dm = block_of(z_ref, b, OWN), block_of(y_ref, b, OWN), block_of(dm_ref, b, OWN)
         sig_z = jax.nn.sigmoid(z)
         gate = z * sig_z
         scale = lax.rsqrt(first * (1.0 / DI) + epsilon)
@@ -624,19 +562,78 @@
         def _():
             own_out[...] = part
 
+    def weight_grad(q, columns):
+        left = n_ref[:, :, pl.ds(pl.multiple_of(384 * q, 128), 384)].reshape(LEN, 384)
+        return dot(left, dp_ref[:, :, columns].reshape(LEN, -1), 0, 0)
+
+    def out_grad(h, q):
+        at = pl.multiple_of(768 * h + 384 * q, 128)
+        return dot(mixed_ref[...].reshape(LEN, OWN), ct_ref[:, :, pl.ds(at, 384)].reshape(LEN, 384), 0, 0)
+
+    other = 1 - place.c
+    zs = slice(0, OWN)
+    late = slice(OWN, COLS)
+
+    def rows24(ref):
+        return ref.at[:, :, pl.ds(0, 24), :]
+
+    @pl.loop(0, 2)
+    def _(q):
+        two = pl.ds(2 * q, 2)
+        y_ref[two, :, :24, :] = weight_grad(2 * other + q, zs).reshape(2, 8, 24, OWN)
+        z_ref[two, :, :24, :] = out_grad(other, q).reshape(2, 8, 24, OWN)
+
+    swap_z = remote(rows24(y_ref), rz, 88, core_peer)
+    swap_o = remote(rows24(z_ref), ro, 89, core_peer)
+    swap_z.start()
+    swap_o.start()
+
+    @pl.loop(0, 2)
+    def _(q):
+        two = pl.ds(2 * q, 2)
+        dm_ref[two, :, :24, :] = weight_grad(2 * place.c + q, zs).reshape(2, 8, 24, OWN)
+        own_o[two] = out_grad(place.c, q).reshape(2, 8, 24, OWN)
+
+    me_big = place.big
+    g2z, g2o, g2x = [], [], []
+    for k in range(1, 8):
+        them, peer = place.big_of(k), bigs[k - 1]
+        g2z.append(remote(dm_ref.at[:, them, pl.ds(0, 24), :], gz.at[me_big], 92 + k, peer))
+        g2x.append(remote(big_b.at[:, them, pl.ds(0, 24), :], gx.at[me_big], 108 + k, peer))
+        for q in range(2):
+            rows = own_o.at[2 * q + them // 4, pl.ds(2 * lax.rem(them, 4), 2)]
+            g2o.append(remote(rows, gro.at[me_big, q], (100 if q else 148) + k, peer))
+
     state[...] = jnp.zeros_like(state)
     halo[...] = jnp.zeros_like(halo)
 
     @pl.loop(0, BLOCKS)
     def _(i):
         b = BLOCKS - 1 - i
-        conv, raw, core, dcore = cvo_ref[b], raw_ref[b], core_ref[b], dcore_ref[b]
+
+        @pl.when(i == 2)
+        def _():
+            swap_z.wait_recv()
+            swap_o.wait_recv()
+            for r in range(4):
+                dm_ref[r, :, :24, :] += rz[r]
+                own_o[r] += ro[r]
+            for copy in g2z + g2o:
+                copy.start()
+            gz[me_big] = dm_ref[:, me_big, :24, :]
+            for q in range(2):
+                gro[me_big, q] = own_o[
+                    2 * q + me_big // 4, pl.ds(2 * lax.rem(me_big, 4), 2)
+                ]
+
+        conv = block_of(big_b, b, 640)
+        raw, core, dcore = raw_ref[b], core_ref[b], dcore_ref[b]
         sig = jax.nn.sigmoid(conv)
         act = conv * sig
         x, keys, query = act[:, :OWN], act[:, OWN : OWN + NS], act[:, OWN + NS :]
-        shifted = raw + hd_ref[0:1, :]
+        shifted = raw + hd_ref[0:1, :128]
         dt = softplus(shifted)
-        rate = jnp.exp(hd_ref[1:2, :])
+        rate = jnp.exp(hd_ref[1:2, :128])
         log_decay = -rate * dt
         dskip_ref[0:1, :] += jnp.sum(dcore * x, axis=0, keepdims=True)
         cumulative, turned, wide = decay_parts(log_decay)
@@ -676,12 +673,12 @@
         draw = ddt * jax.nn.sigmoid(shifted)
         dhead_ref[0:1, :] += jnp.sum(draw, axis=0, keepdims=True)
         dhead_ref[1:2, :] += jnp.sum(dlog * log_decay, axis=0, keepdims=True)
-        dx = dscaled * dt_wide + sk_ref[0:1, :] * dcore
+        dx = dscaled * dt_wide + skip * dcore
         dact = jnp.concatenate([dx, dkeys, dquery], axis=1)
         dconv = dact * (sig * (1.0 + conv * (1.0 - sig)))
         extended = jnp.concatenate([dconv, halo[...]], axis=0)
         halo[...] = dconv[:8, :]
-        xbc = xbc_ref[b]
+        xbc = block_of(big_a, b, 640)
         dxbc = jnp.zeros_like(xbc)
         for k in range(KCONV):
             moved = extended[3 - k : 3 - k + BLOCK, :]
@@ -692,6 +689,54 @@
         draw_own = jnp.where(lane < 6, draw, 0.0)
         dp_ref[b, :, 1024:] = pltpu.roll(draw_own, 6 * me, 1).astype(bf16)
 
+    @pl.loop(0, 2)
+    def _(q):
+        two = pl.ds(2 * q, 2)
+        big_a[two, :, :24, :] = weight_grad(2 * other + q, late).reshape(2, 8, 24, 768)
+
+    swap_x = remote(rows24(big_a), rx, 90, core_peer)
+    swap_x.start()
+
+    @pl.loop(0, 2)
+    def _(q):
+        two = pl.ds(2 * q, 2)
+        big_b[two, :, :24, :] = weight_grad(2 * place.c + q, late).reshape(2, 8, 24, 768)
+
+    def in_copy(b):
+        return remote(ct_ref.at[b], gi_ref.at[me], 116 + b, (place.d, b), 124 + me)
+
+    @pl.loop(0, BLOCKS)
+    def _(i):
+        b = lax.rem(me + 1 + i, BLOCKS)
+        part = dot(dp_ref[b], w_ref[...].reshape(D, COLS), 1, 1)
+
+        @pl.when(i < BLOCKS - 1)
+        def _():
+            ct_ref[b] = part.astype(bf16)
+            in_copy(b).start()
+
+        @pl.when(i == BLOCKS - 1)
+        def _():
+            own_dn[...] = part
+
+    swap_x.wait_recv()
+    for r in range(4):
+        big_b[r, :, :24, :] += rx[r]
+    for copy in g2x:
+        copy.start()
+    gx[me_big] = big_b[:, me_big, :24, :]
+
+    for copy in g2z + g2o:
+        copy.wait_recv()
+    total = gz[0]
+    total_o = gro[0]
+    for j in range(1, 8):
+        total += gz[j]
+        total_o += gro[j]
+    piece[:, :, :OWN] = total
+    for q in range(2):
+        piece_o_ref[:, 384 * q : 384 * q + 384] = total_o[q].reshape(48, 384).astype(bf16)
+
     locals_[3].wait()
     own_out[...] += hid_v[...].astype(f32)
 
@@ -703,8 +748,78 @@
 
     out_ref[...] = own_out[...].astype(bf16)
 
-    for copy in smalls + hids + cots + sums + w_x + [w_core]:
+    for copy in g2x:
+        copy.wait_recv()
+    total = gx[0]
+    for j in range(1, 8):
+        total += gx[j]
+    piece[:, :, OWN:] = total
+    owners = []
+    for k in range(1, 8):
+        them = place.shard_of(k)
+        copy = remote(piece.at[lax.rem(them, 4)], ow.at[me], 132 + k, place.shard_peer(k))
+        goes = them // 4 == place.c
+        pl.when(goes)(copy.start)
+        owners.append((copy, goes))
+
+    @pl.when(mine)
+    def _():
+        ow[me] = piece[place.z]
+
+    @pl.loop(1, BLOCKS)
+    def _(k):
+        j = lax.rem(me + k, BLOCKS)
+        remote(ct_ref.at[j], gi_ref.at[j], 116 + j, (place.d, j), 124 + j).wait_recv()
+        own_dn[...] += gi_ref[j].astype(f32)
+
+    locals_[4].wait()
+    u = hid_v[...].astype(f32)
+    scale = lax.rsqrt(jnp.mean(u * u, axis=1, keepdims=True) + epsilon)
+    d_normed = own_dn[...]
+    gained = gain_ref[:, :D] * d_normed
+    unit = u * scale
+    grad = scale * gained - unit * (scale * scale * jnp.mean(u * gained, axis=1, keepdims=True))
+    igrad_ref[...] = (cot_v[...].astype(f32) + grad).astype(bf16)
+
+    sg[...] = jnp.zeros_like(sg)
+    sg[0:1, :] = jnp.sum(d_normed * unit, axis=0, keepdims=True)
+    sg[1:6, :640] = dconv_ref[0:5, :]
+    sg[1:2, 640:1024] = dgain_ref[0:1, :]
+    sg[2:3, 640:1024] = dskip_ref[0:1, :]
+    sg[3:5, 640:768] = dhead_ref[0:2, :]
+    sgs = [remote(sg, sg_all.at[me], 140 + k, place.shard_peer(k)) for k in range(1, 8)]
+    for copy in sgs:
+        copy.start()
+    sg_all[me] = sg[...]
+
+    for k in range(1, 8):
+        @pl.when(mine)
+        def _(k=k):
+            owners[k - 1][0].wait_recv()
+
+    @pl.when(mine)
+    def _():
+        common = ow[0, :, 2 * OWN :]
+        for j in range(1, 8):
+            common += ow[j, :, 2 * OWN :]
+        for j in range(8):
+            slab_ref[:, OWN * j : OWN * (j + 1)] = ow[j, :, :OWN].astype(bf16)
+            slab_ref[:, DI + OWN * j : DI + OWN * (j + 1)] = ow[j, :, OWN : 2 * OWN].astype(bf16)
+        slab_ref[:, 2 * DI :] = common.astype(bf16)
+
+    @pl.when(jnp.logical_not(mine))
+    def _():
+        slab_ref[...] = jnp.zeros_like(slab_ref)
+
+    for copy in sgs:
+        copy.wait_recv()
+
+    for copy in smalls + hids + cots + sums + w_x + [w_core, swap_z, swap_o, swap_x]:
         copy.wait_send()
+    for copy in g2z + g2o + g2x + sgs:
+        copy.wait_send()
+    for copy, goes in owners:
+        pl.when(goes)(copy.wait_send)
 
     @pl.when(mine)
     def _():
@@ -714,42 +829,53 @@
 
     @pl.loop(1, BLOCKS)
     def _(k):
-        out_copy(lax.rem(me + k, BLOCKS)).wait_send()
+        b = lax.rem(me + k, BLOCKS)
+        out_copy(b).wait_send()
+        in_copy(b).wait_send()
 
 
 def sds(shape, dtype=f32):
     return jax.ShapeDtypeStruct(shape, dtype)
 
 
-def run_whole(hid, cot, wide, small, wo, hd, sk):
+def run_whole(hid, cot, in_master, out_master, small, hd):
     any_spec = pl.BlockSpec(memory_space=pl.ANY)
     vmem = pl.BlockSpec(memory_space=pltpu.VMEM)
 
     def v(*shape, dtype=f32):
         return pltpu.VMEM(shape, dtype)
 
+    tokens = (8, BLOCK, D)
+    part = (8, BLOCK, OWN)
+    split = (4, 8, 32, OWN)
     return pl.pallas_call(
         whole_kernel,
-        in_specs=[any_spec] * 4 + [vmem] * 3,
-        out_specs=tuple([vmem] * 11),
+        in_specs=[any_spec] * 5 + [vmem],
+        out_specs=tuple([vmem] * 5),
         out_shape=(
-            sds((BLOCK, D), bf16), sds((8, BLOCK, D), bf16), sds((8, BLOCK, D), bf16),
-            sds((8, 192, COLS), bf16), sds((8, BLOCK, COLS), bf16), sds((8, BLOCK, OWN), bf16),
-            sds((1, D)), sds((8, OWN)), sds((8, OWN)), sds((8, 640)), sds((8, 128)),
+            sds((BLOCK, D), bf16), sds((BLOCK, D), bf16), sds((24, WIDE), bf16),
+            sds((48, 768), bf16), sds((8, 8, D)),
         ),
         scratch_shapes=[
-            v(8, 8, 640), v(1, 4608), v(8, CONVC), v(8, BLOCK, OWN), v(8, BLOCK, 640),
-            v(8, BLOCK, 640), v(8, BLOCK, 128), v(8, BLOCK, OWN), v(8, BLOCK, OWN),
-            v(8, BLOCK, OWN), v(8, NS, OWN), v(16, 128), v(8, 16, 128), v(BLOCK, 128),
-            v(8, BLOCK, OWN), v(8, BLOCK, D, dtype=bf16), v(8, BLOCK, D, dtype=bf16),
-            v(BLOCK, D), v(NS, OWN), v(8, 640), v(BLOCK, D, dtype=bf16),
-            pltpu.SemaphoreType.DMA((88,)), pltpu.SemaphoreType.DMA((88,)),
-            pltpu.SemaphoreType.DMA((7,)),
+            v(*tokens, dtype=bf16), v(*tokens, dtype=bf16), v(8, 192, COLS, dtype=bf16), v(*split),
+            v(4, 8, 32, 768), v(4, 8, 32, 768), v(8, BLOCK, 128), v(*part), v(*split), v(*split),
+            v(8, NS, OWN), v(*part),
+            v(8, BLOCK, COLS, dtype=bf16), v(*part, dtype=bf16), v(*tokens, dtype=bf16),
+            v(*tokens, dtype=bf16), v(BLOCK, D), v(6, BLOCK, 768), v(48, PROJ),
+            v(48, WIDE, dtype=bf16),
+            v(OWN, D, dtype=bf16), v(8, 8, 640), v(1, 4608), v(8, CONVC),
+            v(16, 128), v(8, 16, 128), v(BLOCK, 128), v(4, 8, 24, OWN), v(4, 8, 24, OWN),
+            v(4, 8, 24, OWN), v(8, 4, 24, OWN), v(8, 2, 2, 24, OWN), v(4, 8, 24, 768),
+            v(8, 4, 24, 768), v(*tokens, dtype=bf16),
+            v(BLOCK, D), v(4, 24, COLS), v(8, 24, COLS), v(8, D), v(8, OWN), v(8, OWN), v(8, 640),
+            v(8, 128), v(NS, OWN), v(8, 640), v(BLOCK, D, dtype=bf16), v(BLOCK, D, dtype=bf16),
+            pltpu.SemaphoreType.DMA((156,)), pltpu.SemaphoreType.DMA((156,)),
+            pltpu.SemaphoreType.DMA((15,)),
         ],
         compiler_params=pltpu.CompilerParams(
-            collective_id=1, has_side_effects=True, vmem_limit_bytes=VMEM_LIMIT
+            collective_id=1, has_side_effects=True, vmem_limit_bytes=62 * 2**20
         ),
-    )(hid, cot, wide, small, wo, hd, sk)
+    )(hid, cot, in_master, out_master, small, hd)
 
 
 def adam_update(master, first, second, gradient, rate, decay):
@@ -769,10 +895,7 @@
     head_master, head_first, head_second,
 ):
     s = lax.axis_index("shard")
-    c = lax.rem(lax.axis_index("dp"), 2)
     low = lambda v: lax.reduce_precision(v, 8, 7)
-    wide = jnp.pad(in_master.astype(bf16), ((0, 0), (0, WIDE - PROJ)))
-    wo = out_master.astype(bf16)
     small = jnp.concatenate(
         [
             jnp.pad(low(conv_master), ((0, 0), (0, 224))),
@@ -782,83 +905,38 @@
         axis=0,
     )
     heads = low(head_master)
-    hd = jnp.pad(heads, ((0, 5), (0, 122)))
-    sk = jnp.repeat(heads[2], HD)[None]
-    layer_out, normed, ct, w, dproj, mixed, gn, dgain, dskip, dconv, dhead = run_whole(
-        hidden[0], cotangent[0], wide, small, wo, hd, sk
-    )
-    normed, ct, w = normed.reshape(LEN, D), ct.reshape(LEN, D), w.reshape(D, COLS)
-    dproj, mixed = dproj.reshape(LEN, COLS), mixed.reshape(LEN, OWN)
-    dgain, dskip, dconv, dhead = dgain[0], dskip[0], dconv[:5], dhead[:2, :6]
-    grad_o = dot(mixed, ct, 0, 0)
-    grad_w = dot(normed, dproj, 0, 0)
-    part_in = dot(dproj, w, 1, 1).astype(bf16).reshape(8, BLOCK, D)
-    (got_in,) = exchange(3, scatter_body, (part_in,), (sds((8, BLOCK, D), bf16),), 7, 1)
-    inputs = hidden[0].astype(f32)
-    d_normed = jnp.sum(got_in.astype(f32), axis=0)
-    scale = lax.rsqrt(jnp.mean(inputs * inputs, axis=-1, keepdims=True) + epsilon)
-    gained = gn * d_normed
-    grad_inputs = scale * gained - inputs * scale**3 * jnp.mean(
-        inputs * gained, axis=-1, keepdims=True
-    )
-    input_grad = (cotangent[0].astype(f32) + grad_inputs).astype(bf16)
-    dnorm = jnp.sum(d_normed * inputs * scale, axis=0)
-    small_grad = jnp.concatenate(
+    hd = jnp.concatenate(
         [
-            dnorm, dgain, dconv[:, :OWN].reshape(-1), dconv[:, OWN:].reshape(-1),
-            dhead.reshape(-1), jnp.sum(dskip.reshape(6, HD), axis=1), jnp.zeros((1006,), f32),
-        ]
-    ).reshape(48, 128)
-
-    grad_w = grad_w.reshape(8, 8, 24, COLS)
-    grad_o = grad_o.reshape(8, 48, D)
-    swap_w, swap_o = exchange(
-        4, swap_body, (grad_w, grad_o), (sds((4, 8, 24, COLS), f32), sds((8, 48, 768), f32)), 2, 0
-    )
-    half_w = (
-        lax.dynamic_slice_in_dim(grad_w, 4 * c, 4, 0).astype(f32) + swap_w.astype(f32)
-    ).astype(bf16)
-    half_o = (
-        lax.dynamic_slice_in_dim(grad_o, 768 * c, 768, 2).astype(f32) + swap_o.astype(f32)
-    ).astype(bf16)
-    got_w, got_o = exchange(
-        5, reduce_body, (half_w, half_o),
-        (sds((8, 4, 24, COLS), bf16), sds((8, 48, 768), bf16)), 14, 2,
-    )
-    piece_w = jnp.sum(got_w.astype(f32), axis=0)
-    piece_o = jnp.sum(got_o.astype(f32), axis=0)
-    own_w, small_all = exchange(
-        6, owner_body, (piece_w, small_grad), (sds((8, 24, COLS)), sds((8, 48, 128))), 14, 2
-    )
-    own_w = own_w.transpose(1, 0, 2)
-    slab = jnp.concatenate(
+            jnp.pad(heads, ((0, 0), (0, OWN - 6))),
+            jnp.repeat(heads[2], HD)[None],
+            jnp.zeros((4, OWN), f32),
+        ],
+        axis=0,
+    )
+    layer_out, input_grad, slab, piece_o, sg = run_whole(
+        hidden[0], cotangent[0], in_master, out_master, small, hd
+    )
+    g_gain = jnp.concatenate([jnp.sum(sg[:, 0], axis=0), sg[:, 1, 640:1024].reshape(-1)])
+    g_conv = jnp.concatenate(
         [
-            own_w[:, :, :OWN].reshape(24, DI),
-            own_w[:, :, OWN : 2 * OWN].reshape(24, DI),
-            jnp.sum(own_w[:, :, 2 * OWN :], axis=1),
+            sg[:, 1:6, :OWN].transpose(1, 0, 2).reshape(5, DI),
+            jnp.sum(sg[:, 1:6, OWN:640], axis=0),
         ],
         axis=1,
     )
-    flat = small_all.reshape(8, 6144)
-    g_gain = jnp.concatenate([jnp.sum(flat[:, :D], axis=0), flat[:, D : D + OWN].reshape(-1)])
-    g_conv = jnp.concatenate(
-        [
-            flat[:, 1920:3840].reshape(8, 5, OWN).transpose(1, 0, 2).reshape(5, DI),
-            jnp.sum(flat[:, 3840:5120], axis=0).reshape(5, 256),
-        ],
-        axis=1,
-    )
+    mine = lax.dynamic_index_in_dim(sg, s, 0, keepdims=False)
     own_small = jnp.concatenate(
         [
             lax.dynamic_slice(g_gain, (576 * s,), (576,)),
             lax.dynamic_slice(g_conv, (0, 416 * s), (5, 416)).reshape(-1),
-            lax.dynamic_slice(flat, (s, 5120), (1, 18))[0],
+            mine[3, 640:646], mine[4, 640:646],
+            jnp.sum(mine[2, 640:1024].reshape(6, HD), axis=1),
             jnp.zeros((398,), f32),
         ]
     ).reshape(24, 128)
     total_w, total_o, total_small = exchange(
         7, spread_body, (slab, piece_o, own_small),
-        (sds((8, 24, WIDE)), sds((8, 48, D)), sds((16, 24, 128))), 45, 3,
+        (sds((8, 24, WIDE), bf16), sds((8, 48, D), bf16), sds((16, 24, 128))), 45, 3,
     )
     total_small = jnp.sum(total_small, axis=0).reshape(-1)
     totals = (

time: 384 us -> 315 us (0.82)
  matrix products: 23.4 us -> 0 us
  other arithmetic: 43.6 us -> 24.5 us
  Pallas kernels: 302 us -> 283 us
  local copies, waits for them, and re-layouts: 13.3 us -> 6.83 us
    pallas_call x5 -> x1, Pallas kernels: 157 us -> 39.8 us  [exchange(): pl.pallas_call(kernel, out_shape=outs, in_specs=[any_spec] * len(ins), ou...]
    pallas_call x1, Pallas kernels: 145 us -> 243 us  [run_whole(): pl.pallas_call(whole_kernel, in_specs=[any_spec] * 5 + [vmem], out_specs=...]
    dot_general x3 -> x0, matrix products: 23.4 us -> none  [dot(): lax.dot_general(a, b, (((ca,), (cb,)), ((), ())), precision=precision, pr...]
    convert_element_type x5 -> x0, other arithmetic: 12.8 us -> none  [the longest x1 4.7 us: on_device(): half_w = (lax.dynamic_slice_in_dim(grad_w, 4 * c, 4, 0).astype(f32) + swa...]
    dot_general x2 -> x0, local copies, waits for them, and re-layouts: 5.8 us -> none  [dot(): lax.dot_general(a, b, (((ca,), (cb,)), ((), ())), precision=precision, pr...]
    reduce_sum x8 -> x3, other arithmetic: 6.94 us -> 2.01 us  [the longest x1 1.03 us: on_device(): jnp.sum(sg[:, 0], axis=0)]
where the time goes in v3:
time: 315 us
  Pallas kernels  283 us (90%)
  other arithmetic  24.5 us (8%)
  local copies, waits for them, and re-layouts  6.83 us (2%)
    pallas_call x1, Pallas kernels, run_whole(): pl.pallas_call(whole_kernel, in_specs=[any_spec] * 5 + [vmem], out_specs=...  243 us
    pallas_call x1, Pallas kernels, exchange(): pl.pallas_call(kernel, out_shape=outs, in_specs=[any_spec] * len(ins), ou...  39.8 us
    sub x5, other arithmetic, adam_update(): return (first_new, second_new, master - rate * (scaled + decay * master))  18.9 us

profile of v3, /device:TPU:1, one launch (start us, length us, event | category | flops | bytes accessed | tf_op | source)
XLA Modules:
  0.0 315.0 jit_solution(7502236975557397680)
XLA Ops:
  0.7 0.7 reduce_precision.9
  1.4 0.7 reduce_precision.10
  2.1 0.1 pad.24.clone
  2.2 0.7 fusion.4.small
  2.8 0.7 reduce_precision.11
  3.5 0.1 broadcast_in_dim.23
  3.6 0.1 broadcast_in_dim_reshape.3
  3.7 0.1 pad.21.clone
  3.8 0.7 fusion.7.hd_ref
  4.4 242.9 %shard_map.296 = (bf16[128,1536]{1,0:T(8,128)(2,1)}, bf16[128,1536]{1,0:T(8,128)(2,1)}, bf16[24,6528]{1,0:T(8,128)(2,1)}, bf16[48,768]{1,0:T(8,128)(2,1)}, f32[8,8,1536]{2,1,0:T(8,128)}) custom-call(bf16[128,1536]{1,0:T(8,128)(2,1)} %bitcast.26, bf16[128,1536]{1,0:T(8,128)(2,1)} %bitcast.27, f32[192,6448]{1,0:T(8,128)} %in_ref.1, f32[384,1536]{1,0:T(8,128)} %out_w.1, ...), custom_call_target="tpu_custom_call" | custom-call | tf_op jit(solution)/shard_map/pallas_call | solution.py:851
  247.4 1.0 slice_reduce_fusion.1
  248.4 0.9 slice.38
  249.3 0.1 fusion.9
  249.4 0.9 slice.39
  250.3 0.9 slice_reduce_fusion
  251.2 0.1 fusion.6
  251.2 0.1 reshape.59
  251.3 0.8 dynamic-slice_bitcast_fusion
  252.2 0.1 reshape_squeeze.7
  252.2 0.1 reduce_sum.38
  252.4 0.7 concatenate.19
  253.0 39.8 %shard_map.297 = (bf16[8,24,6528]{2,1,0:T(8,128)(2,1)}, bf16[8,48,1536]{2,1,0:T(8,128)(2,1)}, f32[16,24,128]{2,1,0:T(8,128)}) custom-call(bf16[24,6528]{1,0:T(8,128)(2,1)} %get-tuple-element.27.refs_0_, bf16[48,768]{1,0:T(8,128)(2,1)} %get-tuple-element.28.refs_1_, f32[24,128]{1,0:T(8,128)} %bitcast.34), custom_call_target="tpu_custom_call" | custom-call | tf_op jit(solution)/shard_map/pallas_call | solution.py:101
  292.9 0.0 copy-start
  292.9 0.0 copy-start.1
  292.9 0.0 copy-start.2
  292.9 0.0 copy-start.3
  292.9 12.7 %multiply_subtract_fusion = (f32[192,6448]{1,0:T(8,128)}, f32[192,6448]{1,0:T(8,128)}, f32[192,6448]{1,0:T(8,128)}) fusion(f32[192,6448]{1,0:T(8,128)} %in_ref.1, bf16[192,6528]{1,0:T(8,128)(2,1)} %bitcast.25, f32[192,6448]{1,0:T(8,128)} %param.21, f32[192,6448]{1,0:T(8,128)} %param.20), kind=kLoop, calls=%fused_computation.4 | loop fusion | flops 19808256 | bytes 32188416 | tf_op jit(solution)/shard_map/sub | solution.py:889
  305.6 0.6 copy-done.2
  306.2 0.5 copy-done.3
  306.8 0.0 copy-start.7
  306.8 0.0 copy-start.8
  306.8 0.0 copy-start.9
  306.8 0.0 copy-start.11
  306.8 0.0 copy-start.14
  306.8 0.0 copy-start.15
  306.8 0.0 copy-start.5
  306.8 0.0 copy-start.4
  306.8 4.4 %multiply_subtract_fusion.1 = (f32[384,1536]{1,0:T(8,128)}, f32[384,1536]{1,0:T(8,128)}, f32[384,1536]{1,0:T(8,128)}) fusion(f32[384,1536]{1,0:T(8,128)S(1)} %copy-done, bf16[8,48,1536]{2,1,0:T(8,128)(2,1)S(1)} %copy-done.3, f32[384,1536]{1,0:T(8,128)S(1)} %copy-done.1, f32[384,1536]{1,0:T(8,128)S(1)} %copy-done.2), kind=kLoop, calls=%fused_computation.10 | loop fusion | flops 9437184 | bytes 15335424 | tf_op jit(solution)/shard_map/sub | solution.py:889
  311.2 0.0 copy-done.6
  311.3 0.6 multiply_subtract_fusion.3
  311.9 0.1 slice.53
  312.0 0.1 reshape.63
  312.1 0.6 multiply_subtract_fusion.2
  312.7 0.1 slice.54
  312.8 0.1 reshape.64
  312.9 0.6 multiply_subtract_fusion.4
  313.5 0.7 copy.36
  314.2 0.7 copy.37
  (26 shorter events, 0.1 us)
Async XLA Ops:
  292.9 12.7 %copy-start = (f32[384,1536]{1,0:T(8,128)S(1)}, f32[384,1536]{1,0:T(8,128)}, u32[]{:S(2)}) copy-start(f32[384,1536]{1,0:T(8,128)} %out_w.1) | copy-start | bytes 7077892
  292.9 12.7 %copy-start.1 = (f32[384,1536]{1,0:T(8,128)S(1)}, f32[384,1536]{1,0:T(8,128)}, u32[]{:S(2)}) copy-start(f32[384,1536]{1,0:T(8,128)} %param.24) | copy-start | bytes 7077892
  292.9 13.3 %copy-start.2 = (f32[384,1536]{1,0:T(8,128)S(1)}, f32[384,1536]{1,0:T(8,128)}, u32[]{:S(2)}) copy-start(f32[384,1536]{1,0:T(8,128)} %param.23) | copy-start | bytes 7077892
  292.9 13.8 %copy-start.3 = (bf16[8,48,1536]{2,1,0:T(8,128)(2,1)S(1)}, bf16[8,48,1536]{2,1,0:T(8,128)(2,1)}, u32[]{:S(2)}) copy-start(bf16[8,48,1536]{2,1,0:T(8,128)(2,1)} %get-tuple-element.31) | copy-start | bytes 3538948
  306.7 4.5 %copy-start.6 = (f32[16,24,128]{2,1,0:T(8,128)S(1)}, f32[16,24,128]{2,1,0:T(8,128)}, u32[]{:S(2)}) copy-start(f32[16,24,128]{2,1,0:T(8,128)} %get-tuple-element.32) | copy-start | bytes 589828
  306.7 4.5 %copy-start.10 = (f32[576]{0:T(1024)S(1)}, f32[576]{0:T(1024)}, u32[]{:S(2)}) copy-start(f32[576]{0:T(1024)} %param.25) | copy-start | bytes 6916
  306.8 4.5 %copy-start.12 = (f32[576]{0:T(1024)S(1)}, f32[576]{0:T(1024)}, u32[]{:S(2)}) copy-start(f32[576]{0:T(1024)} %param.27) | copy-start | bytes 6916
  306.8 4.5 %copy-start.13 = (f32[576]{0:T(1024)S(1)}, f32[576]{0:T(1024)}, u32[]{:S(2)}) copy-start(f32[576]{0:T(1024)} %param.26) | copy-start | bytes 6916
  306.8 5.3 %copy-start.7 = (f32[5,416]{1,0:T(8,128)S(1)}, f32[5,416]{1,0:T(8,128)}, u32[]{:S(2)}) copy-start(f32[5,416]{1,0:T(8,128)} %param.28) | copy-start | bytes 24964
  306.8 5.3 %copy-start.8 = (f32[5,416]{1,0:T(8,128)S(1)}, f32[5,416]{1,0:T(8,128)}, u32[]{:S(2)}) copy-start(f32[5,416]{1,0:T(8,128)} %param.30) | copy-start | bytes 24964
  306.8 5.3 %copy-start.9 = (f32[5,416]{1,0:T(8,128)S(1)}, f32[5,416]{1,0:T(8,128)}, u32[]{:S(2)}) copy-start(f32[5,416]{1,0:T(8,128)} %param.29) | copy-start | bytes 24964
  306.8 6.1 %copy-start.11 = (f32[3,6]{1,0:T(4,128)S(1)}, f32[3,6]{1,0:T(4,128)}, u32[]{:S(2)}) copy-start(f32[3,6]{1,0:T(4,128)} %param.31) | copy-start | bytes 220
  306.8 6.1 %copy-start.14 = (f32[3,6]{1,0:T(4,128)S(1)}, f32[3,6]{1,0:T(4,128)}, u32[]{:S(2)}) copy-start(f32[3,6]{1,0:T(4,128)} %param.33) | copy-start | bytes 220
  306.8 6.0 %copy-start.15 = (f32[3,6]{1,0:T(4,128)S(1)}, f32[3,6]{1,0:T(4,128)}, u32[]{:S(2)}) copy-start(f32[3,6]{1,0:T(4,128)} %param.32) | copy-start | bytes 220
  306.8 6.6 %copy-start.5 = (bf16[128,1536]{1,0:T(8,128)(2,1)S(1)}, bf16[128,1536]{1,0:T(8,128)(2,1)}, u32[]{:S(2)}) copy-start(bf16[128,1536]{1,0:T(8,128)(2,1)} %get-tuple-element.25) | copy-start | bytes 1179652
  306.8 7.4 %copy-start.4 = (bf16[128,1536]{1,0:T(8,128)(2,1)S(1)}, bf16[128,1536]{1,0:T(8,128)(2,1)}, u32[]{:S(2)}) copy-start(bf16[128,1536]{1,0:T(8,128)(2,1)} %get-tuple-element.26) | copy-start | bytes 1179652

commit v4 on v3

--- a/solution.py
+++ b/solution.py
@@ -58,6 +58,12 @@
 
     def big_peer(self, k):
         return (self.big_of(k) * 2 + self.c, self.s)
+
+    def z_peer(self, k):
+        return (self.d, self.yl * 4 + lax.rem(self.z + k, 4))
+
+    def y_partner(self):
+        return (self.d, (1 - self.yl) * 4 + self.z)
 
     def core_peer(self):
         return (self.big * 2 + 1 - self.c, self.s)
@@ -198,6 +204,190 @@
             copy.wait_recv()
 
 
+class Gather:
+    def __init__(self, place, remote, src, buf, base):
+        def at(dy, dz, lo, hi):
+            index = lax.rem(place.yl + dy, 2) * 4 + lax.rem(place.z + dz, 4)
+            return buf.at[index, pl.ds(lo, hi - lo)]
+
+        def onward(view, index, peer):
+            return remote(view, view, base + index, peer)
+
+        up, down, over = place.z_peer(1), place.z_peer(3), place.y_partner()
+        self.copies = [
+            remote(src, buf.at[place.s], base, up),
+            remote(src, buf.at[place.s], base + 1, down),
+            remote(src, buf.at[place.s], base + 2, over),
+            onward(at(0, 3, 0, 64), 3, up),
+            onward(at(0, 1, 64, 128), 4, down),
+            onward(at(0, 3, 64, 128), 5, over),
+            onward(at(0, 1, 64, 128), 6, over),
+            onward(at(0, 2, 64, 128), 7, over),
+            onward(at(1, 0, 0, 64), 8, up),
+            onward(at(1, 0, 0, 64), 9, down),
+            onward(at(1, 3, 0, 32), 10, up),
+            onward(at(1, 1, 32, 64), 11, down),
+        ]
+
+    def after(self, arrived, *indices):
+        self.copies[arrived].wait_recv()
+        for index in indices:
+            self.copies[index].start()
+
+    def begin(self):
+        for copy in (self.copies[2], self.copies[0], self.copies[1]):
+            copy.start()
+
+    def first(self):
+        self.after(2, 8, 9)
+        self.after(0, 3, 5)
+        self.after(1, 4, 6)
+
+    def second(self):
+        self.after(8, 10)
+        self.after(9, 11)
+        self.after(4, 7)
+
+    def last(self):
+        for index in (3, 5, 6, 7, 10, 11):
+            self.copies[index].wait_recv()
+
+    def sent(self):
+        for copy in self.copies:
+            copy.wait_send()
+
+
+class Scatter:
+    def __init__(self, place, remote, part, ra, rb, ra2, rb2, total, base):
+        self.place, self.remote, self.base = place, remote, base
+        self.part, self.ra, self.rb, self.ra2, self.rb2, self.total = part, ra, rb, ra2, rb2, total
+        self.top, self.low = pl.ds(0, 64), pl.ds(64, 64)
+
+    def along_z(self, b, source):
+        place = self.place
+        return self.remote(
+            self.part.at[b, self.top],
+            self.ra.at[place.z, b // 4],
+            self.base + b,
+            (place.d, place.yl * 4 + lax.rem(b, 4)),
+            self.base + source * 2 + b // 4,
+        )
+
+    def along_y(self, b):
+        z = lax.rem(b, 4)
+        return self.remote(
+            self.part.at[b, self.low], self.rb.at[z], self.base + 8 + z, self.place.y_partner()
+        )
+
+    def send(self, b):
+        pl.when(lax.rem(b, 4) != self.place.z)(self.along_z(b, self.place.z).start)
+        pl.when(b // 4 != self.place.yl)(self.along_y(b).start)
+
+    def other(self):
+        return (1 - self.place.yl) * 4 + self.place.z
+
+    def over(self):
+        return self.remote(
+            self.part.at[self.other(), self.top], self.ra2, self.base + 12, self.place.y_partner()
+        )
+
+    def back(self, z):
+        place = self.place
+        return self.remote(
+            self.part.at[place.yl * 4 + z, self.low],
+            self.rb2.at[place.z],
+            self.base + 13 + z,
+            (place.d, place.yl * 4 + z),
+            self.base + 13 + place.z,
+        )
+
+    def others(self):
+        return [lax.rem(self.place.z + k, 4) for k in (1, 2, 3)]
+
+    def middle(self):
+        place, part = self.place, self.part
+        for z in self.others():
+            for y in range(2):
+                self.along_z(y * 4 + z, z).wait_recv()
+
+        def sum_z(block, y):
+            total = part[block, :64].astype(f32)
+            for z in self.others():
+                total += self.ra[z, y].astype(f32)
+            return total
+
+        part[self.other(), :64] = sum_z(self.other(), 1 - place.yl).astype(bf16)
+        self.over().start()
+        self.total[:64] = sum_z(place.s, place.yl)
+        for z in range(4):
+            self.along_y((1 - place.yl) * 4 + z).wait_recv()
+        for z in self.others():
+            block = place.yl * 4 + z
+            part[block, 64:] = (part[block, 64:].astype(f32) + self.rb[z].astype(f32)).astype(bf16)
+            self.back(z).start()
+        self.total[64:] = part[place.s, 64:].astype(f32) + self.rb[place.z].astype(f32)
+
+    def last(self):
+        self.over().wait_recv()
+        self.total[:64] += self.ra2[...].astype(f32)
+        for z in self.others():
+            self.remote(
+                self.part.at[self.place.yl * 4 + z, self.low], self.rb2.at[z],
+                self.base + 13 + z, (self.place.d, self.place.yl * 4 + z),
+            ).wait_recv()
+            self.total[64:] += self.rb2[z].astype(f32)
+
+    def sent(self):
+        place = self.place
+        for z in self.others():
+            for y in range(2):
+                self.along_z(y * 4 + z, place.z).wait_send()
+            self.back(z).wait_send()
+        for z in range(4):
+            self.along_y((1 - place.yl) * 4 + z).wait_send()
+        self.over().wait_send()
+
+
+class Reduce:
+    def __init__(self, place, remote, view, read, write, gx, gy, base):
+        self.place, self.view, self.read, self.write, self.gx, self.gy = place, view, read, write, gx, gy
+        self.along = [
+            remote(
+                view(y * 4 + lax.rem(place.x + k, 4)), gx.at[k - 1, y], base + 2 * k + y,
+                place.big_peer(k),
+            )
+            for k in (1, 2, 3)
+            for y in range(2)
+        ]
+        self.other = (1 - place.yh) * 4 + place.x
+        self.over = remote(view(self.other), gy, base + 8, place.big_peer(4))
+
+    def begin(self):
+        for copy in self.along:
+            copy.start()
+
+    def total(self, big, y):
+        total = self.read(big)
+        for k in range(3):
+            total += self.gx[k, y]
+        return total
+
+    def middle(self):
+        for copy in self.along:
+            copy.wait_recv()
+        self.write(self.other, self.total(self.other, 1 - self.place.yh))
+        self.over.start()
+
+    def last(self):
+        total = self.total(self.place.big, self.place.yh)
+        self.over.wait_recv()
+        return total + self.gy[...]
+
+    def sent(self):
+        for copy in self.along + [self.over]:
+            copy.wait_send()
+
+
 def dot(a, b, ca, cb, precision=None):
     return lax.dot_general(
         a, b, (((ca,), (cb,)), ((), ())), precision=precision, preferred_element_type=f32
@@ -314,8 +504,8 @@
     hid, cot, in_ref, out_w, small, hd_ref,
     out_ref, igrad_ref, slab_ref, piece_o_ref, sg_all,
     n_ref, ct_ref, w_ref, z_ref, big_a, big_b, raw_ref, core_ref, y_ref, dm_ref, st_ref, dcore_ref,
-    dp_ref, mixed_ref, po_ref, go_ref, own_out, wo_f, wq_f, wq, wo_ref, sm_ref, gain_ref, conv_ref,
-    sums_ref, got_sums, turned_sums, rz, ro, own_o, gz, gro, rx, gx, gi_ref, own_dn,
+    dp_ref, mixed_ref, po_ref, ra_ref, rb_ref, ra2_ref, rb2_ref, own_out, wo_f, wq_f, wq, wo_ref, sm_ref, gain_ref, conv_ref,
+    sums_ref, got_sums, turned_sums, rz, ro, own_o, gz, gz2, go, go2, rx, gx, gx2, ia_ref, ib_ref, ia2_ref, ib2_ref, own_dn,
     piece, ow, sg, dgain_ref, dskip_ref, dconv_ref, dhead_ref,
     state, halo, hid_v, cot_v, send, recv, own,
 ):
@@ -383,8 +573,8 @@
         for i, (src, dst) in enumerate(weight_parts(me))
     ]
     smalls = [remote(small, sm_ref.at[me], k, place.shard_peer(k)) for k in range(1, 8)]
-    hids = [remote(hid, n_ref.at[me], 16 + k, place.shard_peer(k)) for k in range(1, 8)]
-    cots = [remote(cot, ct_ref.at[me], 24 + k, place.shard_peer(k)) for k in range(1, 8)]
+    hids = Gather(place, remote, hid, n_ref, 8)
+    cots = Gather(place, remote, cot, ct_ref, 20)
     weights = []
     for k in range(1, 8):
         weights.append(
@@ -404,8 +594,7 @@
 
     for copy in smalls:
         copy.start()
-    for copy in hids:
-        copy.start()
+    hids.begin()
 
     def from_offset(k):
         return lax.rem(place.yl + k // 4, 2)
@@ -421,20 +610,42 @@
         for copy in own_w:
             copy.wait()
 
-    def w_rows(x, c):
-        return w_ref.at[pl.ds(4 * c, 4), pl.ds(pl.multiple_of(48 * x, 16), 48), :]
-
-    w_x = [
-        remote(w_rows(place.x, place.c), w_rows(place.x, place.c), 32 + k, x_peers[k - 1])
-        for k in (1, 2, 3)
+    w_up, w_down = place.big_peer(1), place.big_peer(3)
+
+    def w_quarter(k, lo=0, n=4):
+        rows = pl.ds(pl.multiple_of(48 * lax.rem(place.x + k, 4), 16), 48)
+        return w_ref.at[pl.ds(4 * place.c + lo, n), rows, :]
+
+    def w_on(view, index, peer):
+        return remote(view, view, 32 + index, peer)
+
+    w_copies = [
+        w_on(w_quarter(0), 0, w_up),
+        w_on(w_quarter(0), 1, w_down),
+        w_on(w_quarter(0), 2, core_peer),
+        w_on(w_quarter(3, 0, 2), 3, w_up),
+        w_on(w_quarter(3), 4, core_peer),
+        w_on(w_quarter(1, 2, 2), 5, w_down),
+        w_on(w_quarter(1), 6, core_peer),
+        w_on(w_quarter(2, 0, 2), 7, core_peer),
+        w_on(w_quarter(2, 2, 2), 8, core_peer),
     ]
-    for copy in w_x:
+    for copy in w_copies[:3]:
         copy.start()
-    for copy in w_x:
-        copy.wait_recv()
-    w_half = w_ref.at[pl.ds(4 * place.c, 4)]
-    w_core = remote(w_half, w_half, 36, core_peer)
-    w_core.start()
+
+    def w_after(arrived, *indices):
+        w_copies[arrived].wait_recv()
+        for index in indices:
+            w_copies[index].start()
+
+    locals_[1].wait()
+    hids.first()
+    w_after(0, 3, 4)
+    w_after(1, 5, 6)
+    hids.second()
+    cots.begin()
+    w_after(3, 7)
+    w_after(5, 8)
 
     locals_[0].wait()
     for copy in smalls:
@@ -447,12 +658,10 @@
     def conv_row(k):
         return jnp.concatenate([conv_ref[k : k + 1, cv_at], conv_ref[k : k + 1, DI:]], axis=1)
 
-    locals_[1].wait()
-    for copy in hids:
-        copy.wait_recv()
-    for copy in cots:
-        copy.start()
-    w_core.wait_recv()
+    hids.last()
+    hids.sent()
+    for index in (2, 4, 6, 7, 8):
+        w_copies[index].wait_recv()
 
     for copy in wo_parts:
         copy.wait()
@@ -496,8 +705,9 @@
             y_ref[i, 4 * j : 4 * j + 4] = (core + skip * act[at, :OWN]).reshape(4, 32, OWN)
 
     locals_[2].wait()
-    for copy in cots:
-        copy.wait_recv()
+    cots.first()
+    cots.second()
+    cots.last()
 
     @pl.loop(0, LEN // TB)
     def _(i):
@@ -530,8 +740,7 @@
     dconv_ref[...] = jnp.zeros_like(dconv_ref)
     dhead_ref[...] = jnp.zeros_like(dhead_ref)
 
-    def out_copy(b):
-        return remote(po_ref.at[b], go_ref.at[me], 72 + b, (place.d, b), 80 + me)
+    outs = Scatter(place, remote, po_ref, ra_ref, rb_ref, ra2_ref, rb2_ref, own_out, 72)
 
     @pl.loop(0, BLOCKS)
     def _(i):
@@ -551,16 +760,8 @@
         dz = dgated * y * (sig_z * (1.0 + z * (1.0 - sig_z)))
         dp_ref[b, :, :OWN] = dz.astype(bf16)
         dcore_ref[b] = dgated * gate
-        part = dot(mixed, wo_ref[...], 1, 0)
-
-        @pl.when(i < BLOCKS - 1)
-        def _():
-            po_ref[b] = part.astype(bf16)
-            out_copy(b).start()
-
-        @pl.when(i == BLOCKS - 1)
-        def _():
-            own_out[...] = part
+        po_ref[b] = dot(mixed, wo_ref[...], 1, 0).astype(bf16)
+        outs.send(b)
 
     def weight_grad(q, columns):
         left = n_ref[:, :, pl.ds(pl.multiple_of(384 * q, 128), 384)].reshape(LEN, 384)
@@ -583,8 +784,8 @@
         y_ref[two, :, :24, :] = weight_grad(2 * other + q, zs).reshape(2, 8, 24, OWN)
         z_ref[two, :, :24, :] = out_grad(other, q).reshape(2, 8, 24, OWN)
 
-    swap_z = remote(rows24(y_ref), rz, 88, core_peer)
-    swap_o = remote(rows24(z_ref), ro, 89, core_peer)
+    swap_z = remote(rows24(y_ref), rz, 156, core_peer)
+    swap_o = remote(rows24(z_ref), ro, 157, core_peer)
     swap_z.start()
     swap_o.start()
 
@@ -592,17 +793,25 @@
     def _(q):
         two = pl.ds(2 * q, 2)
         dm_ref[two, :, :24, :] = weight_grad(2 * place.c + q, zs).reshape(2, 8, 24, OWN)
-        own_o[two] = out_grad(place.c, q).reshape(2, 8, 24, OWN)
-
-    me_big = place.big
-    g2z, g2o, g2x = [], [], []
-    for k in range(1, 8):
-        them, peer = place.big_of(k), bigs[k - 1]
-        g2z.append(remote(dm_ref.at[:, them, pl.ds(0, 24), :], gz.at[me_big], 92 + k, peer))
-        g2x.append(remote(big_b.at[:, them, pl.ds(0, 24), :], gx.at[me_big], 108 + k, peer))
-        for q in range(2):
-            rows = own_o.at[2 * q + them // 4, pl.ds(2 * lax.rem(them, 4), 2)]
-            g2o.append(remote(rows, gro.at[me_big, q], (100 if q else 148) + k, peer))
+        own_o[q] = out_grad(place.c, q).reshape(8, 2, 24, OWN)
+
+    def reducer(ref, gx_ref, gy_ref, base):
+        def write(big, total):
+            ref[:, big, :24, :] = total
+
+        return Reduce(
+            place, remote, lambda big: ref.at[:, big, pl.ds(0, 24), :],
+            lambda big: ref[:, big, :24, :], write, gx_ref, gy_ref, base,
+        )
+
+    def write_o(big, total):
+        own_o[:, big] = total
+
+    sum_z = reducer(dm_ref, gz, gz2, 92)
+    sum_x = reducer(big_b, gx, gx2, 102)
+    sum_o = Reduce(
+        place, remote, lambda big: own_o.at[:, big], lambda big: own_o[:, big], write_o, go, go2, 112
+    )
 
     state[...] = jnp.zeros_like(state)
     halo[...] = jnp.zeros_like(halo)
@@ -611,20 +820,18 @@
     def _(i):
         b = BLOCKS - 1 - i
 
-        @pl.when(i == 2)
+        @pl.when(i == 1)
         def _():
             swap_z.wait_recv()
             swap_o.wait_recv()
             for r in range(4):
                 dm_ref[r, :, :24, :] += rz[r]
-                own_o[r] += ro[r]
-            for copy in g2z + g2o:
-                copy.start()
-            gz[me_big] = dm_ref[:, me_big, :24, :]
             for q in range(2):
-                gro[me_big, q] = own_o[
-                    2 * q + me_big // 4, pl.ds(2 * lax.rem(me_big, 4), 2)
-                ]
+                own_o[q] += ro[2 * q : 2 * q + 2].reshape(8, 2, 24, OWN)
+            sum_z.begin()
+            sum_o.begin()
+
+        pl.when(i == 5)(outs.middle)
 
         conv = block_of(big_b, b, 640)
         raw, core, dcore = raw_ref[b], core_ref[b], dcore_ref[b]
@@ -694,7 +901,7 @@
         two = pl.ds(2 * q, 2)
         big_a[two, :, :24, :] = weight_grad(2 * other + q, late).reshape(2, 8, 24, 768)
 
-    swap_x = remote(rows24(big_a), rx, 90, core_peer)
+    swap_x = remote(rows24(big_a), rx, 158, core_peer)
     swap_x.start()
 
     @pl.loop(0, 2)
@@ -702,62 +909,38 @@
         two = pl.ds(2 * q, 2)
         big_b[two, :, :24, :] = weight_grad(2 * place.c + q, late).reshape(2, 8, 24, 768)
 
-    def in_copy(b):
-        return remote(ct_ref.at[b], gi_ref.at[me], 116 + b, (place.d, b), 124 + me)
+    cots.sent()
+    ins = Scatter(place, remote, ct_ref, ia_ref, ib_ref, ia2_ref, ib2_ref, own_dn, 122)
 
     @pl.loop(0, BLOCKS)
     def _(i):
         b = lax.rem(me + 1 + i, BLOCKS)
-        part = dot(dp_ref[b], w_ref[...].reshape(D, COLS), 1, 1)
-
-        @pl.when(i < BLOCKS - 1)
-        def _():
-            ct_ref[b] = part.astype(bf16)
-            in_copy(b).start()
-
-        @pl.when(i == BLOCKS - 1)
-        def _():
-            own_dn[...] = part
+        ct_ref[b] = dot(dp_ref[b], w_ref[...].reshape(D, COLS), 1, 1).astype(bf16)
+        ins.send(b)
 
     swap_x.wait_recv()
     for r in range(4):
         big_b[r, :, :24, :] += rx[r]
-    for copy in g2x:
-        copy.start()
-    gx[me_big] = big_b[:, me_big, :24, :]
-
-    for copy in g2z + g2o:
-        copy.wait_recv()
-    total = gz[0]
-    total_o = gro[0]
-    for j in range(1, 8):
-        total += gz[j]
-        total_o += gro[j]
-    piece[:, :, :OWN] = total
+    sum_x.begin()
+    sum_z.middle()
+    sum_o.middle()
+
+    outs.last()
+    locals_[3].wait()
+    out_ref[...] = (own_out[...] + hid_v[...].astype(f32)).astype(bf16)
+
+    piece[:, :, :OWN] = sum_z.last()
+    total_o = sum_o.last()
     for q in range(2):
         piece_o_ref[:, 384 * q : 384 * q + 384] = total_o[q].reshape(48, 384).astype(bf16)
-
-    locals_[3].wait()
-    own_out[...] += hid_v[...].astype(f32)
-
-    @pl.loop(1, BLOCKS)
-    def _(k):
-        j = lax.rem(me + k, BLOCKS)
-        remote(po_ref.at[j], go_ref.at[j], 72 + j, (place.d, j), 80 + j).wait_recv()
-        own_out[...] += go_ref[j].astype(f32)
-
-    out_ref[...] = own_out[...].astype(bf16)
-
-    for copy in g2x:
-        copy.wait_recv()
-    total = gx[0]
-    for j in range(1, 8):
-        total += gx[j]
-    piece[:, :, OWN:] = total
+    ins.middle()
+
+    sum_x.middle()
+    piece[:, :, OWN:] = sum_x.last()
     owners = []
     for k in range(1, 8):
         them = place.shard_of(k)
-        copy = remote(piece.at[lax.rem(them, 4)], ow.at[me], 132 + k, place.shard_peer(k))
+        copy = remote(piece.at[lax.rem(them, 4)], ow.at[me], 140 + k, place.shard_peer(k))
         goes = them // 4 == place.c
         pl.when(goes)(copy.start)
         owners.append((copy, goes))
@@ -766,12 +949,7 @@
     def _():
         ow[me] = piece[place.z]
 
-    @pl.loop(1, BLOCKS)
-    def _(k):
-        j = lax.rem(me + k, BLOCKS)
-        remote(ct_ref.at[j], gi_ref.at[j], 116 + j, (place.d, j), 124 + j).wait_recv()
-        own_dn[...] += gi_ref[j].astype(f32)
-
+    ins.last()
     locals_[4].wait()
     u = hid_v[...].astype(f32)
     scale = lax.rsqrt(jnp.mean(u * u, axis=1, keepdims=True) + epsilon)
@@ -787,7 +965,7 @@
     sg[1:2, 640:1024] = dgain_ref[0:1, :]
     sg[2:3, 640:1024] = dskip_ref[0:1, :]
     sg[3:5, 640:768] = dhead_ref[0:2, :]
-    sgs = [remote(sg, sg_all.at[me], 140 + k, place.shard_peer(k)) for k in range(1, 8)]
+    sgs = [remote(sg, sg_all.at[me], 148 + k, place.shard_peer(k)) for k in range(1, 8)]
     for copy in sgs:
         copy.start()
     sg_all[me] = sg[...]
@@ -814,10 +992,10 @@
     for copy in sgs:
         copy.wait_recv()
 
-    for copy in smalls + hids + cots + sums + w_x + [w_core, swap_z, swap_o, swap_x]:
+    for copy in smalls + sums + w_copies + sgs + [swap_z, swap_o, swap_x]:
         copy.wait_send()
-    for copy in g2z + g2o + g2x + sgs:
-        copy.wait_send()
+    for group_of in (outs, ins, sum_z, sum_o, sum_x):
+        group_of.sent()
     for copy, goes in owners:
         pl.when(goes)(copy.wait_send)
 
@@ -827,12 +1005,6 @@
             for copy in parts:
                 copy.wait_send()
 
-    @pl.loop(1, BLOCKS)
-    def _(k):
-        b = lax.rem(me + k, BLOCKS)
-        out_copy(b).wait_send()
-        in_copy(b).wait_send()
-
 
 def sds(shape, dtype=f32):
     return jax.ShapeDtypeStruct(shape, dtype)
@@ -848,6 +1020,10 @@
     tokens = (8, BLOCK, D)
     part = (8, BLOCK, OWN)
     split = (4, 8, 32, OWN)
+    landing = [
+        v(4, 2, 64, D, dtype=bf16), v(4, 64, D, dtype=bf16), v(64, D, dtype=bf16),
+        v(4, 64, D, dtype=bf16),
+    ]
     return pl.pallas_call(
         whole_kernel,
         in_specs=[any_spec] * 5 + [vmem],
@@ -861,15 +1037,15 @@
             v(4, 8, 32, 768), v(4, 8, 32, 768), v(8, BLOCK, 128), v(*part), v(*split), v(*split),
             v(8, NS, OWN), v(*part),
             v(8, BLOCK, COLS, dtype=bf16), v(*part, dtype=bf16), v(*tokens, dtype=bf16),
-            v(*tokens, dtype=bf16), v(BLOCK, D), v(6, BLOCK, 768), v(48, PROJ),
+            *landing, v(BLOCK, D), v(6, BLOCK, 768), v(48, PROJ),
             v(48, WIDE, dtype=bf16),
             v(OWN, D, dtype=bf16), v(8, 8, 640), v(1, 4608), v(8, CONVC),
             v(16, 128), v(8, 16, 128), v(BLOCK, 128), v(4, 8, 24, OWN), v(4, 8, 24, OWN),
-            v(4, 8, 24, OWN), v(8, 4, 24, OWN), v(8, 2, 2, 24, OWN), v(4, 8, 24, 768),
-            v(8, 4, 24, 768), v(*tokens, dtype=bf16),
+            v(2, 8, 2, 24, OWN), v(3, 2, 4, 24, OWN), v(4, 24, OWN), v(3, 2, 2, 2, 24, OWN),
+            v(2, 2, 24, OWN), v(4, 8, 24, 768), v(3, 2, 4, 24, 768), v(4, 24, 768), *landing,
             v(BLOCK, D), v(4, 24, COLS), v(8, 24, COLS), v(8, D), v(8, OWN), v(8, OWN), v(8, 640),
             v(8, 128), v(NS, OWN), v(8, 640), v(BLOCK, D, dtype=bf16), v(BLOCK, D, dtype=bf16),
-            pltpu.SemaphoreType.DMA((156,)), pltpu.SemaphoreType.DMA((156,)),
+            pltpu.SemaphoreType.DMA((160,)), pltpu.SemaphoreType.DMA((160,)),
             pltpu.SemaphoreType.DMA((15,)),
         ],
         compiler_params=pltpu.CompilerParams(

time: 315 us -> 239 us (0.76)
  Pallas kernels: 283 us -> 206 us
    pallas_call x1, Pallas kernels: 243 us -> 169 us  [run_whole(): pl.pallas_call(whole_kernel, in_specs=[any_spec] * 5 + [vmem], out_specs=...]
where the time goes in v4:
time: 239 us; the launch traced here: 238 us
  Pallas kernels  206 us (86%)
  other arithmetic  24.5 us (10%)
  local copies, waits for them, and re-layouts  6.83 us (3%)
    pallas_call x1, Pallas kernels, run_whole(): pl.pallas_call(whole_kernel, in_specs=[any_spec] * 5 + [vmem], out_specs=...  169 us
    pallas_call x1, Pallas kernels, exchange(): pl.pallas_call(kernel, out_shape=outs, in_specs=[any_spec] * len(ins), ou...  36.7 us
    sub x5, other arithmetic, adam_update(): return (first_new, second_new, master - rate * (scaled + decay * master))  18.9 us

profile of v4, /device:TPU:1, one launch (start us, length us, event | category | flops | bytes accessed | tf_op | source)
XLA Modules:
  0.0 238.3 jit_solution(15456099359810733949)
XLA Ops:
  0.7 0.7 reduce_precision.9
  1.4 0.7 reduce_precision.10
  2.1 0.1 pad.24.clone
  2.2 0.7 fusion.4.small
  2.8 0.7 reduce_precision.11
  3.5 0.1 broadcast_in_dim.23
  3.6 0.1 broadcast_in_dim_reshape.3
  3.7 0.1 pad.21.clone
  3.8 0.7 fusion.7.hd_ref
  4.4 169.4 %shard_map.296 = (bf16[128,1536]{1,0:T(8,128)(2,1)}, bf16[128,1536]{1,0:T(8,128)(2,1)}, bf16[24,6528]{1,0:T(8,128)(2,1)}, bf16[48,768]{1,0:T(8,128)(2,1)}, f32[8,8,1536]{2,1,0:T(8,128)}) custom-call(bf16[128,1536]{1,0:T(8,128)(2,1)} %bitcast.26, bf16[128,1536]{1,0:T(8,128)(2,1)} %bitcast.27, f32[192,6448]{1,0:T(8,128)} %in_ref.1, f32[384,1536]{1,0:T(8,128)} %out_w.1, ...), custom_call_target="tpu_custom_call" | custom-call | tf_op jit(solution)/shard_map/pallas_call | solution.py:1027
  173.9 1.0 slice_reduce_fusion.1
  174.9 0.9 slice.38
  175.8 0.1 fusion.9
  175.9 0.9 slice.39
  176.8 0.9 slice_reduce_fusion
  177.7 0.1 fusion.6
  177.7 0.1 reshape.59
  177.8 0.8 dynamic-slice_bitcast_fusion
  178.7 0.1 reshape_squeeze.7
  178.7 0.1 reduce_sum.38
  178.9 0.7 concatenate.19
  179.5 36.7 %shard_map.297 = (bf16[8,24,6528]{2,1,0:T(8,128)(2,1)}, bf16[8,48,1536]{2,1,0:T(8,128)(2,1)}, f32[16,24,128]{2,1,0:T(8,128)}) custom-call(bf16[24,6528]{1,0:T(8,128)(2,1)} %get-tuple-element.27.refs_0_, bf16[48,768]{1,0:T(8,128)(2,1)} %get-tuple-element.28.refs_1_, f32[24,128]{1,0:T(8,128)} %bitcast.34), custom_call_target="tpu_custom_call" | custom-call | tf_op jit(solution)/shard_map/pallas_call | solution.py:107
  216.3 0.0 copy-start
  216.3 0.0 copy-start.1
  216.3 0.0 copy-start.2
  216.3 0.0 copy-start.3
  216.3 12.7 %multiply_subtract_fusion = (f32[192,6448]{1,0:T(8,128)}, f32[192,6448]{1,0:T(8,128)}, f32[192,6448]{1,0:T(8,128)}) fusion(f32[192,6448]{1,0:T(8,128)} %in_ref.1, bf16[192,6528]{1,0:T(8,128)(2,1)} %bitcast.25, f32[192,6448]{1,0:T(8,128)} %param.21, f32[192,6448]{1,0:T(8,128)} %param.20), kind=kLoop, calls=%fused_computation.4 | loop fusion | flops 19808256 | bytes 32188416 | tf_op jit(solution)/shard_map/sub | solution.py:1065
  229.0 0.0 copy-done
  229.0 0.0 copy-done.1
  229.0 0.6 copy-done.2
  229.6 0.5 copy-done.3
  230.1 0.0 copy-start.7
  230.1 0.0 copy-start.8
  230.2 0.0 copy-start.9
  230.2 0.0 copy-start.11
  230.2 0.0 copy-start.14
  230.2 0.0 copy-start.15
  230.2 4.4 %multiply_subtract_fusion.1 = (f32[384,1536]{1,0:T(8,128)}, f32[384,1536]{1,0:T(8,128)}, f32[384,1536]{1,0:T(8,128)}) fusion(f32[384,1536]{1,0:T(8,128)S(1)} %copy-done, bf16[8,48,1536]{2,1,0:T(8,128)(2,1)S(1)} %copy-done.3, f32[384,1536]{1,0:T(8,128)S(1)} %copy-done.1, f32[384,1536]{1,0:T(8,128)S(1)} %copy-done.2), kind=kLoop, calls=%fused_computation.10 | loop fusion | flops 9437184 | bytes 15335424 | tf_op jit(solution)/shard_map/sub | solution.py:1065
  234.6 0.6 multiply_subtract_fusion.3
  235.3 0.1 slice.53
  235.3 0.1 reshape.63
  235.4 0.0 copy-done.8
  235.4 0.6 multiply_subtract_fusion.2
  236.1 0.1 slice.54
  236.1 0.1 reshape.64
  236.2 0.6 multiply_subtract_fusion.4
  236.8 0.7 copy.36
  237.6 0.7 copy.37
  (26 shorter events, 0.1 us)
Async XLA Ops:
  216.3 12.7 %copy-start = (f32[384,1536]{1,0:T(8,128)S(1)}, f32[384,1536]{1,0:T(8,128)}, u32[]{:S(2)}) copy-start(f32[384,1536]{1,0:T(8,128)} %out_w.1) | copy-start | bytes 7077892
  216.3 12.7 %copy-start.1 = (f32[384,1536]{1,0:T(8,128)S(1)}, f32[384,1536]{1,0:T(8,128)}, u32[]{:S(2)}) copy-start(f32[384,1536]{1,0:T(8,128)} %param.24) | copy-start | bytes 7077892
  216.3 13.3 %copy-start.2 = (f32[384,1536]{1,0:T(8,128)S(1)}, f32[384,1536]{1,0:T(8,128)}, u32[]{:S(2)}) copy-start(f32[384,1536]{1,0:T(8,128)} %param.23) | copy-start | bytes 7077892
  216.3 13.8 %copy-start.3 = (bf16[8,48,1536]{2,1,0:T(8,128)(2,1)S(1)}, bf16[8,48,1536]{2,1,0:T(8,128)(2,1)}, u32[]{:S(2)}) copy-start(bf16[8,48,1536]{2,1,0:T(8,128)(2,1)} %get-tuple-element.31) | copy-start | bytes 3538948
  230.1 4.5 %copy-start.6 = (f32[16,24,128]{2,1,0:T(8,128)S(1)}, f32[16,24,128]{2,1,0:T(8,128)}, u32[]{:S(2)}) copy-start(f32[16,24,128]{2,1,0:T(8,128)} %get-tuple-element.32) | copy-start | bytes 589828
  230.1 4.5 %copy-start.10 = (f32[576]{0:T(1024)S(1)}, f32[576]{0:T(1024)}, u32[]{:S(2)}) copy-start(f32[576]{0:T(1024)} %param.25) | copy-start | bytes 6916
  230.1 4.5 %copy-start.12 = (f32[576]{0:T(1024)S(1)}, f32[576]{0:T(1024)}, u32[]{:S(2)}) copy-start(f32[576]{0:T(1024)} %param.27) | copy-start | bytes 6916
  230.1 4.5 %copy-start.13 = (f32[576]{0:T(1024)S(1)}, f32[576]{0:T(1024)}, u32[]{:S(2)}) copy-start(f32[576]{0:T(1024)} %param.26) | copy-start | bytes 6916
  230.1 5.3 %copy-start.7 = (f32[5,416]{1,0:T(8,128)S(1)}, f32[5,416]{1,0:T(8,128)}, u32[]{:S(2)}) copy-start(f32[5,416]{1,0:T(8,128)} %param.28) | copy-start | bytes 24964
  230.1 5.3 %copy-start.8 = (f32[5,416]{1,0:T(8,128)S(1)}, f32[5,416]{1,0:T(8,128)}, u32[]{:S(2)}) copy-start(f32[5,416]{1,0:T(8,128)} %param.30) | copy-start | bytes 24964
  230.2 5.3 %copy-start.9 = (f32[5,416]{1,0:T(8,128)S(1)}, f32[5,416]{1,0:T(8,128)}, u32[]{:S(2)}) copy-start(f32[5,416]{1,0:T(8,128)} %param.29) | copy-start | bytes 24964
  230.2 6.1 %copy-start.11 = (f32[3,6]{1,0:T(4,128)S(1)}, f32[3,6]{1,0:T(4,128)}, u32[]{:S(2)}) copy-start(f32[3,6]{1,0:T(4,128)} %param.31) | copy-start | bytes 220
  230.2 6.1 %copy-start.14 = (f32[3,6]{1,0:T(4,128)S(1)}, f32[3,6]{1,0:T(4,128)}, u32[]{:S(2)}) copy-start(f32[3,6]{1,0:T(4,128)} %param.33) | copy-start | bytes 220
  230.2 6.0 %copy-start.15 = (f32[3,6]{1,0:T(4,128)S(1)}, f32[3,6]{1,0:T(4,128)}, u32[]{:S(2)}) copy-start(f32[3,6]{1,0:T(4,128)} %param.32) | copy-start | bytes 220
  230.2 6.6 %copy-start.5 = (bf16[128,1536]{1,0:T(8,128)(2,1)S(1)}, bf16[128,1536]{1,0:T(8,128)(2,1)}, u32[]{:S(2)}) copy-start(bf16[128,1536]{1,0:T(8,128)(2,1)} %get-tuple-element.25) | copy-start | bytes 1179652
  230.2 7.4 %copy-start.4 = (bf16[128,1536]{1,0:T(8,128)(2,1)S(1)}, bf16[128,1536]{1,0:T(8,128)(2,1)}, u32[]{:S(2)}) copy-start(bf16[128,1536]{1,0:T(8,128)(2,1)} %get-tuple-element.26) | copy-start | bytes 1179652

commit v5 on v4

--- a/solution.py
+++ b/solution.py
@@ -33,7 +33,7 @@
 adam_epsilon = 1e-08
 rates = (0.05, 0.04, 0.25, 0.5, 0.5)
 decays = (0.1, 0.1, 0.0, 0.0, 0.0)
-VMEM_LIMIT = 60 * 2**20
+TOP = 96
 
 
 class Place:
@@ -70,138 +70,6 @@
 
     def other_core_of(self, k):
         return (self.big_of(k) * 2 + 1 - self.c, self.s)
-
-
-ORDER = (6, 2, 5, 7, 1, 3, 4)
-
-
-def exchange(cid, body, ins, outs, sems, locals_):
-    def kernel(*refs):
-        in_refs = refs[: len(ins)]
-        out_refs = refs[len(ins) : len(ins) + len(outs)]
-        send, recv, own = refs[len(ins) + len(outs) :]
-        place = Place()
-
-        def meet(peers):
-            barrier = pltpu.get_barrier_semaphore()
-            for peer in peers:
-                pl.semaphore_signal(barrier, inc=1, device_id=peer, device_id_type=MESH)
-            pl.semaphore_wait(barrier, len(peers))
-
-        def remote(src, dst, index, peer):
-            return pltpu.make_async_remote_copy(
-                src_ref=src,
-                dst_ref=dst,
-                send_sem=send.at[index],
-                recv_sem=recv.at[index],
-                device_id=peer,
-                device_id_type=MESH,
-            )
-
-        def local(src, dst, index):
-            return pltpu.make_async_copy(src, dst, own.at[index])
-
-        body(place, meet, remote, local, in_refs, out_refs)
-
-    any_spec = pl.BlockSpec(memory_space=pl.ANY)
-    return pl.pallas_call(
-        kernel,
-        out_shape=outs,
-        in_specs=[any_spec] * len(ins),
-        out_specs=tuple([any_spec] * len(outs)),
-        scratch_shapes=[
-            pltpu.SemaphoreType.DMA((sems,)),
-            pltpu.SemaphoreType.DMA((sems,)),
-            pltpu.SemaphoreType.DMA((max(locals_, 1),)),
-        ],
-        compiler_params=pltpu.CompilerParams(collective_id=cid, has_side_effects=True),
-    )(*ins)
-
-
-def spread_body(place, meet, remote, local, ins, outs):
-    slab, go, small = ins
-    slab_out, go_out, small_out = outs
-    core = place.core_peer()
-    everyone = [place.big_peer(k) for k in ORDER] + [core]
-    everyone += [place.other_core_of(k) for k in ORDER]
-    meet(everyone)
-    valid = place.yl == place.c
-    at = pl.multiple_of(place.c * 768, 128)
-
-    def half(index):
-        return go_out.at[index, :, pl.ds(at, 768)]
-
-    other_at = pl.multiple_of((1 - place.c) * 768, 128)
-    own_small = local(small, small_out.at[place.d], 0)
-    own_go = local(go, half(place.big), 1)
-    own_slab = local(slab, slab_out.at[place.big], 2)
-    own_small.start()
-    own_go.start()
-    smalls = [
-        remote(small, small_out.at[place.d], n, peer) for n, peer in enumerate(everyone)
-    ]
-    slabs = [
-        remote(slab, slab_out.at[place.big], 15 + n, place.big_peer(k))
-        for n, k in enumerate(ORDER)
-    ]
-    gos = [
-        remote(go, half(place.big), 22 + n, place.big_peer(k)) for n, k in enumerate(ORDER)
-    ]
-    to_core_slab = remote(slab, slab_out.at[place.big], 29, core)
-    to_core_go = remote(go, half(place.big), 30, core)
-
-    @pl.when(valid)
-    def _():
-        own_slab.start()
-        for copy in slabs:
-            copy.start()
-        to_core_slab.start()
-
-    for copy in gos:
-        copy.start()
-    to_core_go.start()
-    for copy in smalls:
-        copy.start()
-    forward_gos = []
-    forward_slabs = []
-    for n, k in enumerate(ORDER):
-        origin = lax.rem(place.yh + k // 4, 2) * 4 + lax.rem(place.x + 4 - k % 4, 4)
-        gos[n].wait_recv()
-        go_copy = remote(half(origin), half(origin), 31 + n, core)
-        go_copy.start()
-        forward_gos.append(go_copy)
-        slab_copy = remote(slab_out.at[origin], slab_out.at[origin], 38 + n, core)
-
-        @pl.when(valid)
-        def _(n=n, slab_copy=slab_copy):
-            slabs[n].wait_recv()
-            slab_copy.start()
-
-        forward_slabs.append(slab_copy)
-    own_small.wait()
-    own_go.wait()
-    for copy in smalls:
-        copy.wait()
-    for copy in gos:
-        copy.wait_send()
-    to_core_go.wait()
-    for copy in forward_gos:
-        copy.wait()
-
-    @pl.when(valid)
-    def _():
-        own_slab.wait()
-        for copy in slabs:
-            copy.wait_send()
-        to_core_slab.wait_send()
-        for copy in forward_slabs:
-            copy.wait_send()
-
-    @pl.when(jnp.logical_not(valid))
-    def _():
-        to_core_slab.wait_recv()
-        for copy in forward_slabs:
-            copy.wait_recv()
 
 
 class Gather:
@@ -261,7 +129,7 @@
     def __init__(self, place, remote, part, ra, rb, ra2, rb2, total, base):
         self.place, self.remote, self.base = place, remote, base
         self.part, self.ra, self.rb, self.ra2, self.rb2, self.total = part, ra, rb, ra2, rb2, total
-        self.top, self.low = pl.ds(0, 64), pl.ds(64, 64)
+        self.top, self.low = pl.ds(0, TOP), pl.ds(TOP, BLOCK - TOP)
 
     def along_z(self, b, source):
         place = self.place
@@ -311,31 +179,31 @@
                 self.along_z(y * 4 + z, z).wait_recv()
 
         def sum_z(block, y):
-            total = part[block, :64].astype(f32)
+            total = part[block, :TOP].astype(f32)
             for z in self.others():
                 total += self.ra[z, y].astype(f32)
             return total
 
-        part[self.other(), :64] = sum_z(self.other(), 1 - place.yl).astype(bf16)
+        part[self.other(), :TOP] = sum_z(self.other(), 1 - place.yl).astype(bf16)
         self.over().start()
-        self.total[:64] = sum_z(place.s, place.yl)
+        self.total[:TOP] = sum_z(place.s, place.yl)
         for z in range(4):
             self.along_y((1 - place.yl) * 4 + z).wait_recv()
         for z in self.others():
             block = place.yl * 4 + z
-            part[block, 64:] = (part[block, 64:].astype(f32) + self.rb[z].astype(f32)).astype(bf16)
+            part[block, TOP:] = (part[block, TOP:].astype(f32) + self.rb[z].astype(f32)).astype(bf16)
             self.back(z).start()
-        self.total[64:] = part[place.s, 64:].astype(f32) + self.rb[place.z].astype(f32)
+        self.total[TOP:] = part[place.s, TOP:].astype(f32) + self.rb[place.z].astype(f32)
 
     def last(self):
         self.over().wait_recv()
-        self.total[:64] += self.ra2[...].astype(f32)
+        self.total[:TOP] += self.ra2[...].astype(f32)
         for z in self.others():
             self.remote(
                 self.part.at[self.place.yl * 4 + z, self.low], self.rb2.at[z],
                 self.base + 13 + z, (self.place.d, self.place.yl * 4 + z),
             ).wait_recv()
-            self.total[64:] += self.rb2[z].astype(f32)
+            self.total[TOP:] += self.rb2[z].astype(f32)
 
     def sent(self):
         place = self.place
@@ -385,6 +253,29 @@
 
     def sent(self):
         for copy in self.along + [self.over]:
+            copy.wait_send()
+
+
+class Direct:
+    def __init__(self, place, remote, src, view, base):
+        own, core = view(place.big), place.core_peer()
+        self.copies = [remote(src, own, base + k, place.big_peer(k)) for k in range(1, 8)]
+        self.cores = [remote(src, own, base + 8, core)]
+        for k in range(1, 8):
+            block = view(lax.rem(place.yh + k // 4, 2) * 4 + lax.rem(place.x + 4 - k % 4, 4))
+            self.cores.append(remote(block, block, base + 8 + k, core))
+
+    def begin(self):
+        for copy in self.copies + self.cores[:1]:
+            copy.start()
+
+    def forward(self):
+        for k in range(1, 8):
+            self.copies[k - 1].wait_recv()
+            self.cores[k].start()
+
+    def sent(self):
+        for copy in self.copies + self.cores:
             copy.wait_send()
 
 
@@ -501,12 +392,12 @@
 
 
 def whole_kernel(
-    hid, cot, in_ref, out_w, small, hd_ref,
-    out_ref, igrad_ref, slab_ref, piece_o_ref, sg_all,
+    hid, cot, in_ref, out_w, conv_in, gain_in, head_in,
+    out_ref, igrad_ref, slabs, gos, total_small,
     n_ref, ct_ref, w_ref, z_ref, big_a, big_b, raw_ref, core_ref, y_ref, dm_ref, st_ref, dcore_ref,
-    dp_ref, mixed_ref, po_ref, ra_ref, rb_ref, ra2_ref, rb2_ref, own_out, wo_f, wq_f, wq, wo_ref, sm_ref, gain_ref, conv_ref,
-    sums_ref, got_sums, turned_sums, rz, ro, own_o, gz, gz2, go, go2, rx, gx, gx2, ia_ref, ib_ref, ia2_ref, ib2_ref, own_dn,
-    piece, ow, sg, dgain_ref, dskip_ref, dconv_ref, dhead_ref,
+    dp_ref, mixed_ref, po_ref, ra_ref, rb_ref, ra2_ref, rb2_ref, own_out, wq_f, wq, wo_ref, sm_ref, gain_ref, conv_ref,
+    sums_ref, got_sums, turned_sums, rz, ro, own_o, gz, gz2, go, go2, rx, gx, gx2, ia_ref, ib_ref, ia2_ref, ib2_ref,
+    piece_z, piece_x, ow_z, ow_x, slab_ref, piece_o_ref, small_out, smalls_dp, sg, sg_all, small, hd_ref, gvec, cvec, dgain_ref, dskip_ref, dconv_ref, dhead_ref,
     state, halo, hid_v, cot_v, send, recv, own,
 ):
     place = Place()
@@ -516,14 +407,21 @@
     )
     wq_load.start()
     wq[:, WIDE - 128 :] = jnp.zeros((48, 128), bf16)
+    small[...] = jnp.zeros_like(small)
+    small[:5, :416] = conv_in[...].astype(bf16).astype(f32)
+    small[5:6, :576] = gain_in[...].astype(bf16).astype(f32)
+    hd_ref[...] = jnp.zeros_like(hd_ref)
+    hd_ref[:3, :6] = head_in[...].astype(bf16).astype(f32)
+    hd_ref[3:4, :] = widen(hd_ref[:, :128])[2:3]
     barrier = pltpu.get_barrier_semaphore()
     core_peer = place.core_peer()
     bigs = [place.big_peer(k) for k in range(1, 8)]
     x_peers = bigs[:3]
     group = [place.shard_peer(k) for k in range(1, 8)]
-    for peer in group + bigs + [core_peer]:
+    everyone = bigs + [core_peer] + [place.other_core_of(k) for k in range(1, 8)]
+    for peer in group + everyone:
         pl.semaphore_signal(barrier, inc=1, device_id=peer, device_id_type=MESH)
-    pl.semaphore_wait(barrier, 15)
+    pl.semaphore_wait(barrier, 22)
 
     def remote(src, dst, index, peer, other=None):
         return pltpu.make_async_remote_copy(
@@ -547,7 +445,6 @@
         )
 
     locals_ = [
-        pltpu.make_async_copy(small, sm_ref.at[me], own.at[0]),
         pltpu.make_async_copy(hid, n_ref.at[me], own.at[1]),
         pltpu.make_async_copy(cot, ct_ref.at[me], own.at[2]),
         pltpu.make_async_copy(hid, hid_v, own.at[3]),
@@ -558,11 +455,11 @@
     mine = place.yl == place.c
     wo_parts = [
         pltpu.make_async_copy(
-            out_w.at[pl.ds(BLOCK * (p % 3), BLOCK), pl.ds(768 * (p // 3), 768)],
-            wo_f.at[p],
-            own.at[8 + p],
+            out_w.at[pl.ds(32 * (p % 12), 32), pl.ds(768 * (p // 12), 768)],
+            big_a.at[p // 8, p % 8],
+            own.at[17 + p],
         )
-        for p in range(6)
+        for p in range(24)
     ]
     for copy in wo_parts:
         copy.start()
@@ -584,70 +481,91 @@
             ]
         )
 
-    @pl.when(mine)
-    def _():
-        for copy in own_w:
-            copy.start()
-        for parts in weights:
-            for copy in parts:
-                copy.start()
-
+    def w_begin(some):
+        @pl.when(mine)
+        def _():
+            for i in some:
+                own_w[i].start()
+            for parts in weights:
+                for i in some:
+                    parts[i].start()
+
+    w_begin((1, 2))
     for copy in smalls:
         copy.start()
     hids.begin()
-
-    def from_offset(k):
-        return lax.rem(place.yl + k // 4, 2)
-
-    for k in range(1, 8):
-        @pl.when(from_offset(k) == place.c)
-        def _(k=k):
-            for copy in weights[k - 1]:
-                copy.wait_recv()
-
-    @pl.when(mine)
-    def _():
-        for copy in own_w:
-            copy.wait()
+    w_begin((0,))
+
+    def w_arrived(some):
+        for k in range(1, 8):
+            @pl.when(lax.rem(place.yl + k // 4, 2) == place.c)
+            def _(k=k):
+                for i in some:
+                    weights[k - 1][i].wait_recv()
+
+        @pl.when(mine)
+        def _():
+            for i in some:
+                own_w[i].wait()
 
     w_up, w_down = place.big_peer(1), place.big_peer(3)
 
-    def w_quarter(k, lo=0, n=4):
-        rows = pl.ds(pl.multiple_of(48 * lax.rem(place.x + k, 4), 16), 48)
-        return w_ref.at[pl.ds(4 * place.c + lo, n), rows, :]
-
-    def w_on(view, index, peer):
-        return remote(view, view, 32 + index, peer)
-
-    w_copies = [
-        w_on(w_quarter(0), 0, w_up),
-        w_on(w_quarter(0), 1, w_down),
-        w_on(w_quarter(0), 2, core_peer),
-        w_on(w_quarter(3, 0, 2), 3, w_up),
-        w_on(w_quarter(3), 4, core_peer),
-        w_on(w_quarter(1, 2, 2), 5, w_down),
-        w_on(w_quarter(1), 6, core_peer),
-        w_on(w_quarter(2, 0, 2), 7, core_peer),
-        w_on(w_quarter(2, 2, 2), 8, core_peer),
-    ]
-    for copy in w_copies[:3]:
-        copy.start()
-
-    def w_after(arrived, *indices):
-        w_copies[arrived].wait_recv()
-        for index in indices:
-            w_copies[index].start()
-
-    locals_[1].wait()
+    class Quarters:
+        def __init__(self, columns, base):
+            def quarter(k, lo=0, n=4):
+                rows = pl.ds(pl.multiple_of(48 * lax.rem(place.x + k, 4), 16), 48)
+                return w_ref.at[pl.ds(4 * place.c + lo, n), rows, columns]
+
+            def on(view, index, peer):
+                return remote(view, view, base + index, peer)
+
+            self.copies = [
+                on(quarter(0), 0, w_up),
+                on(quarter(0), 1, w_down),
+                on(quarter(0), 2, core_peer),
+                on(quarter(3, 0, 2), 3, w_up),
+                on(quarter(3), 4, core_peer),
+                on(quarter(1, 2, 2), 5, w_down),
+                on(quarter(1), 6, core_peer),
+                on(quarter(2, 0, 2), 7, core_peer),
+                on(quarter(2, 2, 2), 8, core_peer),
+            ]
+
+        def begin(self):
+            for copy in self.copies[:3]:
+                copy.start()
+
+        def after(self, arrived, *indices):
+            self.copies[arrived].wait_recv()
+            for index in indices:
+                self.copies[index].start()
+
+        def first(self):
+            self.after(0, 3, 4)
+            self.after(1, 5, 6)
+
+        def second(self):
+            self.after(3, 7)
+            self.after(5, 8)
+
+        def last(self):
+            for index in (2, 4, 6, 7, 8):
+                self.copies[index].wait_recv()
+
+    w_scan = Quarters(pl.ds(OWN, 768), 32)
+    w_gate = Quarters(pl.ds(0, OWN), 240)
+    w_arrived((1, 2))
+    w_scan.begin()
+    locals_[0].wait()
     hids.first()
-    w_after(0, 3, 4)
-    w_after(1, 5, 6)
+    w_scan.first()
     hids.second()
+    w_arrived((0,))
+    w_gate.begin()
     cots.begin()
-    w_after(3, 7)
-    w_after(5, 8)
-
-    locals_[0].wait()
+    w_scan.second()
+
+    sm_ref[me] = small[...]
     for copy in smalls:
         copy.wait_recv()
     gain_ref[...] = jnp.concatenate([sm_ref[p, 5:6, :576] for p in range(8)], axis=1)
@@ -660,14 +578,14 @@
 
     hids.last()
     hids.sent()
-    for index in (2, 4, 6, 7, 8):
-        w_copies[index].wait_recv()
+    w_scan.last()
 
     for copy in wo_parts:
         copy.wait()
-    for p in range(6):
-        at = 768 * (p // 3)
-        wo_ref[BLOCK * (p % 3) : BLOCK * (p % 3 + 1), at : at + 768] = wo_f[p].astype(bf16)
+    for p in range(24):
+        at = 768 * (p // 12)
+        rows = slice(32 * (p % 12), 32 * (p % 12) + 32)
+        wo_ref[rows, at : at + 768] = big_a[p // 8, p % 8].astype(bf16)
     state[...] = jnp.zeros_like(state)
     halo[...] = jnp.zeros_like(halo)
     skip = hd_ref[3:4, :]
@@ -675,15 +593,26 @@
     @pl.loop(0, LEN // TB)
     def _(i):
         two = pl.ds(2 * i, 2)
+
+        @pl.when(i == 1)
+        def _():
+            w_gate.first()
+
+        @pl.when(i == 2)
+        def _():
+            w_gate.second()
+
+        @pl.when(i == 3)
+        def _():
+            cots.first()
+
         u = n_ref[two].reshape(TB, D).astype(f32)
         scale = lax.rsqrt(jnp.mean(u * u, axis=1, keepdims=True) + epsilon)
         normed = (u * scale * gain_ref[:, :D]).astype(bf16)
         n_ref[two] = normed.reshape(2, BLOCK, D)
-        project = dot(normed, w_ref[...].reshape(D, COLS), 1, 0)
-        z = project[:, :OWN]
-        xbc = project[:, OWN : OWN + 640]
-        raw = pltpu.roll(project[:, 1024:1152], 128 - 6 * me, 1)
-        z_ref[i] = z.reshape(8, 32, OWN)
+        project = dot(normed, w_ref[:, :, OWN:].reshape(D, 768), 1, 0)
+        xbc = project[:, :640]
+        raw = pltpu.roll(project[:, 640:], 128 - 6 * me, 1)
         big_a[i, :, :, :640] = xbc.reshape(8, 32, 640)
         raw_ref[two] = raw.reshape(2, BLOCK, 128)
         extended = jnp.concatenate([halo[...], xbc], axis=0)
@@ -704,9 +633,16 @@
             core_ref[2 * i + j] = core
             y_ref[i, 4 * j : 4 * j + 4] = (core + skip * act[at, :OWN]).reshape(4, 32, OWN)
 
-    locals_[2].wait()
-    cots.first()
     cots.second()
+    w_gate.last()
+
+    @pl.loop(0, LEN // TB)
+    def _(i):
+        normed = n_ref[pl.ds(2 * i, 2)].reshape(TB, D)
+        z = dot(normed, w_ref[:, :, :OWN].reshape(D, OWN), 1, 0)
+        z_ref[i] = z.reshape(8, 32, OWN)
+
+    locals_[1].wait()
     cots.last()
 
     @pl.loop(0, LEN // TB)
@@ -795,20 +731,25 @@
         dm_ref[two, :, :24, :] = weight_grad(2 * place.c + q, zs).reshape(2, 8, 24, OWN)
         own_o[q] = out_grad(place.c, q).reshape(8, 2, 24, OWN)
 
-    def reducer(ref, gx_ref, gy_ref, base):
+    def rows_fns(ref, first, n):
+        some = pl.ds(first, n)
+
+        def view(big):
+            return ref.at[some, big, pl.ds(0, 24), :]
+
+        def read(big):
+            return ref[some, big, :24, :]
+
         def write(big, total):
-            ref[:, big, :24, :] = total
-
-        return Reduce(
-            place, remote, lambda big: ref.at[:, big, pl.ds(0, 24), :],
-            lambda big: ref[:, big, :24, :], write, gx_ref, gy_ref, base,
-        )
+            ref[some, big, :24, :] = total
+
+        return view, read, write
 
     def write_o(big, total):
         own_o[:, big] = total
 
-    sum_z = reducer(dm_ref, gz, gz2, 92)
-    sum_x = reducer(big_b, gx, gx2, 102)
+    sum_z = Reduce(place, remote, *rows_fns(dm_ref, 0, 4), gz, gz2, 92)
+    sum_x = Reduce(place, remote, *rows_fns(big_b, 0, 4), gx, gx2, 102)
     sum_o = Reduce(
         place, remote, lambda big: own_o.at[:, big], lambda big: own_o[:, big], write_o, go, go2, 112
     )
@@ -910,7 +851,7 @@
         big_b[two, :, :24, :] = weight_grad(2 * place.c + q, late).reshape(2, 8, 24, 768)
 
     cots.sent()
-    ins = Scatter(place, remote, ct_ref, ia_ref, ib_ref, ia2_ref, ib2_ref, own_dn, 122)
+    ins = Scatter(place, remote, ct_ref, ia_ref, ib_ref, ia2_ref, ib2_ref, own_out, 122)
 
     @pl.loop(0, BLOCKS)
     def _(i):
@@ -918,42 +859,84 @@
         ct_ref[b] = dot(dp_ref[b], w_ref[...].reshape(D, COLS), 1, 1).astype(bf16)
         ins.send(b)
 
-    swap_x.wait_recv()
-    for r in range(4):
-        big_b[r, :, :24, :] += rx[r]
-    sum_x.begin()
+        @pl.when(i == 3)
+        def _():
+            swap_x.wait_recv()
+            for r in range(4):
+                big_b[r, :, :24, :] += rx[r]
+            sum_x.begin()
+
     sum_z.middle()
     sum_o.middle()
 
-    outs.last()
-    locals_[3].wait()
-    out_ref[...] = (own_out[...] + hid_v[...].astype(f32)).astype(bf16)
-
-    piece[:, :, :OWN] = sum_z.last()
+    at_o = pl.multiple_of(768 * place.c, 128)
+    o_all = Spread(
+        place, remote, piece_o_ref,
+        lambda big, lo, hi: gos.at[big, :, pl.ds(pl.multiple_of(at_o + lo, 128), hi - lo)],
+        (256, 384, 768), 160,
+    )
+    z_all = Spread(
+        place, remote, slab_ref.at[:, pl.ds(0, DI)],
+        lambda big, lo, hi: slabs.at[big, :, pl.ds(lo, hi - lo)], (768, 1536, DI), 180,
+    )
+    x_all = Direct(
+        place, remote, slab_ref.at[:, pl.ds(DI, WIDE - DI)],
+        lambda big: slabs.at[big, :, pl.ds(DI, WIDE - DI)], 200,
+    )
+
+    def to_owners(piece, ow, base):
+        copies = []
+        for k in range(1, 8):
+            them = place.shard_of(k)
+            copy = remote(piece.at[lax.rem(them, 4)], ow.at[me], base + k, place.shard_peer(k))
+            goes = them // 4 == place.c
+            pl.when(goes)(copy.start)
+            copies.append((copy, goes))
+
+        @pl.when(mine)
+        def _():
+            ow[me] = piece[place.z]
+
+        return copies
+
+    piece_z[...] = sum_z.last()
+    owners_z = to_owners(piece_z, ow_z, 140)
     total_o = sum_o.last()
     for q in range(2):
         piece_o_ref[:, 384 * q : 384 * q + 384] = total_o[q].reshape(48, 384).astype(bf16)
-    ins.middle()
-
-    sum_x.middle()
-    piece[:, :, OWN:] = sum_x.last()
-    owners = []
-    for k in range(1, 8):
-        them = place.shard_of(k)
-        copy = remote(piece.at[lax.rem(them, 4)], ow.at[me], 140 + k, place.shard_peer(k))
-        goes = them // 4 == place.c
-        pl.when(goes)(copy.start)
-        owners.append((copy, goes))
+    o_all.begin()
+    own_go = pltpu.make_async_copy(
+        piece_o_ref, gos.at[place.big, :, pl.ds(at_o, 768)], own.at[15]
+    )
+    own_go.start()
+
+    outs.last()
+    locals_[2].wait()
+    out_ref[...] = (own_out[...] + hid_v[...].astype(f32)).astype(bf16)
 
     @pl.when(mine)
     def _():
-        ow[me] = piece[place.z]
-
+        for copy, _ in owners_z:
+            copy.wait_recv()
+        for j in range(8):
+            slab_ref[:, OWN * j : OWN * (j + 1)] = ow_z[j].astype(bf16)
+        z_all.begin()
+
+    ins.middle()
+    for n in range(4):
+        o_all.step(n)
+        pl.when(mine)(functools.partial(z_all.step, n))
+    sum_x.middle()
+    for n in range(4, 8):
+        o_all.step(n)
+        pl.when(mine)(functools.partial(z_all.step, n))
+    piece_x[...] = sum_x.last()
+    owners_x = to_owners(piece_x, ow_x, 232)
     ins.last()
-    locals_[4].wait()
+    locals_[3].wait()
     u = hid_v[...].astype(f32)
     scale = lax.rsqrt(jnp.mean(u * u, axis=1, keepdims=True) + epsilon)
-    d_normed = own_dn[...]
+    d_normed = own_out[...]
     gained = gain_ref[:, :D] * d_normed
     unit = u * scale
     grad = scale * gained - unit * (scale * scale * jnp.mean(u * gained, axis=1, keepdims=True))
@@ -963,44 +946,84 @@
     sg[0:1, :] = jnp.sum(d_normed * unit, axis=0, keepdims=True)
     sg[1:6, :640] = dconv_ref[0:5, :]
     sg[1:2, 640:1024] = dgain_ref[0:1, :]
-    sg[2:3, 640:1024] = dskip_ref[0:1, :]
-    sg[3:5, 640:768] = dhead_ref[0:2, :]
     sgs = [remote(sg, sg_all.at[me], 148 + k, place.shard_peer(k)) for k in range(1, 8)]
     for copy in sgs:
         copy.start()
     sg_all[me] = sg[...]
 
-    for k in range(1, 8):
-        @pl.when(mine)
-        def _(k=k):
-            owners[k - 1][0].wait_recv()
-
     @pl.when(mine)
     def _():
-        common = ow[0, :, 2 * OWN :]
+        for copy, _ in owners_x:
+            copy.wait_recv()
+        common = ow_x[0, :, OWN:]
         for j in range(1, 8):
-            common += ow[j, :, 2 * OWN :]
+            common += ow_x[j, :, OWN:]
         for j in range(8):
-            slab_ref[:, OWN * j : OWN * (j + 1)] = ow[j, :, :OWN].astype(bf16)
-            slab_ref[:, DI + OWN * j : DI + OWN * (j + 1)] = ow[j, :, OWN : 2 * OWN].astype(bf16)
+            slab_ref[:, DI + OWN * j : DI + OWN * (j + 1)] = ow_x[j, :, :OWN].astype(bf16)
         slab_ref[:, 2 * DI :] = common.astype(bf16)
+        x_all.begin()
+
+    own_slab = pltpu.make_async_copy(slab_ref, slabs.at[place.big], own.at[16])
+    pl.when(mine)(own_slab.start)
+    for copy in sgs:
+        copy.wait_recv()
+    small_out[...] = jnp.zeros_like(small_out)
+    gvec[:, :D] = sg_all[0, 0:1, :]
+    cvec[...] = jnp.zeros_like(cvec)
+    cvec[:5, DI:CONVC] = sg_all[0, 1:6, OWN:640]
+    for j in range(1, 8):
+        gvec[:, :D] += sg_all[j, 0:1, :]
+        cvec[:5, DI:CONVC] += sg_all[j, 1:6, OWN:640]
+    for j in range(8):
+        gvec[:, D + OWN * j : D + OWN * (j + 1)] = sg_all[j, 1:2, 640:1024]
+        cvec[:5, OWN * j : OWN * (j + 1)] = sg_all[j, 1:6, :OWN]
+    near = gvec[:, pl.ds(pl.multiple_of(128 * (9 * me // 2), 128), 640)]
+    small_out[5:6, :576] = jnp.where(lax.rem(me, 2) == 1, near[:, 64:640], near[:, :576])
+    near = cvec[:, pl.ds(pl.multiple_of(128 * (13 * me // 4), 128), 640)]
+    shift = lax.rem(13 * me, 4)
+    taps = near[:, :416]
+    for k in range(1, 4):
+        taps = jnp.where(shift == k, near[:, 32 * k : 32 * k + 416], taps)
+    small_out[:5, :416] = taps[:5]
+    small_out[6:7, :128] = dhead_ref[0:1, :]
+    small_out[6:7, 128:256] = dhead_ref[1:2, :]
+    small_out[6:7, 256:384] = dot_exact(dskip_ref[0:1, :], head_ones(), 1, 0)
+    dps = [remote(small_out, smalls_dp.at[place.d], 216 + n, peer) for n, peer in enumerate(everyone)]
+    for copy in dps:
+        copy.start()
+    smalls_dp[place.d] = small_out[...]
+
+    @pl.when(mine)
+    def _():
+        x_all.forward()
+        own_slab.wait()
 
     @pl.when(jnp.logical_not(mine))
     def _():
-        slab_ref[...] = jnp.zeros_like(slab_ref)
-
-    for copy in sgs:
+        for copy in z_all.cores + x_all.cores:
+            copy.wait_recv()
+
+    for copy in o_all.cores:
         copy.wait_recv()
-
-    for copy in smalls + sums + w_copies + sgs + [swap_z, swap_o, swap_x]:
+    own_go.wait()
+    for copy in dps:
+        copy.wait_recv()
+    total = smalls_dp[0]
+    for j in range(1, 16):
+        total += smalls_dp[j]
+    total_small[...] = total
+
+    for copy in smalls + sums + w_scan.copies + w_gate.copies + sgs + dps + [swap_z, swap_o, swap_x]:
         copy.wait_send()
-    for group_of in (outs, ins, sum_z, sum_o, sum_x):
+    for group_of in (outs, ins, sum_z, sum_o, sum_x, o_all):
         group_of.sent()
-    for copy, goes in owners:
+    for copy, goes in owners_z + owners_x:
         pl.when(goes)(copy.wait_send)
 
     @pl.when(mine)
     def _():
+        z_all.sent()
+        x_all.sent()
         for parts in weights:
             for copy in parts:
                 copy.wait_send()
@@ -1010,7 +1033,7 @@
     return jax.ShapeDtypeStruct(shape, dtype)
 
 
-def run_whole(hid, cot, in_master, out_master, small, hd):
+def run_whole(hid, cot, in_master, out_master, conv, gain, head):
     any_spec = pl.BlockSpec(memory_space=pl.ANY)
     vmem = pl.BlockSpec(memory_space=pltpu.VMEM)
 
@@ -1021,37 +1044,101 @@
     part = (8, BLOCK, OWN)
     split = (4, 8, 32, OWN)
     landing = [
-        v(4, 2, 64, D, dtype=bf16), v(4, 64, D, dtype=bf16), v(64, D, dtype=bf16),
-        v(4, 64, D, dtype=bf16),
+        v(4, 2, TOP, D, dtype=bf16), v(4, BLOCK - TOP, D, dtype=bf16), v(TOP, D, dtype=bf16),
+        v(4, BLOCK - TOP, D, dtype=bf16),
     ]
     return pl.pallas_call(
         whole_kernel,
-        in_specs=[any_spec] * 5 + [vmem],
-        out_specs=tuple([vmem] * 5),
+        in_specs=[any_spec] * 4 + [vmem] * 3,
+        out_specs=(vmem, vmem, any_spec, any_spec, vmem),
         out_shape=(
-            sds((BLOCK, D), bf16), sds((BLOCK, D), bf16), sds((24, WIDE), bf16),
-            sds((48, 768), bf16), sds((8, 8, D)),
+            sds((BLOCK, D), bf16), sds((BLOCK, D), bf16), sds((8, 24, WIDE), bf16),
+            sds((8, 48, D), bf16), sds((8, 640)),
         ),
         scratch_shapes=[
             v(*tokens, dtype=bf16), v(*tokens, dtype=bf16), v(8, 192, COLS, dtype=bf16), v(*split),
             v(4, 8, 32, 768), v(4, 8, 32, 768), v(8, BLOCK, 128), v(*part), v(*split), v(*split),
             v(8, NS, OWN), v(*part),
             v(8, BLOCK, COLS, dtype=bf16), v(*part, dtype=bf16), v(*tokens, dtype=bf16),
-            *landing, v(BLOCK, D), v(6, BLOCK, 768), v(48, PROJ),
+            *landing, v(BLOCK, D), v(48, PROJ),
             v(48, WIDE, dtype=bf16),
             v(OWN, D, dtype=bf16), v(8, 8, 640), v(1, 4608), v(8, CONVC),
             v(16, 128), v(8, 16, 128), v(BLOCK, 128), v(4, 8, 24, OWN), v(4, 8, 24, OWN),
             v(2, 8, 2, 24, OWN), v(3, 2, 4, 24, OWN), v(4, 24, OWN), v(3, 2, 2, 2, 24, OWN),
             v(2, 2, 24, OWN), v(4, 8, 24, 768), v(3, 2, 4, 24, 768), v(4, 24, 768), *landing,
-            v(BLOCK, D), v(4, 24, COLS), v(8, 24, COLS), v(8, D), v(8, OWN), v(8, OWN), v(8, 640),
-            v(8, 128), v(NS, OWN), v(8, 640), v(BLOCK, D, dtype=bf16), v(BLOCK, D, dtype=bf16),
-            pltpu.SemaphoreType.DMA((160,)), pltpu.SemaphoreType.DMA((160,)),
-            pltpu.SemaphoreType.DMA((15,)),
+            v(4, 24, OWN), v(4, 24, 768), v(8, 24, OWN), v(8, 24, 768),
+            v(24, WIDE, dtype=bf16), v(48, 768, dtype=bf16), v(8, 640), v(16, 8, 640), v(8, D), v(8, 8, D), v(8, 640), v(8, OWN), v(1, 4736),
+            v(8, 3456), v(8, OWN), v(8, OWN), v(8, 640), v(8, 128), v(NS, OWN), v(8, 640), v(BLOCK, D, dtype=bf16), v(BLOCK, D, dtype=bf16),
+            pltpu.SemaphoreType.DMA((250,)), pltpu.SemaphoreType.DMA((250,)),
+            pltpu.SemaphoreType.DMA((41,)),
         ],
         compiler_params=pltpu.CompilerParams(
             collective_id=1, has_side_effects=True, vmem_limit_bytes=62 * 2**20
         ),
-    )(hid, cot, in_master, out_master, small, hd)
+    )(hid, cot, in_master, out_master, conv, gain, head)
+
+
+class Spread:
+    def __init__(self, place, remote, src, view, cuts, base):
+        one, two, end = cuts
+
+        def at(dy, dx, lo, hi):
+            return view(lax.rem(place.yh + dy, 2) * 4 + lax.rem(place.x + dx, 4), lo, hi)
+
+        def onward(part, index, peer):
+            return remote(part, part, base + index, peer)
+
+        up, down, over = place.big_peer(1), place.big_peer(3), place.big_peer(4)
+        own = view(place.big, 0, end)
+        self.copies = [
+            remote(src, own, base, up),
+            remote(src, own, base + 1, down),
+            remote(src, own, base + 2, over),
+            onward(at(0, 3, 0, two), 3, up),
+            onward(at(0, 1, two, end), 4, down),
+            onward(at(0, 3, two, end), 5, over),
+            onward(at(0, 1, two, end), 6, over),
+            onward(at(0, 2, two, end), 7, over),
+            onward(at(1, 0, 0, two), 8, up),
+            onward(at(1, 0, 0, two), 9, down),
+            onward(at(1, 3, 0, one), 10, up),
+            onward(at(1, 1, one, two), 11, down),
+        ]
+        core = place.core_peer()
+        self.cores = [remote(src, own, base + 12, core)]
+        for n, (dy, dx, _, _) in enumerate(ARRIVALS[1:]):
+            block = at(dy, dx, 0, end)
+            self.cores.append(remote(block, block, base + 13 + n, core))
+
+    def begin(self):
+        for index in (2, 0, 1):
+            self.copies[index].start()
+        self.cores[0].start()
+
+    def step(self, n):
+        _, _, needs, sends = ARRIVALS[n]
+        for index in needs:
+            self.copies[index].wait_recv()
+        for index in sends:
+            self.copies[index].start()
+        if n:
+            self.cores[n].start()
+
+    def sent(self):
+        for copy in self.copies + self.cores:
+            copy.wait_send()
+
+
+ARRIVALS = (
+    (0, 0, (), ()),
+    (1, 0, (2,), (8, 9)),
+    (0, 3, (0,), (3, 5)),
+    (0, 1, (1,), (4, 6)),
+    (0, 2, (3, 4), (7,)),
+    (1, 3, (8, 5), (10,)),
+    (1, 1, (9, 6), (11,)),
+    (1, 2, (10, 11, 7), ()),
+)
 
 
 def adam_update(master, first, second, gradient, rate, decay):
@@ -1070,63 +1157,19 @@
     gain_master, gain_first, gain_second, conv_master, conv_first, conv_second,
     head_master, head_first, head_second,
 ):
-    s = lax.axis_index("shard")
-    low = lambda v: lax.reduce_precision(v, 8, 7)
-    small = jnp.concatenate(
-        [
-            jnp.pad(low(conv_master), ((0, 0), (0, 224))),
-            jnp.pad(low(gain_master), (0, 64))[None],
-            jnp.zeros((2, 640), f32),
-        ],
-        axis=0,
-    )
-    heads = low(head_master)
-    hd = jnp.concatenate(
-        [
-            jnp.pad(heads, ((0, 0), (0, OWN - 6))),
-            jnp.repeat(heads[2], HD)[None],
-            jnp.zeros((4, OWN), f32),
-        ],
-        axis=0,
-    )
-    layer_out, input_grad, slab, piece_o, sg = run_whole(
-        hidden[0], cotangent[0], in_master, out_master, small, hd
-    )
-    g_gain = jnp.concatenate([jnp.sum(sg[:, 0], axis=0), sg[:, 1, 640:1024].reshape(-1)])
-    g_conv = jnp.concatenate(
-        [
-            sg[:, 1:6, :OWN].transpose(1, 0, 2).reshape(5, DI),
-            jnp.sum(sg[:, 1:6, OWN:640], axis=0),
-        ],
-        axis=1,
-    )
-    mine = lax.dynamic_index_in_dim(sg, s, 0, keepdims=False)
-    own_small = jnp.concatenate(
-        [
-            lax.dynamic_slice(g_gain, (576 * s,), (576,)),
-            lax.dynamic_slice(g_conv, (0, 416 * s), (5, 416)).reshape(-1),
-            mine[3, 640:646], mine[4, 640:646],
-            jnp.sum(mine[2, 640:1024].reshape(6, HD), axis=1),
-            jnp.zeros((398,), f32),
-        ]
-    ).reshape(24, 128)
-    total_w, total_o, total_small = exchange(
-        7, spread_body, (slab, piece_o, own_small),
-        (sds((8, 24, WIDE), bf16), sds((8, 48, D), bf16), sds((16, 24, 128))), 45, 3,
-    )
-    total_small = jnp.sum(total_small, axis=0).reshape(-1)
-    totals = (
-        total_w.reshape(192, WIDE)[:, :PROJ].astype(f32),
-        total_o.reshape(OWN, D).astype(f32),
-        total_small[:576],
-        total_small[576:2656].reshape(5, 416),
-        total_small[2656:2674].reshape(3, 6),
+    layer_out, input_grad, total_w, total_o, total = run_whole(
+        hidden[0], cotangent[0], in_master, out_master, conv_master, gain_master[None], head_master
+    )
+    gradients = (
+        total_w.reshape(192, WIDE)[:, :PROJ].astype(f32), total_o.reshape(OWN, D).astype(f32),
+        total[5, :576], total[:5, :416],
+        jnp.stack([total[6, :6], total[6, 128:134], total[6, 256:262]]),
     )
     masters = (in_master, out_master, gain_master, conv_master, head_master)
     firsts = (in_first, out_first, gain_first, conv_first, head_first)
     seconds = (in_second, out_second, gain_second, conv_second, head_second)
     updated = [
-        adam_update(masters[g], firsts[g], seconds[g], totals[g], rates[g], decays[g])
+        adam_update(masters[g], firsts[g], seconds[g], gradients[g], rates[g], decays[g])
         for g in range(5)
     ]
     return (layer_out[None], input_grad[None]) + tuple(v for group in updated for v in group)

time: 239 us -> 221 us (0.925)
  Pallas kernels: 206 us -> 197 us
  other arithmetic: 24.5 us -> 18.9 us
  local copies, waits for them, and re-layouts: 6.83 us -> 4 us
    pallas_call x2 -> x1, Pallas kernels: 206 us -> 197 us  [run_whole(): pl.pallas_call(whole_kernel, in_specs=[any_spec] * 4 + [vmem] * 3, out_sp...]
where the time goes in v5:
time: 221 us
  Pallas kernels  197 us (89%)
  other arithmetic  18.9 us (9%)
  local copies, waits for them, and re-layouts  4 us (2%)
    pallas_call x1, Pallas kernels, run_whole(): pl.pallas_call(whole_kernel, in_specs=[any_spec] * 4 + [vmem] * 3, out_sp...  197 us
    sub x5, other arithmetic, adam_update(): return (first_new, second_new, master - rate * (scaled + decay * master))  18.9 us

profile of v5, /device:TPU:1, one launch (start us, length us, event | category | flops | bytes accessed | tf_op | source)
XLA Modules:
  0.0 220.7 jit_solution(15085905784675955917)
XLA Ops:
  0.7 1.3 broadcast_in_dim.9.gain_in
  1.9 197.0 %shard_map.296 = (bf16[128,1536]{1,0:T(8,128)(2,1)}, bf16[128,1536]{1,0:T(8,128)(2,1)}, bf16[8,24,6528]{2,1,0:T(8,128)(2,1)}, bf16[8,48,1536]{2,1,0:T(8,128)(2,1)}, f32[8,640]{1,0:T(8,128)}) custom-call(bf16[128,1536]{1,0:T(8,128)(2,1)} %bitcast.14, bf16[128,1536]{1,0:T(8,128)(2,1)} %bitcast.15, f32[192,6448]{1,0:T(8,128)} %in_ref.1, f32[384,1536]{1,0:T(8,128)} %out_w.1, ...), custom_call_target="tpu_custom_call" | custom-call | tf_op jit(solution)/shard_map/pallas_call | solution.py:1050
  198.9 0.0 copy-start
  198.9 0.0 copy-start.1
  198.9 0.0 copy-start.2
  198.9 0.0 copy-start.3
  198.9 12.7 %multiply_subtract_fusion = (f32[192,6448]{1,0:T(8,128)}, f32[192,6448]{1,0:T(8,128)}, f32[192,6448]{1,0:T(8,128)}) fusion(f32[192,6448]{1,0:T(8,128)} %in_ref.1, bf16[192,6528]{1,0:T(8,128)(2,1)} %bitcast.11, f32[192,6448]{1,0:T(8,128)} %param.21, f32[192,6448]{1,0:T(8,128)} %param.20), kind=kLoop, calls=%fused_computation.4 | loop fusion | flops 19808256 | bytes 32188416 | tf_op jit(solution)/shard_map/sub | solution.py:1152
  211.6 0.0 copy-done
  211.6 0.0 copy-done.1
  211.6 0.6 copy-done.2
  212.2 0.5 copy-done.3
  212.7 0.0 copy-start.7
  212.8 0.0 copy-start.10
  212.8 0.0 copy-start.12
  212.8 0.0 copy-start.13
  212.8 0.0 copy-start.6
  212.8 0.0 copy-start.8
  212.8 0.0 copy-start.9
  212.8 0.0 copy-start.11
  212.8 0.0 copy-start.14
  212.8 0.0 copy-start.15
  212.8 0.0 copy-start.5
  212.8 0.0 copy-start.4
  212.9 4.4 %multiply_subtract_fusion.1 = (f32[384,1536]{1,0:T(8,128)}, f32[384,1536]{1,0:T(8,128)}, f32[384,1536]{1,0:T(8,128)}) fusion(f32[384,1536]{1,0:T(8,128)S(1)} %copy-done, bf16[8,48,1536]{2,1,0:T(8,128)(2,1)S(1)} %copy-done.3, f32[384,1536]{1,0:T(8,128)S(1)} %copy-done.1, f32[384,1536]{1,0:T(8,128)S(1)} %copy-done.2), kind=kLoop, calls=%fused_computation.10 | loop fusion | flops 9437184 | bytes 15335424 | tf_op jit(solution)/shard_map/sub | solution.py:1152
  217.2 0.0 copy-done.7
  217.2 0.0 copy-done.10
  217.2 0.0 copy-done.12
  217.3 0.0 copy-done.13
  217.3 0.6 multiply_subtract_fusion.3
  217.9 0.0 copy-done.6
  217.9 0.0 copy-done.8
  217.9 0.0 copy-done.9
  217.9 0.6 multiply_subtract_fusion.2
  218.5 0.0 copy-done.11
  218.5 0.0 copy-done.14
  218.5 0.0 copy-done.15
  218.6 0.6 multiply_subtract_fusion.4
  219.2 0.0 copy-done.5
  219.2 0.7 copy.36
  219.9 0.0 copy-done.4
  219.9 0.7 copy.37
  (2 shorter events, 0.0 us)
Async XLA Ops:
  198.9 12.7 %copy-start = (f32[384,1536]{1,0:T(8,128)S(1)}, f32[384,1536]{1,0:T(8,128)}, u32[]{:S(2)}) copy-start(f32[384,1536]{1,0:T(8,128)} %out_w.1) | copy-start | bytes 7077892
  198.9 12.7 %copy-start.1 = (f32[384,1536]{1,0:T(8,128)S(1)}, f32[384,1536]{1,0:T(8,128)}, u32[]{:S(2)}) copy-start(f32[384,1536]{1,0:T(8,128)} %param.24) | copy-start | bytes 7077892
  198.9 13.3 %copy-start.2 = (f32[384,1536]{1,0:T(8,128)S(1)}, f32[384,1536]{1,0:T(8,128)}, u32[]{:S(2)}) copy-start(f32[384,1536]{1,0:T(8,128)} %param.23) | copy-start | bytes 7077892
  198.9 13.8 %copy-start.3 = (bf16[8,48,1536]{2,1,0:T(8,128)(2,1)S(1)}, bf16[8,48,1536]{2,1,0:T(8,128)(2,1)}, u32[]{:S(2)}) copy-start(bf16[8,48,1536]{2,1,0:T(8,128)(2,1)} %get-tuple-element.25) | copy-start | bytes 3538948
  212.7 4.5 %copy-start.7 = (f32[8,640]{1,0:T(8,128)S(1)}, f32[8,640]{1,0:T(8,128)}, u32[]{:S(2)}) copy-start(f32[8,640]{1,0:T(8,128)} %get-tuple-element.26) | copy-start | bytes 61444
  212.8 4.5 %copy-start.10 = (f32[576]{0:T(1024)S(1)}, f32[576]{0:T(1024)}, u32[]{:S(2)}) copy-start(f32[576]{0:T(1024)} %param.25) | copy-start | bytes 6916
  212.8 4.5 %copy-start.12 = (f32[576]{0:T(1024)S(1)}, f32[576]{0:T(1024)}, u32[]{:S(2)}) copy-start(f32[576]{0:T(1024)} %param.27) | copy-start | bytes 6916
  212.8 4.5 %copy-start.13 = (f32[576]{0:T(1024)S(1)}, f32[576]{0:T(1024)}, u32[]{:S(2)}) copy-start(f32[576]{0:T(1024)} %param.26) | copy-start | bytes 6916
  212.8 5.1 %copy-start.6 = (f32[5,416]{1,0:T(8,128)S(1)}, f32[5,416]{1,0:T(8,128)}, u32[]{:S(2)}) copy-start(f32[5,416]{1,0:T(8,128)} %conv_in.1) | copy-start | bytes 24964
  212.8 5.1 %copy-start.8 = (f32[5,416]{1,0:T(8,128)S(1)}, f32[5,416]{1,0:T(8,128)}, u32[]{:S(2)}) copy-start(f32[5,416]{1,0:T(8,128)} %param.30) | copy-start | bytes 24964
  212.8 5.1 %copy-start.9 = (f32[5,416]{1,0:T(8,128)S(1)}, f32[5,416]{1,0:T(8,128)}, u32[]{:S(2)}) copy-start(f32[5,416]{1,0:T(8,128)} %param.29) | copy-start | bytes 24964
  212.8 5.7 %copy-start.11 = (f32[3,6]{1,0:T(4,128)S(1)}, f32[3,6]{1,0:T(4,128)}, u32[]{:S(2)}) copy-start(f32[3,6]{1,0:T(4,128)} %head_in.1) | copy-start | bytes 220
  212.8 5.7 %copy-start.14 = (f32[3,6]{1,0:T(4,128)S(1)}, f32[3,6]{1,0:T(4,128)}, u32[]{:S(2)}) copy-start(f32[3,6]{1,0:T(4,128)} %param.33) | copy-start | bytes 220
  212.8 5.7 %copy-start.15 = (f32[3,6]{1,0:T(4,128)S(1)}, f32[3,6]{1,0:T(4,128)}, u32[]{:S(2)}) copy-start(f32[3,6]{1,0:T(4,128)} %param.32) | copy-start | bytes 220
  212.8 6.3 %copy-start.5 = (bf16[128,1536]{1,0:T(8,128)(2,1)S(1)}, bf16[128,1536]{1,0:T(8,128)(2,1)}, u32[]{:S(2)}) copy-start(bf16[128,1536]{1,0:T(8,128)(2,1)} %get-tuple-element.22) | copy-start | bytes 1179652
  212.8 7.1 %copy-start.4 = (bf16[128,1536]{1,0:T(8,128)(2,1)S(1)}, bf16[128,1536]{1,0:T(8,128)(2,1)}, u32[]{:S(2)}) copy-start(bf16[128,1536]{1,0:T(8,128)(2,1)} %get-tuple-element.23) | copy-start | bytes 1179652

commit v6 on v5

--- a/solution.py
+++ b/solution.py
@@ -33,7 +33,7 @@
 adam_epsilon = 1e-08
 rates = (0.05, 0.04, 0.25, 0.5, 0.5)
 decays = (0.1, 0.1, 0.0, 0.0, 0.0)
-TOP = 96
+TOP = 80
 
 
 class Place:
@@ -409,7 +409,7 @@
     wq[:, WIDE - 128 :] = jnp.zeros((48, 128), bf16)
     small[...] = jnp.zeros_like(small)
     small[:5, :416] = conv_in[...].astype(bf16).astype(f32)
-    small[5:6, :576] = gain_in[...].astype(bf16).astype(f32)
+    small[5, :576] = gain_in[...].astype(bf16).astype(f32)
     hd_ref[...] = jnp.zeros_like(hd_ref)
     hd_ref[:3, :6] = head_in[...].astype(bf16).astype(f32)
     hd_ref[3:4, :] = widen(hd_ref[:, :128])[2:3]
@@ -678,26 +678,30 @@
 
     outs = Scatter(place, remote, po_ref, ra_ref, rb_ref, ra2_ref, rb2_ref, own_out, 72)
 
-    @pl.loop(0, BLOCKS)
+    @pl.loop(0, BLOCKS // 2)
     def _(i):
-        b = lax.rem(me + 1 + i, BLOCKS)
+        pair = lax.rem(me // 2 + 1 + i, BLOCKS // 2)
         column = turned_sums[...]
-        first = jnp.sum(jnp.where(lane == b, column, 0.0), axis=1, keepdims=True)
-        second = jnp.sum(jnp.where(lane == b + 8, column, 0.0), axis=1, keepdims=True)
-        z, y, dm = block_of(z_ref, b, OWN), block_of(y_ref, b, OWN), block_of(dm_ref, b, OWN)
-        sig_z = jax.nn.sigmoid(z)
-        gate = z * sig_z
-        scale = lax.rsqrt(first * (1.0 / DI) + epsilon)
-        unit = y * gate * scale
-        mixed = (unit * gain).astype(bf16)
-        mixed_ref[b] = mixed
-        dgain_ref[0:1, :] += jnp.sum(dm * unit, axis=0, keepdims=True)
-        dgated = scale * (gain * dm) - unit * (scale * scale * (second * (1.0 / DI)))
-        dz = dgated * y * (sig_z * (1.0 + z * (1.0 - sig_z)))
-        dp_ref[b, :, :OWN] = dz.astype(bf16)
-        dcore_ref[b] = dgated * gate
-        po_ref[b] = dot(mixed, wo_ref[...], 1, 0).astype(bf16)
-        outs.send(b)
+        for j in range(2):
+            b = 2 * pair + j
+            first = jnp.sum(jnp.where(lane == b, column, 0.0), axis=1, keepdims=True)
+            second = jnp.sum(jnp.where(lane == b + 8, column, 0.0), axis=1, keepdims=True)
+            z, y, dm = block_of(z_ref, b, OWN), block_of(y_ref, b, OWN), block_of(dm_ref, b, OWN)
+            sig_z = jax.nn.sigmoid(z)
+            gate = z * sig_z
+            scale = lax.rsqrt(first * (1.0 / DI) + epsilon)
+            unit = y * gate * scale
+            mixed_ref[b] = (unit * gain).astype(bf16)
+            dgain_ref[0:1, :] += jnp.sum(dm * unit, axis=0, keepdims=True)
+            dgated = scale * (gain * dm) - unit * (scale * scale * (second * (1.0 / DI)))
+            dz = dgated * y * (sig_z * (1.0 + z * (1.0 - sig_z)))
+            dp_ref[b, :, :OWN] = dz.astype(bf16)
+            dcore_ref[b] = dgated * gate
+        two = pl.ds(2 * pair, 2)
+        part = dot(mixed_ref[two].reshape(TB, OWN), wo_ref[...], 1, 0)
+        po_ref[two] = part.astype(bf16).reshape(2, BLOCK, D)
+        outs.send(2 * pair)
+        outs.send(2 * pair + 1)
 
     def weight_grad(q, columns):
         left = n_ref[:, :, pl.ds(pl.multiple_of(384 * q, 128), 384)].reshape(LEN, 384)
@@ -772,7 +776,7 @@
             sum_z.begin()
             sum_o.begin()
 
-        pl.when(i == 5)(outs.middle)
+        pl.when(i == 7)(outs.middle)
 
         conv = block_of(big_b, b, 640)
         raw, core, dcore = raw_ref[b], core_ref[b], dcore_ref[b]
@@ -853,13 +857,16 @@
     cots.sent()
     ins = Scatter(place, remote, ct_ref, ia_ref, ib_ref, ia2_ref, ib2_ref, own_out, 122)
 
-    @pl.loop(0, BLOCKS)
+    @pl.loop(0, BLOCKS // 2)
     def _(i):
-        b = lax.rem(me + 1 + i, BLOCKS)
-        ct_ref[b] = dot(dp_ref[b], w_ref[...].reshape(D, COLS), 1, 1).astype(bf16)
-        ins.send(b)
-
-        @pl.when(i == 3)
+        pair = lax.rem(me // 2 + 1 + i, BLOCKS // 2)
+        two = pl.ds(2 * pair, 2)
+        part = dot(dp_ref[two].reshape(TB, COLS), w_ref[...].reshape(D, COLS), 1, 1)
+        ct_ref[two] = part.astype(bf16).reshape(2, BLOCK, D)
+        ins.send(2 * pair)
+        ins.send(2 * pair + 1)
+
+        @pl.when(i == 1)
         def _():
             swap_x.wait_recv()
             for r in range(4):
@@ -1158,7 +1165,7 @@
     head_master, head_first, head_second,
 ):
     layer_out, input_grad, total_w, total_o, total = run_whole(
-        hidden[0], cotangent[0], in_master, out_master, conv_master, gain_master[None], head_master
+        hidden[0], cotangent[0], in_master, out_master, conv_master, gain_master, head_master
     )
     gradients = (
         total_w.reshape(192, WIDE)[:, :PROJ].astype(f32), total_o.reshape(OWN, D).astype(f32),

time: 221 us -> 207 us (0.937)
  Pallas kernels: 197 us -> 185 us
    pallas_call x1, Pallas kernels: 197 us -> 185 us  [run_whole(): pl.pallas_call(whole_kernel, in_specs=[any_spec] * 4 + [vmem] * 3, out_sp...]
where the time goes in v6:
time: 207 us
  Pallas kernels  185 us (89%)
  other arithmetic  18.9 us (9%)
  local copies, waits for them, and re-layouts  2.74 us (1%)
    pallas_call x1, Pallas kernels, run_whole(): pl.pallas_call(whole_kernel, in_specs=[any_spec] * 4 + [vmem] * 3, out_sp...  185 us
    sub x5, other arithmetic, adam_update(): return (first_new, second_new, master - rate * (scaled + decay * master))  18.9 us

profile of v6, /device:TPU:1, one launch (start us, length us, event | category | flops | bytes accessed | tf_op | source)
XLA Modules:
  0.0 207.1 jit_solution(17321952419748453961)
XLA Ops:
  0.7 184.6 %shard_map.296 = (bf16[128,1536]{1,0:T(8,128)(2,1)}, bf16[128,1536]{1,0:T(8,128)(2,1)}, bf16[8,24,6528]{2,1,0:T(8,128)(2,1)}, bf16[8,48,1536]{2,1,0:T(8,128)(2,1)}, f32[8,640]{1,0:T(8,128)}) custom-call(bf16[128,1536]{1,0:T(8,128)(2,1)} %bitcast.12, bf16[128,1536]{1,0:T(8,128)(2,1)} %bitcast.13, f32[192,6448]{1,0:T(8,128)} %in_ref.1, f32[384,1536]{1,0:T(8,128)} %out_w.1, ...), custom_call_target="tpu_custom_call" | custom-call | tf_op jit(solution)/shard_map/pallas_call | solution.py:1057
  185.3 0.0 copy-start
  185.3 0.0 copy-start.1
  185.3 0.0 copy-start.2
  185.3 0.0 copy-start.3
  185.3 12.7 %multiply_subtract_fusion = (f32[192,6448]{1,0:T(8,128)}, f32[192,6448]{1,0:T(8,128)}, f32[192,6448]{1,0:T(8,128)}) fusion(f32[192,6448]{1,0:T(8,128)} %in_ref.1, bf16[192,6528]{1,0:T(8,128)(2,1)} %bitcast.11, f32[192,6448]{1,0:T(8,128)} %param.21, f32[192,6448]{1,0:T(8,128)} %param.20), kind=kLoop, calls=%fused_computation.4 | loop fusion | flops 19808256 | bytes 32188416 | tf_op jit(solution)/shard_map/sub | solution.py:1159
  198.0 0.0 copy-done
  198.0 0.0 copy-done.1
  198.0 0.6 copy-done.2
  198.6 0.5 copy-done.3
  199.2 0.0 copy-start.7
  199.2 0.0 copy-start.8
  199.2 0.0 copy-start.12
  199.2 0.0 copy-start.13
  199.2 0.0 copy-start.6
  199.2 0.0 copy-start.9
  199.2 0.0 copy-start.10
  199.2 0.0 copy-start.11
  199.2 0.0 copy-start.14
  199.2 0.0 copy-start.15
  199.2 0.0 copy-start.5
  199.2 0.0 copy-start.4
  199.3 4.4 %multiply_subtract_fusion.1 = (f32[384,1536]{1,0:T(8,128)}, f32[384,1536]{1,0:T(8,128)}, f32[384,1536]{1,0:T(8,128)}) fusion(f32[384,1536]{1,0:T(8,128)S(1)} %copy-done, bf16[8,48,1536]{2,1,0:T(8,128)(2,1)S(1)} %copy-done.3, f32[384,1536]{1,0:T(8,128)S(1)} %copy-done.1, f32[384,1536]{1,0:T(8,128)S(1)} %copy-done.2), kind=kLoop, calls=%fused_computation.10 | loop fusion | flops 9437184 | bytes 15335424 | tf_op jit(solution)/shard_map/sub | solution.py:1159
  203.6 0.0 copy-done.7
  203.6 0.0 copy-done.8
  203.6 0.0 copy-done.12
  203.7 0.0 copy-done.13
  203.7 0.6 multiply_subtract_fusion.3
  204.3 0.0 copy-done.6
  204.3 0.0 copy-done.9
  204.3 0.0 copy-done.10
  204.3 0.6 multiply_subtract_fusion.2
  204.9 0.0 copy-done.11
  204.9 0.0 copy-done.14
  204.9 0.0 copy-done.15
  205.0 0.6 multiply_subtract_fusion.4
  205.6 0.0 copy-done.5
  205.6 0.7 copy.36
  206.3 0.0 copy-done.4
  206.3 0.7 copy.37
  (2 shorter events, 0.0 us)
Async XLA Ops:
  185.3 12.7 %copy-start = (f32[384,1536]{1,0:T(8,128)S(1)}, f32[384,1536]{1,0:T(8,128)}, u32[]{:S(2)}) copy-start(f32[384,1536]{1,0:T(8,128)} %out_w.1) | copy-start | bytes 7077892
  185.3 12.7 %copy-start.1 = (f32[384,1536]{1,0:T(8,128)S(1)}, f32[384,1536]{1,0:T(8,128)}, u32[]{:S(2)}) copy-start(f32[384,1536]{1,0:T(8,128)} %param.24) | copy-start | bytes 7077892
  185.3 13.3 %copy-start.2 = (f32[384,1536]{1,0:T(8,128)S(1)}, f32[384,1536]{1,0:T(8,128)}, u32[]{:S(2)}) copy-start(f32[384,1536]{1,0:T(8,128)} %param.23) | copy-start | bytes 7077892
  185.3 13.8 %copy-start.3 = (bf16[8,48,1536]{2,1,0:T(8,128)(2,1)S(1)}, bf16[8,48,1536]{2,1,0:T(8,128)(2,1)}, u32[]{:S(2)}) copy-start(bf16[8,48,1536]{2,1,0:T(8,128)(2,1)} %get-tuple-element.25) | copy-start | bytes 3538948
  199.2 4.5 %copy-start.7 = (f32[8,640]{1,0:T(8,128)S(1)}, f32[8,640]{1,0:T(8,128)}, u32[]{:S(2)}) copy-start(f32[8,640]{1,0:T(8,128)} %get-tuple-element.26) | copy-start | bytes 61444
  199.2 4.5 %copy-start.8 = (f32[576]{0:T(1024)S(1)}, f32[576]{0:T(1024)}, u32[]{:S(2)}) copy-start(f32[576]{0:T(1024)} %gain_in.1) | copy-start | bytes 6916
  199.2 4.5 %copy-start.12 = (f32[576]{0:T(1024)S(1)}, f32[576]{0:T(1024)}, u32[]{:S(2)}) copy-start(f32[576]{0:T(1024)} %param.27) | copy-start | bytes 6916
  199.2 4.5 %copy-start.13 = (f32[576]{0:T(1024)S(1)}, f32[576]{0:T(1024)}, u32[]{:S(2)}) copy-start(f32[576]{0:T(1024)} %param.26) | copy-start | bytes 6916
  199.2 5.1 %copy-start.6 = (f32[5,416]{1,0:T(8,128)S(1)}, f32[5,416]{1,0:T(8,128)}, u32[]{:S(2)}) copy-start(f32[5,416]{1,0:T(8,128)} %conv_in.1) | copy-start | bytes 24964
  199.2 5.1 %copy-start.9 = (f32[5,416]{1,0:T(8,128)S(1)}, f32[5,416]{1,0:T(8,128)}, u32[]{:S(2)}) copy-start(f32[5,416]{1,0:T(8,128)} %param.30) | copy-start | bytes 24964
  199.2 5.1 %copy-start.10 = (f32[5,416]{1,0:T(8,128)S(1)}, f32[5,416]{1,0:T(8,128)}, u32[]{:S(2)}) copy-start(f32[5,416]{1,0:T(8,128)} %param.29) | copy-start | bytes 24964
  199.2 5.7 %copy-start.11 = (f32[3,6]{1,0:T(4,128)S(1)}, f32[3,6]{1,0:T(4,128)}, u32[]{:S(2)}) copy-start(f32[3,6]{1,0:T(4,128)} %head_in.1) | copy-start | bytes 220
  199.2 5.7 %copy-start.14 = (f32[3,6]{1,0:T(4,128)S(1)}, f32[3,6]{1,0:T(4,128)}, u32[]{:S(2)}) copy-start(f32[3,6]{1,0:T(4,128)} %param.33) | copy-start | bytes 220
  199.2 5.7 %copy-start.15 = (f32[3,6]{1,0:T(4,128)S(1)}, f32[3,6]{1,0:T(4,128)}, u32[]{:S(2)}) copy-start(f32[3,6]{1,0:T(4,128)} %param.32) | copy-start | bytes 220
  199.2 6.3 %copy-start.5 = (bf16[128,1536]{1,0:T(8,128)(2,1)S(1)}, bf16[128,1536]{1,0:T(8,128)(2,1)}, u32[]{:S(2)}) copy-start(bf16[128,1536]{1,0:T(8,128)(2,1)} %get-tuple-element.22) | copy-start | bytes 1179652
  199.2 7.1 %copy-start.4 = (bf16[128,1536]{1,0:T(8,128)(2,1)S(1)}, bf16[128,1536]{1,0:T(8,128)(2,1)}, u32[]{:S(2)}) copy-start(bf16[128,1536]{1,0:T(8,128)(2,1)} %get-tuple-element.23) | copy-start | bytes 1179652

commit v7 on v6

--- a/solution.py
+++ b/solution.py
@@ -866,7 +866,7 @@
         ins.send(2 * pair)
         ins.send(2 * pair + 1)
 
-        @pl.when(i == 1)
+        @pl.when(i == 0)
         def _():
             swap_x.wait_recv()
             for r in range(4):
@@ -1150,36 +1150,74 @@
 
 def adam_update(master, first, second, gradient, rate, decay):
     first_new = beta_one * first + (1.0 - beta_one) * gradient
-    second_new = beta_two * second + (1.0 - beta_two) * gradient * gradient
-    scaled = (
-        first_new
-        / (1.0 - beta_one**STEP)
-        / (jnp.sqrt(second_new / (1.0 - beta_two**STEP)) + adam_epsilon)
-    )
+    second_new = beta_two * second + (1.0 - beta_two) * (gradient * gradient)
+    square = second_new * (1.0 / (1.0 - beta_two**STEP))
+    root = square * lax.rsqrt(square) + adam_epsilon
+    scaled = first_new * (1.0 / (1.0 - beta_one**STEP)) / root
     return (first_new, second_new, master - rate * (scaled + decay * master))
 
 
-def on_device(
-    hidden, cotangent, in_master, in_first, in_second, out_master, out_first, out_second,
-    gain_master, gain_first, gain_second, conv_master, conv_first, conv_second,
-    head_master, head_first, head_second,
-):
+def adam_kernel(in_sum, out_sum, small, layer, grad, *refs):
+    state, results = refs[:15], refs[15:30]
+    for group, total in enumerate((in_sum, out_sum)):
+        master, first, second = state[3 * group : 3 * group + 3]
+        columns = master.shape[1]
+        half = master.shape[0] // 2
+        for part, lo in [(p, q) for p in range(2) for q in range(0, half, 16)]:
+            inner = slice(lo, min(lo + 16, half))
+            some = slice(half * part + inner.start, half * part + inner.stop)
+            new = adam_update(
+                master[some], first[some], second[some], total[part, inner, :columns].astype(f32),
+                rates[group], decays[group],
+            )
+            for result, value in zip(results[3 * group : 3 * group + 3], new):
+                result[some] = value
+    refs[30][...] = layer[...]
+    refs[31][...] = grad[...]
+
+    @pl.when(pl.program_id(0) == 0)
+    def _():
+        def update(group, gradient, *index):
+            values = [ref[index] for ref in state[3 * group : 3 * group + 3]]
+            new = adam_update(*values, gradient, rates[group], decays[group])
+            for result, value in zip(results[3 * group : 3 * group + 3], new):
+                result[index] = value
+
+        update(2, small[5, :576], slice(None))
+        update(3, small[:5, :416], slice(None), slice(None))
+        for row in range(3):
+            at = 128 * row
+            update(4, small[6:7, at : at + 6], slice(row, row + 1), slice(None))
+
+
+def run_adam(in_sum, out_sum, small, layer, grad, *state):
+    in_block = pl.BlockSpec((48, PROJ), lambda i: (i, 0))
+    out_block = pl.BlockSpec((96, D), lambda i: (i, 0))
+    tokens = pl.BlockSpec((BLOCK // 4, D), lambda i: (i, 0))
+    vmem = pl.BlockSpec(memory_space=pltpu.VMEM)
+    blocks = [in_block] * 3 + [out_block] * 3 + [vmem] * 9
+    return pl.pallas_call(
+        adam_kernel,
+        grid=(4,),
+        in_specs=[
+            pl.BlockSpec((2, 24, WIDE), lambda i: (i, 0, 0)),
+            pl.BlockSpec((2, 48, D), lambda i: (i, 0, 0)),
+            vmem, tokens, tokens,
+        ]
+        + blocks,
+        out_specs=tuple(blocks + [tokens, tokens]),
+        out_shape=tuple([sds(a.shape) for a in state] + [sds((BLOCK, D), bf16)] * 2),
+        compiler_params=pltpu.CompilerParams(vmem_limit_bytes=60 * 2**20),
+    )(in_sum, out_sum, small, layer, grad, *state)
+
+
+def on_device(hidden, cotangent, *state):
+    in_master, out_master, gain_master, conv_master, head_master = state[::3]
     layer_out, input_grad, total_w, total_o, total = run_whole(
         hidden[0], cotangent[0], in_master, out_master, conv_master, gain_master, head_master
     )
-    gradients = (
-        total_w.reshape(192, WIDE)[:, :PROJ].astype(f32), total_o.reshape(OWN, D).astype(f32),
-        total[5, :576], total[:5, :416],
-        jnp.stack([total[6, :6], total[6, 128:134], total[6, 256:262]]),
-    )
-    masters = (in_master, out_master, gain_master, conv_master, head_master)
-    firsts = (in_first, out_first, gain_first, conv_first, head_first)
-    seconds = (in_second, out_second, gain_second, conv_second, head_second)
-    updated = [
-        adam_update(masters[g], firsts[g], seconds[g], gradients[g], rates[g], decays[g])
-        for g in range(5)
-    ]
-    return (layer_out[None], input_grad[None]) + tuple(v for group in updated for v in group)
+    done = run_adam(total_w, total_o, total, layer_out, input_grad, *state)
+    return (done[15][None], done[16][None]) + tuple(done[:15])
 
 
 def solution(mesh):

time: 207 us -> 202 us (0.976)
  other arithmetic: 18.9 us -> 0 us
  Pallas kernels: 185 us -> 201 us
  local copies, waits for them, and re-layouts: 2.74 us -> 0 us
    sub x5 -> x0, other arithmetic: 18.9 us -> none  [adam_update(): return (first_new, second_new, master - rate * (scaled + decay * master))]
    pallas_call x0 -> x1, Pallas kernels: none -> 17.3 us  [run_adam(): pl.pallas_call(adam_kernel, grid=(4,), in_specs=[pl.BlockSpec((2, 24, WID...]
    unnamed x34 -> x0, local copies, waits for them, and re-layouts: 2.72 us -> none
where the time goes in v7:
time: 202 us
  Pallas kernels  201 us (100%)
    pallas_call x1, Pallas kernels, run_whole(): pl.pallas_call(whole_kernel, in_specs=[any_spec] * 4 + [vmem] * 3, out_sp...  184 us
    pallas_call x1, Pallas kernels, run_adam(): pl.pallas_call(adam_kernel, grid=(4,), in_specs=[pl.BlockSpec((2, 24, WID...  17.3 us

profile of v7, /device:TPU:1, one launch (start us, length us, event | category | flops | bytes accessed | tf_op | source)
XLA Modules:
  0.0 202.2 jit_solution(1311445847466770350)
XLA Ops:
  0.7 184.1 %shard_map.296 = (bf16[128,1536]{1,0:T(8,128)(2,1)}, bf16[128,1536]{1,0:T(8,128)(2,1)}, bf16[8,24,6528]{2,1,0:T(8,128)(2,1)}, bf16[8,48,1536]{2,1,0:T(8,128)(2,1)}, f32[8,640]{1,0:T(8,128)}) custom-call(bf16[128,1536]{1,0:T(8,128)(2,1)} %bitcast.4, bf16[128,1536]{1,0:T(8,128)(2,1)} %bitcast.5, f32[192,6448]{1,0:T(8,128)} %refs_0_.1, f32[384,1536]{1,0:T(8,128)} %refs_3_.1, ...), custom_call_target="tpu_custom_call" | custom-call | tf_op jit(solution)/shard_map/pallas_call | solution.py:1057
  184.8 17.3 %shard_map.297 = (f32[192,6448]{1,0:T(8,128)}, f32[192,6448]{1,0:T(8,128)}, f32[192,6448]{1,0:T(8,128)}, f32[384,1536]{1,0:T(8,128)}, f32[384,1536]{1,0:T(8,128)...) custom-call(bf16[8,24,6528]{2,1,0:T(8,128)(2,1)} %get-tuple-element., ...), custom_call_target="tpu_custom_call" | custom-call | tf_op jit(solution)/shard_map/pallas_call | solution.py:1199

commit v8 on v7

--- a/solution.py
+++ b/solution.py
@@ -558,11 +558,11 @@
     w_scan.begin()
     locals_[0].wait()
     hids.first()
+    cots.begin()
     w_scan.first()
     hids.second()
     w_arrived((0,))
     w_gate.begin()
-    cots.begin()
     w_scan.second()
 
     sm_ref[me] = small[...]
@@ -602,7 +602,7 @@
         def _():
             w_gate.second()
 
-        @pl.when(i == 3)
+        @pl.when(i == 1)
         def _():
             cots.first()
 

time: 202 us -> 202 us (level)
  no operation moved by 1% of the time
where the time goes in v8:
time: 202 us
  Pallas kernels  202 us (100%)
    pallas_call x1, Pallas kernels, run_whole(): pl.pallas_call(whole_kernel, in_specs=[any_spec] * 4 + [vmem] * 3, out_sp...  184 us
    pallas_call x1, Pallas kernels, run_adam(): pl.pallas_call(adam_kernel, grid=(4,), in_specs=[pl.BlockSpec((2, 24, WID...  17.3 us

profile of v8, /device:TPU:1, one launch (start us, length us, event | category | flops | bytes accessed | tf_op | source)
XLA Modules:
  0.0 202.3 jit_solution(1396129919024998534)
XLA Ops:
  0.7 184.2 %shard_map.296 = (bf16[128,1536]{1,0:T(8,128)(2,1)}, bf16[128,1536]{1,0:T(8,128)(2,1)}, bf16[8,24,6528]{2,1,0:T(8,128)(2,1)}, bf16[8,48,1536]{2,1,0:T(8,128)(2,1)}, f32[8,640]{1,0:T(8,128)}) custom-call(bf16[128,1536]{1,0:T(8,128)(2,1)} %bitcast.4, bf16[128,1536]{1,0:T(8,128)(2,1)} %bitcast.5, f32[192,6448]{1,0:T(8,128)} %refs_0_.1, f32[384,1536]{1,0:T(8,128)} %refs_3_.1, ...), custom_call_target="tpu_custom_call" | custom-call | tf_op jit(solution)/shard_map/pallas_call | solution.py:1057
  184.9 17.3 %shard_map.297 = (f32[192,6448]{1,0:T(8,128)}, f32[192,6448]{1,0:T(8,128)}, f32[192,6448]{1,0:T(8,128)}, f32[384,1536]{1,0:T(8,128)}, f32[384,1536]{1,0:T(8,128)...) custom-call(bf16[8,24,6528]{2,1,0:T(8,128)(2,1)} %get-tuple-element., ...), custom_call_target="tpu_custom_call" | custom-call | tf_op jit(solution)/shard_map/pallas_call | solution.py:1199
